TPU v7x, 128 devices: a whole 4x4x4 slice. The times are simulated.
128 devices in a mesh: blk: 128 (over y, x, z, core).
Axes of the slice: x: 4, y: 4, z: 4, core: 2. Of those that a mesh axis runs over, the one named last changes fastest.
Arguments:
- old_phase: float32 [2048, 32768], P('blk'), may hold values from -1 to 1
- old_solute: float32 [2048, 32768], P('blk'), may hold values from -0.45 to 0.45
- old_mobility: float32 [2048, 32768], P('blk'), may hold values from 0.25 to 1
- new_global_slot: int32 [2048], P('blk'), may hold values from -1 to 1023, as said below
- neighbors: int32 [1024, 6], P('blk'), may hold values from -1 to 1023, as said below
Outputs:
- phase: float32 [1024, 32768], P('blk')
- solute: float32 [1024, 32768], P('blk')
Inputs may be any that keep to these rules, and one draw needn't show every extreme that they name: Each device's old slots hold its blocks first and -1 after them; the blocks taken in device order and slot order get the consecutive numbers 0 to 1023. The block in an old slot of device p goes to device new_global_slot // 8, at most 2 devices away; in every draw some block moves exactly 2 devices down and some exactly 2 up, some device holds 16 blocks and some none. `neighbors`: the relation is symmetric: if b is the +x (+y, +z) neighbour of a, then a is the -x (-y, -z) neighbour of b. The x neighbours of a block of device p lie on devices p - 1 and p + 1 (every block has both except on the first and last device, where that side is -1); y and z neighbours lie on the block's own device, with -1 at the ends along y and none along z (a block may be its own z neighbour). The layers of blocks line up: if b is the -x (+x) neighbour of a, then the y and z neighbours of b are the -x (+x) neighbours of the y and z neighbours of a, and -1 where those are -1.
All inputs are finite; a program needn't handle non-finite values.
Results may differ from a plain program's by a relative error of at most 0.00014.
Values sent between devices are 32-bit elements; how exact they have to be, the bound alone decides.
No kernel may reach another device: no remote copies, remote signals or barrier semaphores. Data moves between devices by JAX's collectives and lax.ppermute only.
A program may use at most 128 MiB of HBM per device.

v0:
```python
import functools

import jax
import jax.numpy as jnp
from jax import lax
from jax.experimental import pallas as pl
from jax.experimental.pallas import tpu as pltpu
from jax.sharding import PartitionSpec as P

EDGE = 32
FACE = EDGE * EDGE
CELLS = EDGE * FACE
CAP = 8
OLD = 16
FIELDS = 3
HALO = 3
CHUNK_PLANES = 4
CHUNK = CHUNK_PLANES * FACE
CHUNKS = EDGE // CHUNK_PLANES
LANES = 128
EXT = EDGE + 2 * HALO

time_step = 0.15
coupling = 1.5


def windows(slot_ref, here):
    first = slot_ref[0]
    count = jnp.int32(0)
    for i in range(OLD):
        count += (slot_ref[i] >= 0).astype(jnp.int32)
    amount = jnp.bitwise_and(first, CAP - 1)
    row = lax.broadcasted_iota(jnp.int32, (CAP, LANES), 0)

    def masks(k):
        index = row + ((here + k) * CAP - first)
        low = (index >= 0) & (index < CAP) & (index < count)
        high = (index >= CAP) & (index < count)
        return low, high

    return amount, masks


def picked(masks, low_rows, high_rows):
    low, high = masks
    return jnp.where(low, low_rows, jnp.where(high, high_rows, 0.0))


def side_of(here):
    return jnp.where(jnp.bitwise_and(here, 1) == 0, -1, 1)


def pack_kernel(here_ref, slot_ref, phi_ref, conc_ref, mob_ref, far_ref, merge_ref, final_ref):
    here = here_ref[0]
    side = side_of(here)
    amount, masks = windows(slot_ref, here)
    far, merge, final = masks(2 * side), masks(side), masks(-side)
    for f, ref in enumerate((phi_ref, conc_ref, mob_ref)):
        for v in range(CHUNK // LANES):
            lanes = pl.ds(v * LANES, LANES)
            low_rows = pltpu.roll(ref[0:CAP, lanes], amount, 0)
            high_rows = pltpu.roll(ref[CAP:OLD, lanes], amount, 0)
            far_ref[f, :, lanes] = picked(far, low_rows, high_rows)
            merge_ref[f, :, lanes] = picked(merge, low_rows, high_rows)
            final_ref[f, :, lanes] = picked(final, low_rows, high_rows)


def relay_kernel(here_ref, slot_ref, phi_ref, conc_ref, mob_ref, merge_ref, edge_ref, rest_ref):
    here = here_ref[0]
    side = side_of(here)
    amount, masks = windows(slot_ref, here)
    back = masks(-2 * side)
    i = pl.program_id(0)
    outer = (i == 0) | (i == CHUNKS - 1)

    def fill(out_ref):
        for f, ref in enumerate((phi_ref, conc_ref, mob_ref)):
            for v in range(CHUNK // LANES):
                lanes = pl.ds(v * LANES, LANES)
                low_rows = pltpu.roll(ref[0:CAP, lanes], amount, 0)
                high_rows = pltpu.roll(ref[CAP:OLD, lanes], amount, 0)
                out_ref[f, :, lanes] = picked(back, low_rows, high_rows) + merge_ref[f, :, lanes]

    @pl.when(outer)
    def _():
        fill(edge_ref)

    @pl.when(jnp.logical_not(outer))
    def _():
        fill(rest_ref)


def gather_kernel(here_ref, slot_ref, phi_ref, conc_ref, mob_ref, final_ref, far_ref, edge_ref, sum_ref, low_ref, high_ref):
    here = here_ref[0]
    amount, masks = windows(slot_ref, here)
    own = masks(0)
    i = pl.program_id(0)

    def placed(f, ref, lanes):
        low_rows = pltpu.roll(ref[0:CAP, lanes], amount, 0)
        high_rows = pltpu.roll(ref[CAP:OLD, lanes], amount, 0)
        return picked(own, low_rows, high_rows) + final_ref[f, :, lanes] + far_ref[f, :, lanes]

    def fill(with_edge, face_ref, start):
        for f, ref in enumerate((phi_ref, conc_ref, mob_ref)):
            for v in range(CHUNK // LANES):
                lanes = pl.ds(v * LANES, LANES)
                value = placed(f, ref, lanes)
                if with_edge:
                    value = value + edge_ref[f, :, lanes]
                    at = v * LANES - start
                    if 0 <= at < HALO * FACE:
                        face_ref[f, :, pl.ds(at, LANES)] = value
                sum_ref[f, :, lanes] = value

    @pl.when(i == 0)
    def _():
        fill(True, low_ref, 0)

    @pl.when(i == CHUNKS - 1)
    def _():
        fill(True, high_ref, (CHUNK_PLANES - HALO) * FACE)

    @pl.when((i > 0) & (i < CHUNKS - 1))
    def _():
        fill(False, None, 0)


def step_kernel(here_ref, sum_ref, rest_ref, below_ref, above_ref, nbr_ref, phase_ref, solute_ref, phi0, conc0, mob, phi1, conc1, phi2, conc2):
    here = here_ref[0]
    base = here * CAP
    vregs = FACE // LANES
    lane = lax.broadcasted_iota(jnp.int32, (CAP, LANES), 1)
    z = jnp.bitwise_and(lane, EDGE - 1)
    z_first, z_last = z == 0, z == EDGE - 1
    y_first, y_last = lane < EDGE, lane >= LANES - EDGE
    nbr = nbr_ref[...]

    def column(c, start):
        wide = jnp.broadcast_to(nbr[:, c : c + 1], (CAP, LANES))
        valid = wide >= 0
        return jnp.where(valid, wide - start, 0), valid

    below_x, has_below_x = column(0, base - CAP)
    above_x, has_above_x = column(1, base + CAP)
    below_y, has_below_y = column(2, base)
    above_y, has_above_y = column(3, base)
    below_z, _ = column(4, base)
    above_z, _ = column(5, base)
    down_z = jnp.bitwise_or(lane - z, jnp.bitwise_and(z + EDGE - 1, EDGE - 1))
    up_z = jnp.bitwise_or(lane - z, jnp.bitwise_and(z + 1, EDGE - 1))

    def rows(x, index):
        return jnp.take_along_axis(x, index, axis=0, mode="promise_in_bounds")

    def turned(x, index):
        return jnp.take_along_axis(x, index, axis=1, mode="promise_in_bounds")

    start_states = (phi0, conc0, mob)
    first_rest, last_rest = CHUNK_PLANES, EDGE - CHUNK_PLANES

    def place(x, add):
        for f, ref in enumerate(start_states):
            for v in range(vregs):
                lanes = pl.ds(pl.multiple_of(x * FACE + v * LANES, LANES), LANES)
                value = sum_ref[f, :, lanes]
                if add:
                    part = pl.ds(pl.multiple_of((x - first_rest) * FACE + v * LANES, LANES), LANES)
                    value = value + rest_ref[f, :, part]
                ref[x + HALO, :, pl.ds(v * LANES, LANES)] = value

    for x in (*range(first_rest), *range(last_rest, EDGE)):
        place(x, False)

    @pl.loop(first_rest, last_rest)
    def _(x):
        place(x, True)

    for f, ref in enumerate(start_states):
        for d in range(HALO):
            for v in range(vregs):
                lanes = pl.ds(v * LANES, LANES)
                part = pl.ds(d * FACE + v * LANES, LANES)
                mirror_low = ref[2 * HALO - 1 - d, :, lanes]
                ref[d, :, lanes] = jnp.where(has_below_x, rows(below_ref[f, :, part], below_x), mirror_low)
                mirror_high = ref[EDGE + HALO - 1 - d, :, lanes]
                ref[EDGE + HALO + d, :, lanes] = jnp.where(has_above_x, rows(above_ref[f, :, part], above_x), mirror_high)

    def laplacian(ref, x):
        centre = [ref[x, :, pl.ds(v * LANES, LANES)] for v in range(vregs)]
        lower = [pltpu.roll(c, EDGE, 1) for c in centre]
        upper = [pltpu.roll(c, LANES - EDGE, 1) for c in centre]
        out = []
        for v in range(vregs):
            c = centre[v]
            lanes = pl.ds(v * LANES, LANES)
            if v:
                from_lower = lower[v - 1]
            else:
                from_lower = jnp.where(has_below_y, rows(lower[-1], below_y), c)
            if v < vregs - 1:
                from_upper = upper[v + 1]
            else:
                from_upper = jnp.where(has_above_y, rows(upper[0], above_y), c)
            prev_y = jnp.where(y_first, from_lower, lower[v])
            next_y = jnp.where(y_last, from_upper, upper[v])
            prev_z = turned(jnp.where(z_last, rows(c, below_z), c), down_z)
            next_z = turned(jnp.where(z_first, rows(c, above_z), c), up_z)
            total = (ref[x - 1, :, lanes] + ref[x + 1, :, lanes]) + (prev_y + next_y) + (prev_z + next_z)
            out.append(total - 6.0 * c)
        return out, centre

    def advance(phi_ref, conc_ref, x, store):
        lapl_phi, phis = laplacian(phi_ref, x)
        lapl_conc, concs = laplacian(conc_ref, x)
        for v in range(vregs):
            phi, conc = phis[v], concs[v]
            square = phi * phi
            wetting = 1.0 - square
            drive = lapl_phi[v] + phi - square * phi - coupling * conc * wetting * wetting
            change = time_step * mob[x, :, pl.ds(v * LANES, LANES)] * drive
            store(v, phi + change, conc + time_step * lapl_conc[v] + 0.5 * change)

    def into(phi_ref, conc_ref, x):
        def store(v, phi, conc):
            lanes = pl.ds(v * LANES, LANES)
            phi_ref[x, :, lanes] = phi
            conc_ref[x, :, lanes] = conc

        return store

    def out(x):
        def store(v, phi, conc):
            lanes = pl.ds(pl.multiple_of((x - HALO) * FACE + v * LANES, LANES), LANES)
            phase_ref[:, lanes] = phi
            solute_ref[:, lanes] = conc

        return store

    @pl.loop(1, EXT - 1)
    def _(x):
        advance(phi0, conc0, x, into(phi1, conc1, x))

    @pl.loop(2, EXT - 2)
    def _(x):
        advance(phi1, conc1, x, into(phi2, conc2, x))

    @pl.loop(HALO, EXT - HALO)
    def _(x):
        advance(phi2, conc2, x, out(x))


SMEM = pl.BlockSpec(memory_space=pltpu.SMEM)
VMEM = pl.BlockSpec(memory_space=pltpu.VMEM)
PARAMS = pltpu.CompilerParams(vmem_limit_bytes=32 * 2**20)


def shaped(planes):
    return jax.ShapeDtypeStruct((FIELDS, CAP, planes * FACE), jnp.float32)


def cost(flops, moved):
    return pl.CostEstimate(flops=flops, bytes_accessed=moved, transcendentals=0)


OLD_SPEC = pl.BlockSpec((OLD, CHUNK), lambda i: (0, i))
CHUNK_SPEC = pl.BlockSpec((FIELDS, CAP, CHUNK), lambda i: (0, 0, i))
EDGE_SPEC = pl.BlockSpec((FIELDS, CAP, CHUNK), lambda i: (0, 0, jnp.where(i == CHUNKS - 1, 1, 0)))
REST_SPEC = pl.BlockSpec((FIELDS, CAP, CHUNK), lambda i: (0, 0, jnp.clip(i - 1, 0, CHUNKS - 3)))
FACE_SPEC = pl.BlockSpec((FIELDS, CAP, HALO * FACE), lambda i: (0, 0, 0))
MB = 2**20


def on_device(old_phase, old_solute, old_mobility, new_global_slot, neighbors):
    count = lax.axis_size("blk")
    here = lax.axis_index("blk").astype(jnp.int32).reshape(1)
    olds = (old_phase, old_solute, old_mobility)
    devices = range(count)

    def sent(block, route):
        return lax.ppermute(block, "blk", [(p, q) for p, q in route if 0 <= q < count])

    def outward(p):
        return -2 if p % 2 == 0 else 2

    far_send, merge_send, final_send = pl.pallas_call(
        pack_kernel,
        grid=(CHUNKS,),
        in_specs=[SMEM, SMEM] + [OLD_SPEC] * 3,
        out_specs=[CHUNK_SPEC] * 3,
        out_shape=[shaped(EDGE)] * 3,
        compiler_params=PARAMS,
        cost_estimate=cost(10**6, 15 * MB),
        name="pack",
    )(here, new_global_slot, *olds)

    merge_got = sent(merge_send, [(p, p ^ 1) for p in devices])
    far_got = sent(far_send, [(p, p + outward(p)) for p in devices])
    final_got = sent(final_send, [(p, p ^ 1) for p in devices])

    edge_send, rest_send = pl.pallas_call(
        relay_kernel,
        grid=(CHUNKS,),
        in_specs=[SMEM, SMEM] + [OLD_SPEC] * 3 + [CHUNK_SPEC],
        out_specs=[EDGE_SPEC, REST_SPEC],
        out_shape=[shaped(2 * CHUNK_PLANES), shaped(EDGE - 2 * CHUNK_PLANES)],
        compiler_params=PARAMS,
        cost_estimate=cost(10**6, 12 * MB),
        name="relay",
    )(here, new_global_slot, *olds, merge_got)
    edge_got = sent(edge_send, [(p, p - outward(p)) for p in devices])
    rest_got = sent(rest_send, [(p, p - outward(p)) for p in devices])

    partial_sum, low, high = pl.pallas_call(
        gather_kernel,
        grid=(CHUNKS,),
        in_specs=[SMEM, SMEM] + [OLD_SPEC] * 3 + [CHUNK_SPEC, CHUNK_SPEC, EDGE_SPEC],
        out_specs=[CHUNK_SPEC, FACE_SPEC, FACE_SPEC],
        out_shape=[shaped(EDGE), shaped(HALO), shaped(HALO)],
        compiler_params=PARAMS,
        cost_estimate=cost(10**6, 15 * MB),
        name="gather",
    )(here, new_global_slot, *olds, final_got, far_got, edge_got)
    below = sent(high, [(p, p + 1) for p in devices])
    above = sent(low, [(p, p - 1) for p in devices])

    state = pltpu.VMEM((EXT, CAP, FACE), jnp.float32)
    phase, solute = pl.pallas_call(
        step_kernel,
        in_specs=[SMEM] + [VMEM] * 5,
        out_specs=[VMEM] * 2,
        out_shape=[jax.ShapeDtypeStruct((CAP, CELLS), jnp.float32)] * 2,
        scratch_shapes=[state] * 7,
        compiler_params=PARAMS,
        cost_estimate=cost(40 * 10**6, 8 * MB),
        name="substeps",
    )(here, partial_sum, rest_got, below, above, neighbors)
    return phase, solute


def solution(mesh):
    placed = (P("blk", None), P("blk", None), P("blk", None), P("blk"), P("blk", None))
    return jax.shard_map(
        on_device,
        mesh=mesh,
        in_specs=placed,
        out_specs=(P("blk", None), P("blk", None)),
        check_vma=False,
    )
```

profile of v0, /device:TPU:24, one launch (start us, length us, event | category | flops | bytes accessed | tf_op | source)
XLA Modules:
  0.0 123.8 jit_solution(15560264235880395573)
XLA Ops:
  0.6 0.0 copy-start
  0.6 1.6 %copy-done = f32[16,32768]{1,0:T(8,128)S(1)} copy-done((f32[16,32768]{1,0:T(8,128)S(1)}, f32[16,32768]{1,0:T(8,128)}, u32[]{:S(2)}) %copy-start) | copy-done | bytes 2097176
  2.2 0.0 copy-start.1
  2.2 1.6 %copy-done.1 = f32[16,32768]{1,0:T(8,128)S(1)} copy-done((f32[16,32768]{1,0:T(8,128)S(1)}, f32[16,32768]{1,0:T(8,128)}, u32[]{:S(2)}) %copy-start.1) | copy-done | bytes 2097176
  3.8 0.0 copy-start.2
  3.8 1.6 %copy-done.2 = f32[16,32768]{1,0:T(8,128)S(1)} copy-done((f32[16,32768]{1,0:T(8,128)S(1)}, f32[16,32768]{1,0:T(8,128)}, u32[]{:S(2)}) %copy-start.2) | copy-done | bytes 2097176
  5.4 0.0 copy-start.3
  5.4 0.7 copy-done.3
  6.1 2.9 %pack.1 = (f32[3,8,32768]{2,1,0:T(8,128)S(1)}, f32[3,8,32768]{2,1,0:T(8,128)S(1)}, f32[3,8,32768]{2,1,0:T(8,128)S(1)}) custom-call(s32[1]{0:T(128)} %bitcast.here_ref, s32[16]{0:T(128)S(1)} %copy-done.3, f32[16,32768]{1,0:T(8,128)S(1)} %copy-done, f32[16,32768]{1,0:T(8,128)S(1)} %copy-done.1, f32[16,32768]{1,0:T(8,128)S(1)} %copy-done.2), custom_call_target="tpu_custom_call" | custom-call | flops 1000000 | bytes 15728640 | tf_op jit(solution)/shard_map/pack/pallas_call | solution.py:286
  9.0 0.1 collective-permute-start.2
  9.1 0.5 collective-permute-start
  9.6 8.3 %collective-permute-start.1 = (f32[3,8,32768]{2,1,0:T(8,128)S(1)}, f32[3,8,32768]{2,1,0:T(8,128)S(1)}, u32[]{:S(2)}, u32[]{:S(2)}) collective-permute-start(f32[3,8,32768]{2,1,0:T(8,128)S(1)} %get-tuple-element.11), channel_id=1, source_target_pairs={{1,3},{2,0},{3,5},{4,2},{5,7},{6,4},{7,9},{8,6},{9,11},{10,8},{11,... | collective-permute-start | bytes 9437192 | tf_op jit(solution)/shard_map/ppermute | solution.py:281
  17.9 0.0 collective-permute-done.2.merge_ref
  17.9 2.6 %relay.1 = (f32[3,8,8192]{2,1,0:T(8,128)S(1)}, f32[3,8,24576]{2,1,0:T(8,128)S(1)}) custom-call(s32[1]{0:T(128)} %bitcast.here_ref, s32[16]{0:T(128)S(1)} %copy-done.3, f32[16,32768]{1,0:T(8,128)S(1)} %copy-done, f32[16,32768]{1,0:T(8,128)S(1)} %copy-done.1, f32[16,32768]{1,0:T(8,128)S(1)} %copy-done.2, f32[3,8,32768]{2,1,0:T(8,128)S(1)} %collective-permute-done.2.merge_ref), custom_call_target="tpu_custom_call" | custom-call | flops 1000000 | bytes 12582912 | tf_op jit(solution)/shard_map/relay/pallas_call | solution.py:301
  20.5 1.9 %collective-permute-start.4 = (f32[3,8,24576]{2,1,0:T(8,128)S(1)}, f32[3,8,24576]{2,1,0:T(8,128)S(1)}, u32[]{:S(2)}, u32[]{:S(2)}) collective-permute-start(f32[3,8,24576]{2,1,0:T(8,128)S(1)} %get-tuple-element.15), channel_id=1, source_target_pairs={{0,2},{2,4},{3,1},{4,6},{5,3},{6,8},{7,5},{8,10},{9,7},{10,12},{11... | collective-permute-start | bytes 7077896 | tf_op jit(solution)/shard_map/ppermute | solution.py:281
  22.5 0.0 copy-start.4
  22.5 2.5 %collective-permute-start.3 = (f32[3,8,8192]{2,1,0:T(8,128)S(1)}, f32[3,8,8192]{2,1,0:T(8,128)S(1)}, u32[]{:S(2)}, u32[]{:S(2)}) collective-permute-start(f32[3,8,8192]{2,1,0:T(8,128)S(1)} %get-tuple-element.13), channel_id=1, source_target_pairs={{0,2},{2,4},{3,1},{4,6},{5,3},{6,8},{7,5},{8,10},{9,7},{10,12},{11... | collective-permute-start | bytes 2359304 | tf_op jit(solution)/shard_map/ppermute | solution.py:281
  25.0 0.0 collective-permute-done.final_ref
  25.0 54.3 %collective-permute-done.1.far_ref = f32[3,8,32768]{2,1,0:T(8,128)S(1)} collective-permute-done((f32[3,8,32768]{2,1,0:T(8,128)S(1)}, f32[3,8,32768]{2,1,0:T(8,128)S(1)}, u32[]{:S(2)}, u32[]{:S(2)}) %collective-permute-start.1) | collective-permute-done | bytes 3145760 | tf_op jit(solution)/shard_map/ppermute | solution.py:281
  79.3 6.9 %collective-permute-done.3.edge_ref = f32[3,8,8192]{2,1,0:T(8,128)S(1)} collective-permute-done((f32[3,8,8192]{2,1,0:T(8,128)S(1)}, f32[3,8,8192]{2,1,0:T(8,128)S(1)}, u32[]{:S(2)}, u32[]{:S(2)}) %collective-permute-start.3) | collective-permute-done | bytes 786464 | tf_op jit(solution)/shard_map/ppermute | solution.py:281
  86.2 3.0 %gather.1 = (f32[3,8,32768]{2,1,0:T(8,128)S(1)}, f32[3,8,3072]{2,1,0:T(8,128)S(1)}, f32[3,8,3072]{2,1,0:T(8,128)S(1)}) custom-call(s32[1]{0:T(128)} %bitcast.here_ref, s32[16]{0:T(128)S(1)} %copy-done.3, f32[16,32768]{1,0:T(8,128)S(1)} %copy-done, f32[16,32768]{1,0:T(8,128)S(1)} %copy-done.1, f32[16,32768]{1,0:T(8,128)S(1)} %copy-done.2, ...), custom_call_target="tpu_custom_call" | custom-call | flops 1000000 | bytes 15728640 | tf_op jit(solution)/shard_map/gather/pallas_call | solution.py:314
  89.2 2.2 %collective-permute-start.5 = (f32[3,8,3072]{2,1,0:T(8,128)S(1)}, f32[3,8,3072]{2,1,0:T(8,128)S(1)}, u32[]{:S(2)}, u32[]{:S(2)}) collective-permute-start(f32[3,8,3072]{2,1,0:T(8,128)S(1)} %get-tuple-element.16), channel_id=1, source_target_pairs={{0,1},{1,2},{2,3},{3,4},{4,5},{5,6},{6,7},{7,8},{8,9},{9,10},{10,1... | collective-permute-start | bytes 884744 | tf_op jit(solution)/shard_map/ppermute | solution.py:281
  91.4 7.9 %collective-permute-start.6 = (f32[3,8,3072]{2,1,0:T(8,128)S(1)}, f32[3,8,3072]{2,1,0:T(8,128)S(1)}, u32[]{:S(2)}, u32[]{:S(2)}) collective-permute-start(f32[3,8,3072]{2,1,0:T(8,128)S(1)} %get-tuple-element.17), channel_id=1, source_target_pairs={{1,0},{2,1},{3,2},{4,3},{5,4},{6,5},{7,6},{8,7},{9,8},{10,9},{11,1... | collective-permute-start | bytes 884744 | tf_op jit(solution)/shard_map/ppermute | solution.py:281
  99.3 2.5 %collective-permute-done.5.below_ref = f32[3,8,3072]{2,1,0:T(8,128)S(1)} collective-permute-done((f32[3,8,3072]{2,1,0:T(8,128)S(1)}, f32[3,8,3072]{2,1,0:T(8,128)S(1)}, u32[]{:S(2)}, u32[]{:S(2)}) %collective-permute-start.5) | collective-permute-done | bytes 294944 | tf_op jit(solution)/shard_map/ppermute | solution.py:281
  101.8 1.8 %collective-permute-done.6.above_ref = f32[3,8,3072]{2,1,0:T(8,128)S(1)} collective-permute-done((f32[3,8,3072]{2,1,0:T(8,128)S(1)}, f32[3,8,3072]{2,1,0:T(8,128)S(1)}, u32[]{:S(2)}, u32[]{:S(2)}) %collective-permute-start.6) | collective-permute-done | bytes 294944 | tf_op jit(solution)/shard_map/ppermute | solution.py:281
  103.5 0.0 collective-permute-done.4.rest_ref
  103.5 0.0 copy-done.4
  103.5 20.3 %substeps.1 = (f32[8,32768]{1,0:T(8,128)}, f32[8,32768]{1,0:T(8,128)}) custom-call(s32[1]{0:T(128)} %bitcast.here_ref, f32[3,8,32768]{2,1,0:T(8,128)S(1)} %get-tuple-element.14.sum_ref, f32[3,8,24576]{2,1,0:T(8,128)S(1)} %collective-permute-done.4.rest_ref, f32[3,8,3072]{2,1,0:T(8,128)S(1)} %collective-permute-done.5.below_ref, ...), custom_call_target="tpu_custom_call" | custom-call | flops 40000000 | bytes 8388608 | tf_op jit(solution)/shard_map/substeps/pallas_call | solution.py:328
Async XLA Ops:
  0.6 1.6 %copy-start = (f32[16,32768]{1,0:T(8,128)S(1)}, f32[16,32768]{1,0:T(8,128)}, u32[]{:S(2)}) copy-start(f32[16,32768]{1,0:T(8,128)} %phi_ref.5) | copy-start | bytes 6291460
  2.2 1.6 %copy-start.1 = (f32[16,32768]{1,0:T(8,128)S(1)}, f32[16,32768]{1,0:T(8,128)}, u32[]{:S(2)}) copy-start(f32[16,32768]{1,0:T(8,128)} %conc_ref.5) | copy-start | bytes 6291460
  3.8 1.6 %copy-start.2 = (f32[16,32768]{1,0:T(8,128)S(1)}, f32[16,32768]{1,0:T(8,128)}, u32[]{:S(2)}) copy-start(f32[16,32768]{1,0:T(8,128)} %mob_ref.5) | copy-start | bytes 6291460
  5.4 0.7 copy-start.3
  9.0 8.9 %collective-permute-start.2 = (f32[3,8,32768]{2,1,0:T(8,128)S(1)}, f32[3,8,32768]{2,1,0:T(8,128)S(1)}, u32[]{:S(2)}, u32[]{:S(2)}) collective-permute-start(f32[3,8,32768]{2,1,0:T(8,128)S(1)} %get-tuple-element.12), channel_id=1, source_target_pairs={{0,1},{1,0},{2,3},{3,2},{4,5},{5,4},{6,7},{7,6},{8,9},{9,8},{10,11... | collective-permute-start | bytes 9437192 | tf_op jit(solution)/shard_map/ppermute | solution.py:281
  9.1 16.0 %collective-permute-start = (f32[3,8,32768]{2,1,0:T(8,128)S(1)}, f32[3,8,32768]{2,1,0:T(8,128)S(1)}, u32[]{:S(2)}, u32[]{:S(2)}) collective-permute-start(f32[3,8,32768]{2,1,0:T(8,128)S(1)} %get-tuple-element.10), channel_id=1, source_target_pairs={{0,1},{1,0},{2,3},{3,2},{4,5},{5,4},{6,7},{7,6},{8,9},{9,8},{10,11... | collective-permute-start | bytes 9437192 | tf_op jit(solution)/shard_map/ppermute | solution.py:281
  9.6 69.8 %collective-permute-start.1 = (f32[3,8,32768]{2,1,0:T(8,128)S(1)}, f32[3,8,32768]{2,1,0:T(8,128)S(1)}, u32[]{:S(2)}, u32[]{:S(2)}) collective-permute-start(f32[3,8,32768]{2,1,0:T(8,128)S(1)} %get-tuple-element.11), channel_id=1, source_target_pairs={{1,3},{2,0},{3,5},{4,2},{5,7},{6,4},{7,9},{8,6},{9,11},{10,8},{11,... | collective-permute-start | bytes 9437192 | tf_op jit(solution)/shard_map/ppermute | solution.py:281
  20.5 83.0 %collective-permute-start.4 = (f32[3,8,24576]{2,1,0:T(8,128)S(1)}, f32[3,8,24576]{2,1,0:T(8,128)S(1)}, u32[]{:S(2)}, u32[]{:S(2)}) collective-permute-start(f32[3,8,24576]{2,1,0:T(8,128)S(1)} %get-tuple-element.15), channel_id=1, source_target_pairs={{0,2},{2,4},{3,1},{4,6},{5,3},{6,8},{7,5},{8,10},{9,7},{10,12},{11... | collective-permute-start | bytes 7077896 | tf_op jit(solution)/shard_map/ppermute | solution.py:281
  22.5 81.1 %copy-start.4 = (s32[8,6]{1,0:T(8,128)S(1)}, s32[8,6]{1,0:T(8,128)}, u32[]{:S(2)}) copy-start(s32[8,6]{1,0:T(8,128)} %nbr_ref.1) | copy-start | bytes 580
  22.5 63.7 %collective-permute-start.3 = (f32[3,8,8192]{2,1,0:T(8,128)S(1)}, f32[3,8,8192]{2,1,0:T(8,128)S(1)}, u32[]{:S(2)}, u32[]{:S(2)}) collective-permute-start(f32[3,8,8192]{2,1,0:T(8,128)S(1)} %get-tuple-element.13), channel_id=1, source_target_pairs={{0,2},{2,4},{3,1},{4,6},{5,3},{6,8},{7,5},{8,10},{9,7},{10,12},{11... | collective-permute-start | bytes 2359304 | tf_op jit(solution)/shard_map/ppermute | solution.py:281
  89.2 12.6 %collective-permute-start.5 = (f32[3,8,3072]{2,1,0:T(8,128)S(1)}, f32[3,8,3072]{2,1,0:T(8,128)S(1)}, u32[]{:S(2)}, u32[]{:S(2)}) collective-permute-start(f32[3,8,3072]{2,1,0:T(8,128)S(1)} %get-tuple-element.16), channel_id=1, source_target_pairs={{0,1},{1,2},{2,3},{3,4},{4,5},{5,6},{6,7},{7,8},{8,9},{9,10},{10,1... | collective-permute-start | bytes 884744 | tf_op jit(solution)/shard_map/ppermute | solution.py:281
  91.4 12.2 %collective-permute-start.6 = (f32[3,8,3072]{2,1,0:T(8,128)S(1)}, f32[3,8,3072]{2,1,0:T(8,128)S(1)}, u32[]{:S(2)}, u32[]{:S(2)}) collective-permute-start(f32[3,8,3072]{2,1,0:T(8,128)S(1)} %get-tuple-element.17), channel_id=1, source_target_pairs={{1,0},{2,1},{3,2},{4,3},{5,4},{6,5},{7,6},{8,7},{9,8},{10,9},{11,1... | collective-permute-start | bytes 884744 | tf_op jit(solution)/shard_map/ppermute | solution.py:281
where the time goes:
time: 124 us
  waiting for transfers between devices  65.4 us (53%)
  Pallas kernels  28.8 us (23%)
  starting transfers between devices  23.4 us (19%)
  local copies, waits for them, and re-layouts  5.43 us (4%)
    ppermute x7, waiting for transfers between devices, sent(): lax.ppermute(block, 'blk', [(p, q) for p, q in route if 0 <= q < count])  65.4 us
    ppermute x7, starting transfers between devices, sent(): lax.ppermute(block, 'blk', [(p, q) for p, q in route if 0 <= q < count])  23.4 us
    pallas_call x1, Pallas kernels, on_device(): pl.pallas_call(step_kernel, in_specs=[SMEM] + [VMEM] * 5, out_specs=[VMEM...  20.3 us
    unnamed x10, local copies, waits for them, and re-layouts  5.43 us
    pallas_call x1, Pallas kernels, on_device(): pl.pallas_call(gather_kernel, grid=(CHUNKS,), in_specs=[SMEM, SMEM] + [OL...  2.98 us
    pallas_call x1, Pallas kernels, on_device(): pl.pallas_call(pack_kernel, grid=(CHUNKS,), in_specs=[SMEM, SMEM] + [OLD_...  2.89 us
    pallas_call x1, Pallas kernels, on_device(): pl.pallas_call(relay_kernel, grid=(CHUNKS,), in_specs=[SMEM, SMEM] + [OLD...  2.65 us
  transfers between devices with their start and end apart: 7, of which 4 were waited for; matrix products, arithmetic and copies ran while one was open for 0% of the time, Pallas kernels for 5%

commit v1 on v0

v1 whole, which is shorter than its diff:
```python
import functools

import jax
import jax.numpy as jnp
from jax import lax
from jax.experimental import pallas as pl
from jax.experimental.pallas import tpu as pltpu
from jax.sharding import PartitionSpec as P

EDGE = 32
FACE = EDGE * EDGE
CELLS = EDGE * FACE
CAP = 8
OLD = 16
FIELDS = 3
HALO = 3
CHUNK_PLANES = 4
CHUNK = CHUNK_PLANES * FACE
CHUNKS = EDGE // CHUNK_PLANES
LANES = 128
EXT = EDGE + 2 * HALO
MID = 16
LATE = EDGE - 2 * CHUNK_PLANES - MID
MID_CHUNKS = MID // CHUNK_PLANES
LATE_CHUNKS = LATE // CHUNK_PLANES
VREGS = FACE // LANES

time_step = 0.15
coupling = 1.5


def windows(slot_ref, here):
    first = slot_ref[0]
    count = jnp.int32(0)
    for i in range(OLD):
        count += (slot_ref[i] >= 0).astype(jnp.int32)
    amount = jnp.bitwise_and(first, CAP - 1)
    row = lax.broadcasted_iota(jnp.int32, (CAP, LANES), 0)

    def masks(k):
        index = row + ((here + k) * CAP - first)
        low = (index >= 0) & (index < CAP) & (index < count)
        high = (index >= CAP) & (index < count)
        return low, high

    return amount, masks


def picked(masks, low_rows, high_rows):
    low, high = masks
    return jnp.where(low, low_rows, jnp.where(high, high_rows, 0.0))


def side_of(here):
    return jnp.where(jnp.bitwise_and(here, 1) == 0, -1, 1)


def vregs_of(planes):
    return [pl.ds(v * LANES, LANES) for v in range(planes * VREGS)]


def aligned(ref, lanes, amount):
    return pltpu.roll(ref[0:CAP, lanes], amount, 0), pltpu.roll(ref[CAP:OLD, lanes], amount, 0)


def load_slots(slot_hbm, slot_ref, sem):
    copy = pltpu.make_async_copy(slot_hbm, slot_ref, sem)
    copy.start()
    copy.wait()


def chunk_at(i):
    return jnp.where(i == 0, 0, jnp.where(i == 1, CHUNKS - 1, i - 1))


def into_parts(i, fill, *refs):
    edge_ref, mid_ref, late_ref = refs
    pl.when(i < 2)(lambda: fill(edge_ref))
    pl.when((i >= 2) & (i < 2 + MID_CHUNKS))(lambda: fill(mid_ref))
    pl.when(i >= 2 + MID_CHUNKS)(lambda: fill(late_ref))


def pack_kernel(here_ref, slot_hbm, phi_hbm, conc_hbm, mob_hbm, pair_hbm, far_hbm, late_hbm, slot_ref, sem):
    load_slots(slot_hbm, slot_ref, sem)
    here = here_ref[0]
    side = side_of(here)
    amount, masks = windows(slot_ref, here)
    far, merge, final = masks(2 * side), masks(side), masks(-side)

    def body(phi_ref, conc_ref, mob_ref, pair_ref, far_ref, late_ref):
        def fill(out_ref):
            for f, ref in enumerate((phi_ref, conc_ref, mob_ref)):
                for lanes in vregs_of(CHUNK_PLANES):
                    rows = aligned(ref, lanes, amount)
                    pair_ref[f, :, lanes] = picked(merge, *rows)
                    pair_ref[FIELDS + f, :, lanes] = picked(final, *rows)
                    out_ref[f, :, lanes] = picked(far, *rows)

        i = pl.program_id(0)
        pl.when(i < 2 + MID_CHUNKS)(lambda: fill(far_ref))
        pl.when(i >= 2 + MID_CHUNKS)(lambda: fill(late_ref))

    pltpu.emit_pipeline(
        body,
        grid=(CHUNKS,),
        in_specs=[pl.BlockSpec((OLD, CHUNK), lambda i: (0, chunk_at(i)))] * 3,
        out_specs=[
            pl.BlockSpec((2 * FIELDS, CAP, CHUNK), lambda i: (0, 0, chunk_at(i))),
            pl.BlockSpec((FIELDS, CAP, CHUNK), lambda i: (0, 0, jnp.minimum(i, 1 + MID_CHUNKS))),
            LATE_SPEC,
        ],
    )(phi_hbm, conc_hbm, mob_hbm, pair_hbm, far_hbm, late_hbm)


def relay_kernel(here_ref, slot_ref, phi_ref, conc_ref, mob_ref, merge_ref, *out_refs):
    here = here_ref[0]
    amount, masks = windows(slot_ref, here)
    back = masks(-2 * side_of(here))

    def fill(out_ref):
        for f, ref in enumerate((phi_ref, conc_ref, mob_ref)):
            for lanes in vregs_of(CHUNK_PLANES):
                out_ref[f, :, lanes] = picked(back, *aligned(ref, lanes, amount)) + merge_ref[f, :, lanes]

    into_parts(pl.program_id(0), fill, *out_refs)


def stay_kernel(here_ref, slot_ref, phi_ref, conc_ref, mob_ref, final_ref, *out_refs):
    here = here_ref[0]
    amount, masks = windows(slot_ref, here)
    own = masks(0)

    def fill(out_ref):
        for f, ref in enumerate((phi_ref, conc_ref, mob_ref)):
            for lanes in vregs_of(CHUNK_PLANES):
                out_ref[f, :, lanes] = picked(own, *aligned(ref, lanes, amount)) + final_ref[f, :, lanes]

    into_parts(pl.program_id(0), fill, *out_refs)


def face_kernel(stay_ref, far_ref, back_ref, edge_ref, low_ref, high_ref):
    first_high = (2 * CHUNK_PLANES - HALO) * FACE
    for f in range(FIELDS):
        for v in range(2 * CHUNK_PLANES * VREGS):
            lanes = pl.ds(v * LANES, LANES)
            value = stay_ref[f, :, lanes] + far_ref[f, :, lanes] + back_ref[f, :, lanes]
            edge_ref[f, :, lanes] = value
            at = v * LANES
            if at < HALO * FACE:
                low_ref[f, :, lanes] = value
            if at >= first_high:
                high_ref[f, :, pl.ds(at - first_high, LANES)] = value


class Stencil:
    def __init__(self, here, nbr):
        base = here * CAP
        self.nbr = nbr
        lane = lax.broadcasted_iota(jnp.int32, (CAP, LANES), 1)
        z = jnp.bitwise_and(lane, EDGE - 1)
        self.z_first, self.z_last = z == 0, z == EDGE - 1
        self.y_first, self.y_last = lane < EDGE, lane >= LANES - EDGE
        self.below_x, self.has_below_x = self.column(0, base - CAP)
        self.above_x, self.has_above_x = self.column(1, base + CAP)
        self.below_y, self.has_below_y = self.column(2, base)
        self.above_y, self.has_above_y = self.column(3, base)
        self.below_z, _ = self.column(4, base)
        self.above_z, _ = self.column(5, base)

    def column(self, c, start):
        wide = jnp.broadcast_to(self.nbr[:, c : c + 1], (CAP, LANES))
        valid = wide >= 0
        return jnp.where(valid, wide - start, 0), valid

    @staticmethod
    def rows(x, index):
        return jnp.take_along_axis(x, index, axis=0, mode="promise_in_bounds")

    def laplacian(self, ref, x):
        centre = [ref[x, :, pl.ds(v * LANES, LANES)] for v in range(VREGS)]
        lower = [pltpu.roll(c, EDGE, 1) for c in centre]
        upper = [pltpu.roll(c, LANES - EDGE, 1) for c in centre]
        out = []
        for v in range(VREGS):
            c = centre[v]
            lanes = pl.ds(v * LANES, LANES)
            if v:
                from_lower = lower[v - 1]
            else:
                from_lower = jnp.where(self.has_below_y, self.rows(lower[-1], self.below_y), c)
            if v < VREGS - 1:
                from_upper = upper[v + 1]
            else:
                from_upper = jnp.where(self.has_above_y, self.rows(upper[0], self.above_y), c)
            prev_y = jnp.where(self.y_first, from_lower, lower[v])
            next_y = jnp.where(self.y_last, from_upper, upper[v])
            prev_z = jnp.where(self.z_first, pltpu.roll(self.rows(c, self.below_z), LANES - EDGE + 1, 1), pltpu.roll(c, 1, 1))
            next_z = jnp.where(self.z_last, pltpu.roll(self.rows(c, self.above_z), EDGE - 1, 1), pltpu.roll(c, LANES - 1, 1))
            total = (ref[x - 1, :, lanes] + ref[x + 1, :, lanes]) + (prev_y + next_y) + (prev_z + next_z)
            out.append(total - 6.0 * c)
        return out, centre

    def advance(self, phi_ref, conc_ref, mob_ref, x, store):
        lapl_phi, phis = self.laplacian(phi_ref, x)
        lapl_conc, concs = self.laplacian(conc_ref, x)
        for v in range(VREGS):
            phi, conc = phis[v], concs[v]
            square = phi * phi
            wetting = 1.0 - square
            drive = lapl_phi[v] + phi - square * phi - coupling * conc * wetting * wetting
            change = time_step * mob_ref[x, :, pl.ds(v * LANES, LANES)] * drive
            store(v, phi + change, conc + time_step * lapl_conc[v] + 0.5 * change)

    def sweep(self, first, last, unroll, source, mob_ref, target, shift=None):
        phi_ref, conc_ref = source
        phi_out, conc_out = target

        def one(x):
            def store(v, phi, conc):
                if shift is None:
                    where = (x, slice(None), pl.ds(v * LANES, LANES))
                else:
                    where = (slice(None), pl.ds(pl.multiple_of((x - shift) * FACE + v * LANES, LANES), LANES))
                phi_out[where] = phi
                conc_out[where] = conc

            self.advance(phi_ref, conc_ref, mob_ref, x, store)

        whole = first + (last - first) // unroll * unroll
        if whole > first:

            @pl.loop(0, (whole - first) // unroll)
            def _(i):
                for u in range(unroll):
                    one(first + i * unroll + u)

        for x in range(whole, last):
            one(x)


def place(states, planes, at, *parts):
    for f, ref in enumerate(states):

        @pl.loop(0, planes)
        def _(x):
            for v in range(VREGS):
                lanes = pl.ds(pl.multiple_of(x * FACE + v * LANES, LANES), LANES)
                value = parts[0][f, :, lanes]
                for part in parts[1:]:
                    value = value + part[f, :, lanes]
                ref[x + at, :, pl.ds(v * LANES, LANES)] = value


MID_AT = HALO + CHUNK_PLANES
LATE_AT = MID_AT + MID
TOP_AT = LATE_AT + LATE


def early_kernel(
    here_ref, edge_ref, stay_ref, far_ref, back_ref, below_ref, above_ref, nbr_ref,
    phase_ref, solute_ref, kept0_ref, kept1_ref, kept2_ref,
    phi0, conc0, mob, phi1, conc1, phi2, conc2,
):
    st = Stencil(here_ref[0], nbr_ref[...])
    states = (phi0, conc0, mob)
    for f, ref in enumerate(states):
        for d in range(2 * CHUNK_PLANES):
            at = HALO + d if d < CHUNK_PLANES else TOP_AT + d - CHUNK_PLANES
            for v in range(VREGS):
                ref[at, :, pl.ds(v * LANES, LANES)] = edge_ref[f, :, pl.ds(d * FACE + v * LANES, LANES)]
    place(states, MID, MID_AT, stay_ref, far_ref.at[:, :, pl.ds(2 * CHUNK, MID * FACE)], back_ref)
    for f, ref in enumerate(states):
        for d in range(HALO):
            for v in range(VREGS):
                lanes = pl.ds(v * LANES, LANES)
                part = pl.ds(d * FACE + v * LANES, LANES)
                mirror_low = ref[2 * HALO - 1 - d, :, lanes]
                ref[d, :, lanes] = jnp.where(st.has_below_x, st.rows(below_ref[f, :, part], st.below_x), mirror_low)
                mirror_high = ref[EDGE + HALO - 1 - d, :, lanes]
                ref[EDGE + HALO + d, :, lanes] = jnp.where(st.has_above_x, st.rows(above_ref[f, :, part], st.above_x), mirror_high)
    st.sweep(1, LATE_AT - 1, 4, (phi0, conc0), mob, (phi1, conc1))
    st.sweep(TOP_AT + 1, EXT - 1, 5, (phi0, conc0), mob, (phi1, conc1))
    st.sweep(2, LATE_AT - 2, 4, (phi1, conc1), mob, (phi2, conc2))
    st.sweep(TOP_AT + 2, EXT - 2, 3, (phi1, conc1), mob, (phi2, conc2))
    st.sweep(HALO, LATE_AT - 3, 4, (phi2, conc2), mob, (phase_ref, solute_ref), HALO)
    st.sweep(TOP_AT + 3, EXT - 3, 1, (phi2, conc2), mob, (phase_ref, solute_ref), HALO)
    for f, ref in enumerate(states):
        for n, x in enumerate((*range(LATE_AT - 3, LATE_AT), *range(TOP_AT, TOP_AT + 3))):
            kept0_ref[f, n] = ref[x]
    for f, ref in enumerate((phi1, conc1)):
        for n, x in enumerate((LATE_AT - 3, LATE_AT - 2, TOP_AT + 1, TOP_AT + 2)):
            kept1_ref[f, n] = ref[x]
    for f, ref in enumerate((phi2, conc2)):
        for n, x in enumerate((LATE_AT - 4, LATE_AT - 3, TOP_AT + 2, TOP_AT + 3)):
            kept2_ref[f, n] = ref[x]


BACK = LATE_AT - 4
LATE_PLANES = TOP_AT + 4 - BACK
OUT_FIRST = LATE_AT - 3
OUT_PLANES = TOP_AT + 3 - OUT_FIRST


def late_kernel(
    here_ref, stay_ref, far_ref, back_ref, nbr_ref, kept0_ref, kept1_ref, kept2_ref, _phase_in, _solute_in,
    phase_hbm, solute_hbm,
    phi0, conc0, mob, phi1, conc1, phi2, conc2, phase_ref, solute_ref, sems,
):
    st = Stencil(here_ref[0], nbr_ref[...])
    states = (phi0, conc0, mob)
    first, last = LATE_AT - BACK, TOP_AT - BACK
    for f, ref in enumerate(states):
        for n, x in enumerate((*range(first - 3, first), *range(last, last + 3))):
            ref[x] = kept0_ref[f, n]
    for f, ref in enumerate((phi1, conc1)):
        for n, x in enumerate((first - 3, first - 2, last + 1, last + 2)):
            ref[x] = kept1_ref[f, n]
    for f, ref in enumerate((phi2, conc2)):
        for n, x in enumerate((first - 4, first - 3, last + 2, last + 3)):
            ref[x] = kept2_ref[f, n]
    place(states, LATE, first, stay_ref, far_ref, back_ref)
    st.sweep(first - 1, last + 1, 5, (phi0, conc0), mob, (phi1, conc1))
    st.sweep(first - 2, last + 2, 4, (phi1, conc1), mob, (phi2, conc2))
    st.sweep(first - 3, last + 3, 7, (phi2, conc2), mob, (phase_ref, solute_ref), first - 3)
    copies = []
    for n, (ref, hbm) in enumerate(((phase_ref, phase_hbm), (solute_ref, solute_hbm))):
        lanes = pl.ds((OUT_FIRST - HALO) * FACE, OUT_PLANES * FACE)
        copies.append(pltpu.make_async_copy(ref, hbm.at[:, lanes], sems.at[n]))
    for copy in copies:
        copy.start()
    for copy in copies:
        copy.wait()


SMEM = pl.BlockSpec(memory_space=pltpu.SMEM)
VMEM = pl.BlockSpec(memory_space=pltpu.VMEM)
HBM = pl.BlockSpec(memory_space=pltpu.HBM)
ANY = pl.BlockSpec(memory_space=pl.ANY)
PARAMS = pltpu.CompilerParams(vmem_limit_bytes=32 * 2**20)


def shaped(planes, fields=FIELDS):
    return jax.ShapeDtypeStruct((fields, CAP, planes * FACE), jnp.float32)


def cost(moved, flops=10**6):
    return pl.CostEstimate(flops=flops, bytes_accessed=moved, transcendentals=0)


OLD_SPEC = pl.BlockSpec((OLD, CHUNK), lambda i: (0, chunk_at(i)))
EDGE_SPEC = pl.BlockSpec((FIELDS, CAP, CHUNK), lambda i: (0, 0, jnp.minimum(i, 1)))
MID_SPEC = pl.BlockSpec((FIELDS, CAP, CHUNK), lambda i: (0, 0, jnp.clip(i - 2, 0, MID_CHUNKS - 1)))
LATE_SPEC = pl.BlockSpec((FIELDS, CAP, CHUNK), lambda i: (0, 0, jnp.clip(i - 2 - MID_CHUNKS, 0, LATE_CHUNKS - 1)))
MERGE_SPEC = pl.BlockSpec((FIELDS, CAP, CHUNK), lambda i: (0, 0, chunk_at(i)))
FINAL_SPEC = pl.BlockSpec((FIELDS, CAP, CHUNK), lambda i: (1, 0, chunk_at(i)))
EDGES = pl.BlockSpec((FIELDS, CAP, 2 * CHUNK), lambda i: (0, 0, 0))
FACES = pl.BlockSpec((FIELDS, CAP, HALO * FACE), lambda i: (0, 0, 0))
MB = 2**20


def on_device(old_phase, old_solute, old_mobility, new_global_slot, neighbors):
    count = lax.axis_size("blk")
    here = lax.axis_index("blk").astype(jnp.int32).reshape(1)
    olds = tuple(pltpu.with_memory_space_constraint(x, pltpu.HBM) for x in (old_phase, old_solute, old_mobility))
    devices = range(count)

    def sent(block, route):
        return lax.ppermute(block, "blk", [(p, q) for p, q in route if 0 <= q < count])

    def outward(p):
        return -2 if p % 2 == 0 else 2

    partner = [(p, p ^ 1) for p in devices]
    far_route = [(p, p + outward(p)) for p in devices]
    back_route = [(p, p - outward(p)) for p in devices]

    def after(block, *others):
        return lax.optimization_barrier((block, *others))[0]

    slots_hbm = pltpu.with_memory_space_constraint(new_global_slot, pltpu.HBM)
    slot_scratch = [pltpu.SMEM((OLD,), jnp.int32), pltpu.SemaphoreType.DMA]
    pair, far_first, far_late = pl.pallas_call(
        pack_kernel,
        in_specs=[SMEM, HBM, HBM, HBM, HBM],
        out_specs=[ANY] * 3,
        out_shape=[shaped(EDGE, 2 * FIELDS), shaped(2 * CHUNK_PLANES + MID), shaped(LATE)],
        scratch_shapes=slot_scratch,
        compiler_params=PARAMS,
        cost_estimate=cost(15 * MB),
        name="pack",
    )(here, slots_hbm, *olds)
    far_first_got = sent(far_first, far_route)
    pair_got = sent(pair, partner)

    three_parts = [shaped(2 * CHUNK_PLANES), shaped(MID), shaped(LATE)]
    back_edge, back_mid, back_late = pl.pallas_call(
        relay_kernel,
        grid=(CHUNKS,),
        in_specs=[SMEM, SMEM] + [OLD_SPEC] * 3 + [MERGE_SPEC],
        out_specs=[EDGE_SPEC, MID_SPEC, LATE_SPEC],
        out_shape=three_parts,
        compiler_params=PARAMS,
        cost_estimate=cost(12 * MB),
        name="relay",
    )(here, new_global_slot, *olds, pair_got)
    back_edge_got = sent(back_edge, back_route)
    back_mid_got = sent(after(back_mid, back_edge_got), back_route)

    stay_edge, stay_mid, stay_late = pl.pallas_call(
        stay_kernel,
        grid=(CHUNKS,),
        in_specs=[SMEM, SMEM] + [OLD_SPEC] * 3 + [FINAL_SPEC],
        out_specs=[EDGE_SPEC, MID_SPEC, LATE_SPEC],
        out_shape=three_parts,
        compiler_params=PARAMS,
        cost_estimate=cost(12 * MB),
        name="stay",
    )(here, new_global_slot, *olds, pair_got)

    edge, low, high = pl.pallas_call(
        face_kernel,
        grid=(1,),
        in_specs=[EDGES] * 3,
        out_specs=[EDGES, FACES, FACES],
        out_shape=[shaped(2 * CHUNK_PLANES), shaped(HALO), shaped(HALO)],
        compiler_params=PARAMS,
        cost_estimate=cost(3 * MB),
        name="faces",
    )(stay_edge, far_first_got, back_edge_got)
    below = sent(high, [(p, p + 1) for p in devices])
    above = sent(low, [(p, p - 1) for p in devices])
    far_late_got = sent(after(far_late, low), far_route)
    back_late_got = sent(after(back_late, back_mid_got, below, above), back_route)

    state = pltpu.VMEM((EXT, CAP, FACE), jnp.float32)
    whole = jax.ShapeDtypeStruct((CAP, CELLS), jnp.float32)

    def kept(fields, planes):
        return jax.ShapeDtypeStruct((fields, planes, CAP, FACE), jnp.float32)

    phase, solute, kept0, kept1, kept2 = pl.pallas_call(
        early_kernel,
        in_specs=[SMEM] + [VMEM] * 7,
        out_specs=[VMEM] * 5,
        out_shape=[whole, whole, kept(3, 6), kept(2, 4), kept(2, 4)],
        scratch_shapes=[state] * 7,
        compiler_params=PARAMS,
        cost_estimate=cost(20 * MB),
        name="early_steps",
    )(here, edge, stay_mid, far_first_got, back_mid_got, below, above, neighbors)

    state = pltpu.VMEM((LATE_PLANES, CAP, FACE), jnp.float32)
    rows_out = pltpu.VMEM((CAP, OUT_PLANES * FACE), jnp.float32)
    phase, solute = pl.pallas_call(
        late_kernel,
        in_specs=[SMEM] + [VMEM] * 7 + [HBM] * 2,
        out_specs=[HBM] * 2,
        out_shape=[whole, whole],
        scratch_shapes=[state] * 7 + [rows_out] * 2 + [pltpu.SemaphoreType.DMA((2,))],
        input_output_aliases={8: 0, 9: 1},
        compiler_params=PARAMS,
        cost_estimate=cost(8 * MB),
        name="late_steps",
    )(here, stay_late, far_late_got, back_late_got, neighbors, kept0, kept1, kept2, phase, solute)
    return phase, solute


def solution(mesh):
    placed = (P("blk", None), P("blk", None), P("blk", None), P("blk"), P("blk", None))
    return jax.shard_map(
        on_device,
        mesh=mesh,
        in_specs=placed,
        out_specs=(P("blk", None), P("blk", None)),
        check_vma=False,
    )
```

time: 124 us -> 108 us (0.87)
  waiting for transfers between devices: 65.4 us -> 42.5 us
  starting transfers between devices: 23.4 us -> 29.8 us
  local copies, waits for them, and re-layouts: 5.43 us -> 0.01 us
  Pallas kernels: 28.8 us -> 34.1 us
    ppermute x7 -> x8, waiting for transfers between devices: 65.4 us -> 42.5 us  [sent(): lax.ppermute(block, 'blk', [(p, q) for p, q in route if 0 <= q < count])]
    ppermute x7 -> x8, starting transfers between devices: 23.4 us -> 29.8 us  [sent(): lax.ppermute(block, 'blk', [(p, q) for p, q in route if 0 <= q < count])]
    unnamed x10 -> x4, local copies, waits for them, and re-layouts: 5.43 us -> 0.01 us
    pallas_call x1, Pallas kernels: 2.65 us -> 5.65 us  [on_device(): pl.pallas_call(relay_kernel, grid=(CHUNKS,), in_specs=[SMEM, SMEM] + [OLD...]
    pallas_call x3 -> x5, Pallas kernels: 26.1 us -> 28.4 us  [the longest x1 10.1 us: on_device(): pl.pallas_call(early_kernel, in_specs=[SMEM] + [VMEM] * 7, out_specs=[VME...]
  transfers between devices with their start and end apart: 7 -> 8, of which waited for: 4 -> 6; matrix products, arithmetic and copies ran while one was open for 0% -> 0% of each run, Pallas kernels for 5% -> 20%
where the time goes in v1:
time: 108 us; the launch traced here: 107 us
  waiting for transfers between devices  42.5 us (39%)
  Pallas kernels  34.1 us (32%)
  starting transfers between devices  29.8 us (28%)
    ppermute x8, waiting for transfers between devices, sent(): lax.ppermute(block, 'blk', [(p, q) for p, q in route if 0 <= q < count])  42.5 us
    ppermute x8, starting transfers between devices, sent(): lax.ppermute(block, 'blk', [(p, q) for p, q in route if 0 <= q < count])  29.8 us
    pallas_call x1, Pallas kernels, on_device(): pl.pallas_call(early_kernel, in_specs=[SMEM] + [VMEM] * 7, out_specs=[VME...  10.1 us
    pallas_call x1, Pallas kernels, on_device(): pl.pallas_call(pack_kernel, in_specs=[SMEM, HBM, HBM, HBM, HBM], out_spec...  6.92 us
    pallas_call x1, Pallas kernels, on_device(): pl.pallas_call(stay_kernel, grid=(CHUNKS,), in_specs=[SMEM, SMEM] + [OLD_...  5.68 us
    pallas_call x1, Pallas kernels, on_device(): pl.pallas_call(relay_kernel, grid=(CHUNKS,), in_specs=[SMEM, SMEM] + [OLD...  5.65 us
    pallas_call x1, Pallas kernels, on_device(): pl.pallas_call(late_kernel, in_specs=[SMEM] + [VMEM] * 7 + [HBM] * 2, out...  5.55 us
  transfers between devices with their start and end apart: 8, of which 6 were waited for; matrix products, arithmetic and copies ran while one was open for 0% of the time, Pallas kernels for 20%

profile of v1, /device:TPU:24, one launch (start us, length us, event | category | flops | bytes accessed | tf_op | source)
XLA Modules:
  0.0 107.1 jit_solution(9090707164137290770)
XLA Ops:
  0.6 0.0 copy-start.1
  0.6 6.9 %pack.1 = (f32[6,8,32768]{2,1,0:T(8,128)S(1)}, f32[3,8,24576]{2,1,0:T(8,128)S(1)}, f32[3,8,8192]{2,1,0:T(8,128)S(1)}) custom-call(s32[1]{0:T(128)} %bitcast.here_ref, s32[16]{0:T(128)} %slot_ref.3, f32[16,32768]{1,0:T(8,128)} %phi_ref.3, f32[16,32768]{1,0:T(8,128)} %conc_ref.3, f32[16,32768]{1,0:T(8,128)} %mob_ref.3), custom_call_target="tpu_custom_call" | custom-call | flops 1000000 | bytes 15728640 | tf_op jit(solution)/shard_map/pack/pallas_call | solution.py:382
  7.6 0.1 collective-permute-start
  7.7 8.3 %collective-permute-start.1 = (f32[3,8,24576]{2,1,0:T(8,128)S(1)}, f32[3,8,24576]{2,1,0:T(8,128)S(1)}, u32[]{:S(2)}, u32[]{:S(2)}) collective-permute-start(f32[3,8,24576]{2,1,0:T(8,128)S(1)} %get-tuple-element.26), channel_id=1, source_target_pairs={{1,3},{2,0},{3,5},{4,2},{5,7},{6,4},{7,9},{8,6},{9,11},{10,8},{11,... | collective-permute-start | bytes 7077896 | tf_op jit(solution)/shard_map/ppermute | solution.py:368
  16.0 1.8 %collective-permute-done.final_ref.merge_ref = f32[6,8,32768]{2,1,0:T(8,128)S(1)} collective-permute-done((f32[6,8,32768]{2,1,0:T(8,128)S(1)}, f32[6,8,32768]{2,1,0:T(8,128)S(1)}, u32[]{:S(2)}, u32[]{:S(2)}) %collective-permute-start) | collective-permute-done | bytes 6291488 | tf_op jit(solution)/shard_map/ppermute | solution.py:368
  17.8 0.0 copy-done.1
  17.8 5.7 %relay.1 = (f32[3,8,8192]{2,1,0:T(8,128)S(1)}, f32[3,8,16384]{2,1,0:T(8,128)S(1)}, f32[3,8,8192]{2,1,0:T(8,128)S(1)}) custom-call(s32[1]{0:T(128)} %bitcast.here_ref, s32[16]{0:T(128)S(1)} %copy-done.1, f32[16,32768]{1,0:T(8,128)} %phi_ref.3, f32[16,32768]{1,0:T(8,128)} %conc_ref.3, f32[16,32768]{1,0:T(8,128)} %mob_ref.3, ...), custom_call_target="tpu_custom_call" | custom-call | flops 1000000 | bytes 12582912 | tf_op jit(solution)/shard_map/relay/pallas_call | solution.py:396
  23.5 3.8 %collective-permute-start.2 = (f32[3,8,8192]{2,1,0:T(8,128)S(1)}, f32[3,8,8192]{2,1,0:T(8,128)S(1)}, u32[]{:S(2)}, u32[]{:S(2)}) collective-permute-start(f32[3,8,8192]{2,1,0:T(8,128)S(1)} %get-tuple-element.27), channel_id=1, source_target_pairs={{0,2},{2,4},{3,1},{4,6},{5,3},{6,8},{7,5},{8,10},{9,7},{10,12},{11... | collective-permute-start | bytes 2359304 | tf_op jit(solution)/shard_map/ppermute | solution.py:368
  27.3 22.9 %collective-permute-done.2.back_ref = f32[3,8,8192]{2,1,0:T(8,128)S(1)} collective-permute-done((f32[3,8,8192]{2,1,0:T(8,128)S(1)}, f32[3,8,8192]{2,1,0:T(8,128)S(1)}, u32[]{:S(2)}, u32[]{:S(2)}) %collective-permute-start.2) | collective-permute-done | bytes 786464 | tf_op jit(solution)/shard_map/ppermute | solution.py:368
  50.2 1.9 %collective-permute-start.4 = (f32[3,8,16384]{2,1,0:T(8,128)S(1)}, f32[3,8,16384]{2,1,0:T(8,128)S(1)}, u32[]{:S(2)}, u32[]{:S(2)}) collective-permute-start(f32[3,8,16384]{2,1,0:T(8,128)S(1)} %get-tuple-element.32), channel_id=1, source_target_pairs={{0,2},{2,4},{3,1},{4,6},{5,3},{6,8},{7,5},{8,10},{9,7},{10,12},{11... | collective-permute-start | bytes 4718600 | tf_op jit(solution)/shard_map/ppermute | solution.py:368
  52.2 5.7 %stay.1 = (f32[3,8,8192]{2,1,0:T(8,128)S(1)}, f32[3,8,16384]{2,1,0:T(8,128)S(1)}, f32[3,8,8192]{2,1,0:T(8,128)S(1)}) custom-call(s32[1]{0:T(128)} %bitcast.here_ref, s32[16]{0:T(128)S(1)} %copy-done.1, f32[16,32768]{1,0:T(8,128)} %phi_ref.3, f32[16,32768]{1,0:T(8,128)} %conc_ref.3, f32[16,32768]{1,0:T(8,128)} %mob_ref.3, ...), custom_call_target="tpu_custom_call" | custom-call | flops 1000000 | bytes 12582912 | tf_op jit(solution)/shard_map/stay/pallas_call | solution.py:409
  57.8 0.0 copy-start
  57.9 0.0 collective-permute-done.1.far_ref
  57.9 0.2 faces.1
  58.0 7.1 %collective-permute-start.5 = (f32[3,8,3072]{2,1,0:T(8,128)S(1)}, f32[3,8,3072]{2,1,0:T(8,128)S(1)}, u32[]{:S(2)}, u32[]{:S(2)}) collective-permute-start(f32[3,8,3072]{2,1,0:T(8,128)S(1)} %get-tuple-element.33), channel_id=1, source_target_pairs={{0,1},{1,2},{2,3},{3,4},{4,5},{5,6},{6,7},{7,8},{8,9},{9,10},{10,1... | collective-permute-start | bytes 884744 | tf_op jit(solution)/shard_map/ppermute | solution.py:368
  65.2 2.6 %collective-permute-start.6 = (f32[3,8,3072]{2,1,0:T(8,128)S(1)}, f32[3,8,3072]{2,1,0:T(8,128)S(1)}, u32[]{:S(2)}, u32[]{:S(2)}) collective-permute-start(f32[3,8,3072]{2,1,0:T(8,128)S(1)} %get-tuple-element.28), channel_id=1, source_target_pairs={{1,0},{2,1},{3,2},{4,3},{5,4},{6,5},{7,6},{8,7},{9,8},{10,9},{11,1... | collective-permute-start | bytes 884744 | tf_op jit(solution)/shard_map/ppermute | solution.py:368
  67.8 3.9 %collective-permute-start.3 = (f32[3,8,8192]{2,1,0:T(8,128)S(1)}, f32[3,8,8192]{2,1,0:T(8,128)S(1)}, u32[]{:S(2)}, u32[]{:S(2)}) collective-permute-start(f32[3,8,8192]{2,1,0:T(8,128)S(1)} %get-tuple-element.29), channel_id=1, source_target_pairs={{1,3},{2,0},{3,5},{4,2},{5,7},{6,4},{7,9},{8,6},{9,11},{10,8},{11,... | collective-permute-start | bytes 2359304 | tf_op jit(solution)/shard_map/ppermute | solution.py:368
  71.8 1.8 %collective-permute-done.5.below_ref = f32[3,8,3072]{2,1,0:T(8,128)S(1)} collective-permute-done((f32[3,8,3072]{2,1,0:T(8,128)S(1)}, f32[3,8,3072]{2,1,0:T(8,128)S(1)}, u32[]{:S(2)}, u32[]{:S(2)}) %collective-permute-start.5) | collective-permute-done | bytes 294944 | tf_op jit(solution)/shard_map/ppermute | solution.py:368
  73.5 1.8 %collective-permute-done.6.above_ref = f32[3,8,3072]{2,1,0:T(8,128)S(1)} collective-permute-done((f32[3,8,3072]{2,1,0:T(8,128)S(1)}, f32[3,8,3072]{2,1,0:T(8,128)S(1)}, u32[]{:S(2)}, u32[]{:S(2)}) %collective-permute-start.6) | collective-permute-done | bytes 294944 | tf_op jit(solution)/shard_map/ppermute | solution.py:368
  75.3 8.2 %collective-permute-done.4.back_ref = f32[3,8,16384]{2,1,0:T(8,128)S(1)} collective-permute-done((f32[3,8,16384]{2,1,0:T(8,128)S(1)}, f32[3,8,16384]{2,1,0:T(8,128)S(1)}, u32[]{:S(2)}, u32[]{:S(2)}) %collective-permute-start.4) | collective-permute-done | bytes 1572896 | tf_op jit(solution)/shard_map/ppermute | solution.py:368
  83.5 1.9 %collective-permute-start.7 = (f32[3,8,8192]{2,1,0:T(8,128)S(1)}, f32[3,8,8192]{2,1,0:T(8,128)S(1)}, u32[]{:S(2)}, u32[]{:S(2)}) collective-permute-start(f32[3,8,8192]{2,1,0:T(8,128)S(1)} %get-tuple-element.34), channel_id=1, source_target_pairs={{0,2},{2,4},{3,1},{4,6},{5,3},{6,8},{7,5},{8,10},{9,7},{10,12},{11... | collective-permute-start | bytes 2359304 | tf_op jit(solution)/shard_map/ppermute | solution.py:368
  85.4 0.0 copy-done
  85.4 10.1 %early_steps.1 = (f32[8,32768]{1,0:T(8,128)}, f32[8,32768]{1,0:T(8,128)}, f32[3,6,8,1024]{3,2,1,0:T(8,128)S(1)}, f32[2,4,8,1024]{3,2,1,0:T(8,128)S(1)}, f32[2,4,8,1024]{3,2,1,0:T(8,128)S(1)}) custom-call(s32[1]{0:T(128)} %bitcast.here_ref, f32[3,8,8192]{2,1,0:T(8,128)S(1)} %get-tuple-element.35.edge_ref, f32[3,8,16384]{2,1,0:T(8,128)S(1)} %get-tuple-element.36.stay_ref, ...), custom_call_target="tpu_custom_call" | custom-call | flops 1000000 | bytes 20971520 | tf_op jit(solution)/shard_map/early_steps/pallas_call | solution.py:441
  95.5 0.0 collective-permute-done.3.far_ref
  95.5 6.1 %collective-permute-done.7.back_ref = f32[3,8,8192]{2,1,0:T(8,128)S(1)} collective-permute-done((f32[3,8,8192]{2,1,0:T(8,128)S(1)}, f32[3,8,8192]{2,1,0:T(8,128)S(1)}, u32[]{:S(2)}, u32[]{:S(2)}) %collective-permute-start.7) | collective-permute-done | bytes 786464 | tf_op jit(solution)/shard_map/ppermute | solution.py:368
  101.5 5.6 %late_steps.1 = (f32[8,32768]{1,0:T(8,128)}, f32[8,32768]{1,0:T(8,128)}) custom-call(s32[1]{0:T(128)} %bitcast.here_ref, f32[3,8,8192]{2,1,0:T(8,128)S(1)} %get-tuple-element.23.stay_ref, f32[3,8,8192]{2,1,0:T(8,128)S(1)} %collective-permute-done.3.far_ref, ...), custom_call_target="tpu_custom_call", output_to_operand_aliasing={{0}: (8, {}), {1}: (9, {})} | custom-call | flops 1000000 | bytes 8388608 | tf_op jit(solution)/shard_map/late_steps/pallas_call | solution.py:454
Async XLA Ops:
  0.6 17.2 %copy-start.1 = (s32[16]{0:T(128)S(1)}, s32[16]{0:T(128)}, u32[]{:S(2)}) copy-start(s32[16]{0:T(128)} %slot_ref.3) | copy-start | bytes 196
  7.6 10.2 %collective-permute-start = (f32[6,8,32768]{2,1,0:T(8,128)S(1)}, f32[6,8,32768]{2,1,0:T(8,128)S(1)}, u32[]{:S(2)}, u32[]{:S(2)}) collective-permute-start(f32[6,8,32768]{2,1,0:T(8,128)S(1)} %get-tuple-element.22), channel_id=1, source_target_pairs={{0,1},{1,0},{2,3},{3,2},{4,5},{5,4},{6,7},{7,6},{8,9},{9,8},{10,11... | collective-permute-start | bytes 18874376 | tf_op jit(solution)/shard_map/ppermute | solution.py:368
  7.7 50.2 %collective-permute-start.1 = (f32[3,8,24576]{2,1,0:T(8,128)S(1)}, f32[3,8,24576]{2,1,0:T(8,128)S(1)}, u32[]{:S(2)}, u32[]{:S(2)}) collective-permute-start(f32[3,8,24576]{2,1,0:T(8,128)S(1)} %get-tuple-element.26), channel_id=1, source_target_pairs={{1,3},{2,0},{3,5},{4,2},{5,7},{6,4},{7,9},{8,6},{9,11},{10,8},{11,... | collective-permute-start | bytes 7077896 | tf_op jit(solution)/shard_map/ppermute | solution.py:368
  23.5 26.8 %collective-permute-start.2 = (f32[3,8,8192]{2,1,0:T(8,128)S(1)}, f32[3,8,8192]{2,1,0:T(8,128)S(1)}, u32[]{:S(2)}, u32[]{:S(2)}) collective-permute-start(f32[3,8,8192]{2,1,0:T(8,128)S(1)} %get-tuple-element.27), channel_id=1, source_target_pairs={{0,2},{2,4},{3,1},{4,6},{5,3},{6,8},{7,5},{8,10},{9,7},{10,12},{11... | collective-permute-start | bytes 2359304 | tf_op jit(solution)/shard_map/ppermute | solution.py:368
  50.2 33.2 %collective-permute-start.4 = (f32[3,8,16384]{2,1,0:T(8,128)S(1)}, f32[3,8,16384]{2,1,0:T(8,128)S(1)}, u32[]{:S(2)}, u32[]{:S(2)}) collective-permute-start(f32[3,8,16384]{2,1,0:T(8,128)S(1)} %get-tuple-element.32), channel_id=1, source_target_pairs={{0,2},{2,4},{3,1},{4,6},{5,3},{6,8},{7,5},{8,10},{9,7},{10,12},{11... | collective-permute-start | bytes 4718600 | tf_op jit(solution)/shard_map/ppermute | solution.py:368
  57.8 27.5 %copy-start = (s32[8,6]{1,0:T(8,128)S(1)}, s32[8,6]{1,0:T(8,128)}, u32[]{:S(2)}) copy-start(s32[8,6]{1,0:T(8,128)} %nbr_ref.3) | copy-start | bytes 580
  58.0 15.5 %collective-permute-start.5 = (f32[3,8,3072]{2,1,0:T(8,128)S(1)}, f32[3,8,3072]{2,1,0:T(8,128)S(1)}, u32[]{:S(2)}, u32[]{:S(2)}) collective-permute-start(f32[3,8,3072]{2,1,0:T(8,128)S(1)} %get-tuple-element.33), channel_id=1, source_target_pairs={{0,1},{1,2},{2,3},{3,4},{4,5},{5,6},{6,7},{7,8},{8,9},{9,10},{10,1... | collective-permute-start | bytes 884744 | tf_op jit(solution)/shard_map/ppermute | solution.py:368
  65.2 10.1 %collective-permute-start.6 = (f32[3,8,3072]{2,1,0:T(8,128)S(1)}, f32[3,8,3072]{2,1,0:T(8,128)S(1)}, u32[]{:S(2)}, u32[]{:S(2)}) collective-permute-start(f32[3,8,3072]{2,1,0:T(8,128)S(1)} %get-tuple-element.28), channel_id=1, source_target_pairs={{1,0},{2,1},{3,2},{4,3},{5,4},{6,5},{7,6},{8,7},{9,8},{10,9},{11,1... | collective-permute-start | bytes 884744 | tf_op jit(solution)/shard_map/ppermute | solution.py:368
  67.8 27.6 %collective-permute-start.3 = (f32[3,8,8192]{2,1,0:T(8,128)S(1)}, f32[3,8,8192]{2,1,0:T(8,128)S(1)}, u32[]{:S(2)}, u32[]{:S(2)}) collective-permute-start(f32[3,8,8192]{2,1,0:T(8,128)S(1)} %get-tuple-element.29), channel_id=1, source_target_pairs={{1,3},{2,0},{3,5},{4,2},{5,7},{6,4},{7,9},{8,6},{9,11},{10,8},{11,... | collective-permute-start | bytes 2359304 | tf_op jit(solution)/shard_map/ppermute | solution.py:368
  83.5 18.1 %collective-permute-start.7 = (f32[3,8,8192]{2,1,0:T(8,128)S(1)}, f32[3,8,8192]{2,1,0:T(8,128)S(1)}, u32[]{:S(2)}, u32[]{:S(2)}) collective-permute-start(f32[3,8,8192]{2,1,0:T(8,128)S(1)} %get-tuple-element.34), channel_id=1, source_target_pairs={{0,2},{2,4},{3,1},{4,6},{5,3},{6,8},{7,5},{8,10},{9,7},{10,12},{11... | collective-permute-start | bytes 2359304 | tf_op jit(solution)/shard_map/ppermute | solution.py:368

commit v2 on v1

--- a/solution.py
+++ b/solution.py
@@ -55,87 +55,97 @@
     return jnp.where(jnp.bitwise_and(here, 1) == 0, -1, 1)
 
 
-def vregs_of(planes):
-    return [pl.ds(v * LANES, LANES) for v in range(planes * VREGS)]
-
-
 def aligned(ref, lanes, amount):
     return pltpu.roll(ref[0:CAP, lanes], amount, 0), pltpu.roll(ref[CAP:OLD, lanes], amount, 0)
 
 
-def load_slots(slot_hbm, slot_ref, sem):
-    copy = pltpu.make_async_copy(slot_hbm, slot_ref, sem)
-    copy.start()
-    copy.wait()
-
-
 def chunk_at(i):
     return jnp.where(i == 0, 0, jnp.where(i == 1, CHUNKS - 1, i - 1))
 
 
-def into_parts(i, fill, *refs):
-    edge_ref, mid_ref, late_ref = refs
-    pl.when(i < 2)(lambda: fill(edge_ref))
-    pl.when((i >= 2) & (i < 2 + MID_CHUNKS))(lambda: fill(mid_ref))
-    pl.when(i >= 2 + MID_CHUNKS)(lambda: fill(late_ref))
-
-
-def pack_kernel(here_ref, slot_hbm, phi_hbm, conc_hbm, mob_hbm, pair_hbm, far_hbm, late_hbm, slot_ref, sem):
-    load_slots(slot_hbm, slot_ref, sem)
+def lanes_at(start, v):
+    return pl.ds(pl.multiple_of(start + v * LANES, LANES), LANES)
+
+
+def pack_kernel(
+    here_ref, slot_hbm, phi_hbm, conc_hbm, mob_hbm,
+    phi_ref, conc_ref, mob_ref, merge_ref, final_ref, far_ref, late_ref,
+    slot_ref, slot_sem, sems,
+):
+    olds = tuple(zip((phi_hbm, conc_hbm, mob_hbm), (phi_ref, conc_ref, mob_ref)))
+
+    def copies(i):
+        lanes = pl.ds(pl.multiple_of(chunk_at(i) * CHUNK, CHUNK), CHUNK)
+        return [pltpu.make_async_copy(hbm.at[:, lanes], ref.at[:, lanes], sems.at[i, f]) for f, (hbm, ref) in enumerate(olds)]
+
+    slot_copy = pltpu.make_async_copy(slot_hbm, slot_ref, slot_sem)
+    slot_copy.start()
+
+    @pl.loop(0, CHUNKS)
+    def _(i):
+        for copy in copies(i):
+            copy.start()
+
+    slot_copy.wait()
     here = here_ref[0]
     side = side_of(here)
     amount, masks = windows(slot_ref, here)
     far, merge, final = masks(2 * side), masks(side), masks(-side)
 
-    def body(phi_ref, conc_ref, mob_ref, pair_ref, far_ref, late_ref):
-        def fill(out_ref):
-            for f, ref in enumerate((phi_ref, conc_ref, mob_ref)):
-                for lanes in vregs_of(CHUNK_PLANES):
-                    rows = aligned(ref, lanes, amount)
-                    pair_ref[f, :, lanes] = picked(merge, *rows)
-                    pair_ref[FIELDS + f, :, lanes] = picked(final, *rows)
-                    out_ref[f, :, lanes] = picked(far, *rows)
-
-        i = pl.program_id(0)
-        pl.when(i < 2 + MID_CHUNKS)(lambda: fill(far_ref))
-        pl.when(i >= 2 + MID_CHUNKS)(lambda: fill(late_ref))
-
-    pltpu.emit_pipeline(
-        body,
-        grid=(CHUNKS,),
-        in_specs=[pl.BlockSpec((OLD, CHUNK), lambda i: (0, chunk_at(i)))] * 3,
-        out_specs=[
-            pl.BlockSpec((2 * FIELDS, CAP, CHUNK), lambda i: (0, 0, chunk_at(i))),
-            pl.BlockSpec((FIELDS, CAP, CHUNK), lambda i: (0, 0, jnp.minimum(i, 1 + MID_CHUNKS))),
-            LATE_SPEC,
-        ],
-    )(phi_hbm, conc_hbm, mob_hbm, pair_hbm, far_hbm, late_hbm)
-
-
-def relay_kernel(here_ref, slot_ref, phi_ref, conc_ref, mob_ref, merge_ref, *out_refs):
+    def fill(i, out_ref, out_start):
+        start = chunk_at(i) * CHUNK
+        for f, (_, ref) in enumerate(olds):
+            for v in range(CHUNK // LANES):
+                lanes = lanes_at(start, v)
+                rows = aligned(ref, lanes, amount)
+                merge_ref[f, :, lanes] = picked(merge, *rows)
+                final_ref[f, :, lanes] = picked(final, *rows)
+                out_ref[f, :, lanes_at(out_start, v)] = picked(far, *rows)
+
+    first_steps = 2 + MID_CHUNKS
+
+    @pl.loop(0, first_steps)
+    def _(i):
+        for copy in copies(i):
+            copy.wait()
+        fill(i, far_ref, i * CHUNK)
+
+    @pl.loop(first_steps, CHUNKS)
+    def _(i):
+        for copy in copies(i):
+            copy.wait()
+        fill(i, late_ref, (i - first_steps) * CHUNK)
+
+
+def add_rows(masks, amount, old_refs, add_ref, part_refs):
+    edge_ref, mid_ref, late_ref = part_refs
+    high = CHUNK_PLANES + MID + LATE
+    for out_ref, out_plane, plane, count in (
+        (edge_ref, 0, 0, CHUNK_PLANES),
+        (edge_ref, CHUNK_PLANES, high, CHUNK_PLANES),
+        (mid_ref, 0, CHUNK_PLANES, MID),
+        (late_ref, 0, CHUNK_PLANES + MID, LATE),
+    ):
+
+        @pl.loop(0, count // 2)
+        def _(i):
+            for f, ref in enumerate(old_refs):
+                for v in range(2 * VREGS):
+                    lanes = lanes_at((plane + 2 * i) * FACE, v)
+                    value = picked(masks, *aligned(ref, lanes, amount)) + add_ref[f, :, lanes]
+                    out_ref[f, :, lanes_at((out_plane + 2 * i) * FACE, v)] = value
+
+
+def relay_kernel(here_ref, slot_ref, phi_ref, conc_ref, mob_ref, merge_ref, *part_refs):
     here = here_ref[0]
     amount, masks = windows(slot_ref, here)
-    back = masks(-2 * side_of(here))
-
-    def fill(out_ref):
-        for f, ref in enumerate((phi_ref, conc_ref, mob_ref)):
-            for lanes in vregs_of(CHUNK_PLANES):
-                out_ref[f, :, lanes] = picked(back, *aligned(ref, lanes, amount)) + merge_ref[f, :, lanes]
-
-    into_parts(pl.program_id(0), fill, *out_refs)
-
-
-def stay_kernel(here_ref, slot_ref, phi_ref, conc_ref, mob_ref, final_ref, *out_refs):
+    add_rows(masks(-2 * side_of(here)), amount, (phi_ref, conc_ref, mob_ref), merge_ref, part_refs)
+
+
+def stay_kernel(here_ref, slot_ref, phi_ref, conc_ref, mob_ref, final_ref, *part_refs):
     here = here_ref[0]
     amount, masks = windows(slot_ref, here)
-    own = masks(0)
-
-    def fill(out_ref):
-        for f, ref in enumerate((phi_ref, conc_ref, mob_ref)):
-            for lanes in vregs_of(CHUNK_PLANES):
-                out_ref[f, :, lanes] = picked(own, *aligned(ref, lanes, amount)) + final_ref[f, :, lanes]
-
-    into_parts(pl.program_id(0), fill, *out_refs)
+    add_rows(masks(0), amount, (phi_ref, conc_ref, mob_ref), final_ref, part_refs)
 
 
 def face_kernel(stay_ref, far_ref, back_ref, edge_ref, low_ref, high_ref):
@@ -347,14 +357,6 @@
     return pl.CostEstimate(flops=flops, bytes_accessed=moved, transcendentals=0)
 
 
-OLD_SPEC = pl.BlockSpec((OLD, CHUNK), lambda i: (0, chunk_at(i)))
-EDGE_SPEC = pl.BlockSpec((FIELDS, CAP, CHUNK), lambda i: (0, 0, jnp.minimum(i, 1)))
-MID_SPEC = pl.BlockSpec((FIELDS, CAP, CHUNK), lambda i: (0, 0, jnp.clip(i - 2, 0, MID_CHUNKS - 1)))
-LATE_SPEC = pl.BlockSpec((FIELDS, CAP, CHUNK), lambda i: (0, 0, jnp.clip(i - 2 - MID_CHUNKS, 0, LATE_CHUNKS - 1)))
-MERGE_SPEC = pl.BlockSpec((FIELDS, CAP, CHUNK), lambda i: (0, 0, chunk_at(i)))
-FINAL_SPEC = pl.BlockSpec((FIELDS, CAP, CHUNK), lambda i: (1, 0, chunk_at(i)))
-EDGES = pl.BlockSpec((FIELDS, CAP, 2 * CHUNK), lambda i: (0, 0, 0))
-FACES = pl.BlockSpec((FIELDS, CAP, HALO * FACE), lambda i: (0, 0, 0))
 MB = 2**20
 
 
@@ -378,50 +380,52 @@
         return lax.optimization_barrier((block, *others))[0]
 
     slots_hbm = pltpu.with_memory_space_constraint(new_global_slot, pltpu.HBM)
-    slot_scratch = [pltpu.SMEM((OLD,), jnp.int32), pltpu.SemaphoreType.DMA]
-    pair, far_first, far_late = pl.pallas_call(
+    old_shape = jax.ShapeDtypeStruct((OLD, CELLS), jnp.float32)
+    *olds, merge, final, far_first, far_late = pl.pallas_call(
         pack_kernel,
         in_specs=[SMEM, HBM, HBM, HBM, HBM],
-        out_specs=[ANY] * 3,
-        out_shape=[shaped(EDGE, 2 * FIELDS), shaped(2 * CHUNK_PLANES + MID), shaped(LATE)],
-        scratch_shapes=slot_scratch,
-        compiler_params=PARAMS,
-        cost_estimate=cost(15 * MB),
+        out_specs=[VMEM] * 7,
+        out_shape=[old_shape] * 3 + [shaped(EDGE)] * 2 + [shaped(2 * CHUNK_PLANES + MID), shaped(LATE)],
+        scratch_shapes=[pltpu.SMEM((OLD,), jnp.int32), pltpu.SemaphoreType.DMA, pltpu.SemaphoreType.DMA((CHUNKS, FIELDS))],
+        compiler_params=PARAMS,
+        cost_estimate=cost(6 * MB),
         name="pack",
     )(here, slots_hbm, *olds)
     far_first_got = sent(far_first, far_route)
-    pair_got = sent(pair, partner)
+    merge_got = sent(merge, partner)
+    final_got = sent(final, partner)
 
     three_parts = [shaped(2 * CHUNK_PLANES), shaped(MID), shaped(LATE)]
     back_edge, back_mid, back_late = pl.pallas_call(
         relay_kernel,
-        grid=(CHUNKS,),
-        in_specs=[SMEM, SMEM] + [OLD_SPEC] * 3 + [MERGE_SPEC],
-        out_specs=[EDGE_SPEC, MID_SPEC, LATE_SPEC],
+        in_specs=[SMEM, SMEM] + [VMEM] * 4,
+        out_specs=[VMEM] * 3,
         out_shape=three_parts,
         compiler_params=PARAMS,
-        cost_estimate=cost(12 * MB),
+        cost_estimate=cost(6 * MB),
         name="relay",
-    )(here, new_global_slot, *olds, pair_got)
+    )(here, new_global_slot, *olds, merge_got)
     back_edge_got = sent(back_edge, back_route)
-    back_mid_got = sent(after(back_mid, back_edge_got), back_route)
 
     stay_edge, stay_mid, stay_late = pl.pallas_call(
         stay_kernel,
-        grid=(CHUNKS,),
-        in_specs=[SMEM, SMEM] + [OLD_SPEC] * 3 + [FINAL_SPEC],
-        out_specs=[EDGE_SPEC, MID_SPEC, LATE_SPEC],
+        in_specs=[SMEM, SMEM] + [VMEM] * 4,
+        out_specs=[VMEM] * 3,
         out_shape=three_parts,
         compiler_params=PARAMS,
-        cost_estimate=cost(12 * MB),
+        cost_estimate=cost(6 * MB),
         name="stay",
-    )(here, new_global_slot, *olds, pair_got)
-
+    )(here, new_global_slot, *olds, final_got)
+    back_mid_got = sent(after(back_mid, back_edge_got, stay_edge), back_route)
+    far_late_got = sent(after(far_late, far_first_got), far_route)
+
+    edges = pl.BlockSpec((FIELDS, CAP, 2 * CHUNK), lambda i: (0, 0, 0))
+    faces = pl.BlockSpec((FIELDS, CAP, HALO * FACE), lambda i: (0, 0, 0))
     edge, low, high = pl.pallas_call(
         face_kernel,
         grid=(1,),
-        in_specs=[EDGES] * 3,
-        out_specs=[EDGES, FACES, FACES],
+        in_specs=[edges] * 3,
+        out_specs=[edges, faces, faces],
         out_shape=[shaped(2 * CHUNK_PLANES), shaped(HALO), shaped(HALO)],
         compiler_params=PARAMS,
         cost_estimate=cost(3 * MB),
@@ -429,7 +433,6 @@
     )(stay_edge, far_first_got, back_edge_got)
     below = sent(high, [(p, p + 1) for p in devices])
     above = sent(low, [(p, p - 1) for p in devices])
-    far_late_got = sent(after(far_late, low), far_route)
     back_late_got = sent(after(back_late, back_mid_got, below, above), back_route)
 
     state = pltpu.VMEM((EXT, CAP, FACE), jnp.float32)

time: 108 us -> 101 us (0.935)
  Pallas kernels: 34.1 us -> 23 us
  waiting for transfers between devices: 42.5 us -> 48.4 us
    pallas_call x3, Pallas kernels: 11.5 us -> 4.15 us  [the longest x1 1.99 us: on_device(): pl.pallas_call(relay_kernel, in_specs=[SMEM, SMEM] + [VMEM] * 4, out_spec...]
    ppermute x8 -> x9, waiting for transfers between devices: 42.5 us -> 48.4 us  [sent(): lax.ppermute(block, 'blk', [(p, q) for p, q in route if 0 <= q < count])]
    pallas_call x1, Pallas kernels: 6.92 us -> 3.19 us  [on_device(): pl.pallas_call(pack_kernel, in_specs=[SMEM, HBM, HBM, HBM, HBM], out_spec...]
    ppermute x8 -> x9, starting transfers between devices: 29.8 us -> 28.8 us  [sent(): lax.ppermute(block, 'blk', [(p, q) for p, q in route if 0 <= q < count])]
  transfers between devices with their start and end apart: 8 -> 9, of which waited for: 6 -> 6; matrix products, arithmetic and copies ran while one was open for 0% -> 0% of each run, Pallas kernels for 20% -> 14%
where the time goes in v2:
time: 101 us
  waiting for transfers between devices  48.4 us (48%)
  starting transfers between devices  28.8 us (29%)
  Pallas kernels  23 us (23%)
    ppermute x9, waiting for transfers between devices, sent(): lax.ppermute(block, 'blk', [(p, q) for p, q in route if 0 <= q < count])  48.4 us
    ppermute x9, starting transfers between devices, sent(): lax.ppermute(block, 'blk', [(p, q) for p, q in route if 0 <= q < count])  28.8 us
    pallas_call x1, Pallas kernels, on_device(): pl.pallas_call(early_kernel, in_specs=[SMEM] + [VMEM] * 7, out_specs=[VME...  10.1 us
    pallas_call x1, Pallas kernels, on_device(): pl.pallas_call(late_kernel, in_specs=[SMEM] + [VMEM] * 7 + [HBM] * 2, out...  5.55 us
    pallas_call x1, Pallas kernels, on_device(): pl.pallas_call(pack_kernel, in_specs=[SMEM, HBM, HBM, HBM, HBM], out_spec...  3.19 us
  transfers between devices with their start and end apart: 9, of which 6 were waited for; matrix products, arithmetic and copies ran while one was open for 0% of the time, Pallas kernels for 14%

profile of v2, /device:TPU:24, one launch (start us, length us, event | category | flops | bytes accessed | tf_op | source)
XLA Modules:
  0.0 101.0 jit_solution(611836043712203649)
XLA Ops:
  0.6 0.0 copy-start.1
  0.6 3.2 %pack.1 = (f32[16,32768]{1,0:T(8,128)S(1)}, f32[16,32768]{1,0:T(8,128)S(1)}, f32[16,32768]{1,0:T(8,128)S(1)}, f32[3,8,32768]{2,1,0:T(8,128)S(1)}, f32[3,8,32768]...) custom-call(s32[1]{0:T(128)} %bitcast.here_ref, s32[16]{0:T(128)} %slot_ref.3, ...), custom_call_target="tpu_custom_call" | custom-call | flops 1000000 | bytes 6291456 | tf_op jit(solution)/shard_map/pack/pallas_call | solution.py:384
  3.8 0.1 collective-permute-start.3
  3.9 0.5 collective-permute-start
  4.4 8.3 %collective-permute-start.1 = (f32[3,8,24576]{2,1,0:T(8,128)S(1)}, f32[3,8,24576]{2,1,0:T(8,128)S(1)}, u32[]{:S(2)}, u32[]{:S(2)}) collective-permute-start(f32[3,8,24576]{2,1,0:T(8,128)S(1)} %get-tuple-element.32), channel_id=1, source_target_pairs={{1,3},{2,0},{3,5},{4,2},{5,7},{6,4},{7,9},{8,6},{9,11},{10,8},{11,... | collective-permute-start | bytes 7077896 | tf_op jit(solution)/shard_map/ppermute | solution.py:370
  12.7 0.0 collective-permute-done.3.merge_ref
  12.8 0.0 copy-done.1
  12.8 2.0 %relay.1 = (f32[3,8,8192]{2,1,0:T(8,128)S(1)}, f32[3,8,16384]{2,1,0:T(8,128)S(1)}, f32[3,8,8192]{2,1,0:T(8,128)S(1)}) custom-call(s32[1]{0:T(128)} %bitcast.here_ref, s32[16]{0:T(128)S(1)} %copy-done.1, f32[16,32768]{1,0:T(8,128)S(1)} %get-tuple-element.26.phi_ref, f32[16,32768]{1,0:T(8,128)S(1)} %get-tuple-element.27.conc_ref, ...), custom_call_target="tpu_custom_call" | custom-call | flops 1000000 | bytes 6291456 | tf_op jit(solution)/shard_map/relay/pallas_call | solution.py:399
  14.8 1.9 %collective-permute-start.4 = (f32[3,8,8192]{2,1,0:T(8,128)S(1)}, f32[3,8,8192]{2,1,0:T(8,128)S(1)}, u32[]{:S(2)}, u32[]{:S(2)}) collective-permute-start(f32[3,8,8192]{2,1,0:T(8,128)S(1)} %get-tuple-element.37), channel_id=1, source_target_pairs={{0,2},{2,4},{3,1},{4,6},{5,3},{6,8},{7,5},{8,10},{9,7},{10,12},{11... | collective-permute-start | bytes 2359304 | tf_op jit(solution)/shard_map/ppermute | solution.py:370
  16.7 0.0 collective-permute-done.final_ref
  16.7 2.0 %stay.1 = (f32[3,8,8192]{2,1,0:T(8,128)S(1)}, f32[3,8,16384]{2,1,0:T(8,128)S(1)}, f32[3,8,8192]{2,1,0:T(8,128)S(1)}) custom-call(s32[1]{0:T(128)} %bitcast.here_ref, s32[16]{0:T(128)S(1)} %copy-done.1, f32[16,32768]{1,0:T(8,128)S(1)} %get-tuple-element.26.phi_ref, f32[16,32768]{1,0:T(8,128)S(1)} %get-tuple-element.27.conc_ref, ...), custom_call_target="tpu_custom_call" | custom-call | flops 1000000 | bytes 6291456 | tf_op jit(solution)/shard_map/stay/pallas_call | solution.py:410
  18.7 0.0 copy-start
  18.7 22.6 %collective-permute-done.4.back_ref = f32[3,8,8192]{2,1,0:T(8,128)S(1)} collective-permute-done((f32[3,8,8192]{2,1,0:T(8,128)S(1)}, f32[3,8,8192]{2,1,0:T(8,128)S(1)}, u32[]{:S(2)}, u32[]{:S(2)}) %collective-permute-start.4) | collective-permute-done | bytes 786464 | tf_op jit(solution)/shard_map/ppermute | solution.py:370
  41.4 1.9 %collective-permute-start.5 = (f32[3,8,16384]{2,1,0:T(8,128)S(1)}, f32[3,8,16384]{2,1,0:T(8,128)S(1)}, u32[]{:S(2)}, u32[]{:S(2)}) collective-permute-start(f32[3,8,16384]{2,1,0:T(8,128)S(1)} %get-tuple-element.39), channel_id=1, source_target_pairs={{0,2},{2,4},{3,1},{4,6},{5,3},{6,8},{7,5},{8,10},{9,7},{10,12},{11... | collective-permute-start | bytes 4718600 | tf_op jit(solution)/shard_map/ppermute | solution.py:370
  43.3 5.8 %collective-permute-done.1.far_ref = f32[3,8,24576]{2,1,0:T(8,128)S(1)} collective-permute-done((f32[3,8,24576]{2,1,0:T(8,128)S(1)}, f32[3,8,24576]{2,1,0:T(8,128)S(1)}, u32[]{:S(2)}, u32[]{:S(2)}) %collective-permute-start.1) | collective-permute-done | bytes 2359328 | tf_op jit(solution)/shard_map/ppermute | solution.py:370
  49.1 0.2 faces.1
  49.3 1.9 %collective-permute-start.6 = (f32[3,8,3072]{2,1,0:T(8,128)S(1)}, f32[3,8,3072]{2,1,0:T(8,128)S(1)}, u32[]{:S(2)}, u32[]{:S(2)}) collective-permute-start(f32[3,8,3072]{2,1,0:T(8,128)S(1)} %get-tuple-element.40), channel_id=1, source_target_pairs={{0,1},{1,2},{2,3},{3,4},{4,5},{5,6},{6,7},{7,8},{8,9},{9,10},{10,1... | collective-permute-start | bytes 884744 | tf_op jit(solution)/shard_map/ppermute | solution.py:370
  51.2 7.9 %collective-permute-start.7 = (f32[3,8,3072]{2,1,0:T(8,128)S(1)}, f32[3,8,3072]{2,1,0:T(8,128)S(1)}, u32[]{:S(2)}, u32[]{:S(2)}) collective-permute-start(f32[3,8,3072]{2,1,0:T(8,128)S(1)} %get-tuple-element.41), channel_id=1, source_target_pairs={{1,0},{2,1},{3,2},{4,3},{5,4},{6,5},{7,6},{8,7},{9,8},{10,9},{11,1... | collective-permute-start | bytes 884744 | tf_op jit(solution)/shard_map/ppermute | solution.py:370
  59.1 4.4 %collective-permute-start.2 = (f32[3,8,8192]{2,1,0:T(8,128)S(1)}, f32[3,8,8192]{2,1,0:T(8,128)S(1)}, u32[]{:S(2)}, u32[]{:S(2)}) collective-permute-start(f32[3,8,8192]{2,1,0:T(8,128)S(1)} %get-tuple-element.33), channel_id=1, source_target_pairs={{1,3},{2,0},{3,5},{4,2},{5,7},{6,4},{7,9},{8,6},{9,11},{10,8},{11,... | collective-permute-start | bytes 2359304 | tf_op jit(solution)/shard_map/ppermute | solution.py:370
  63.5 1.3 %collective-permute-done.6.below_ref = f32[3,8,3072]{2,1,0:T(8,128)S(1)} collective-permute-done((f32[3,8,3072]{2,1,0:T(8,128)S(1)}, f32[3,8,3072]{2,1,0:T(8,128)S(1)}, u32[]{:S(2)}, u32[]{:S(2)}) %collective-permute-start.6) | collective-permute-done | bytes 294944 | tf_op jit(solution)/shard_map/ppermute | solution.py:370
  64.8 1.8 %collective-permute-done.7.above_ref = f32[3,8,3072]{2,1,0:T(8,128)S(1)} collective-permute-done((f32[3,8,3072]{2,1,0:T(8,128)S(1)}, f32[3,8,3072]{2,1,0:T(8,128)S(1)}, u32[]{:S(2)}, u32[]{:S(2)}) %collective-permute-start.7) | collective-permute-done | bytes 294944 | tf_op jit(solution)/shard_map/ppermute | solution.py:370
  66.5 10.8 %collective-permute-done.5.back_ref = f32[3,8,16384]{2,1,0:T(8,128)S(1)} collective-permute-done((f32[3,8,16384]{2,1,0:T(8,128)S(1)}, f32[3,8,16384]{2,1,0:T(8,128)S(1)}, u32[]{:S(2)}, u32[]{:S(2)}) %collective-permute-start.5) | collective-permute-done | bytes 1572896 | tf_op jit(solution)/shard_map/ppermute | solution.py:370
  77.3 1.9 %collective-permute-start.8 = (f32[3,8,8192]{2,1,0:T(8,128)S(1)}, f32[3,8,8192]{2,1,0:T(8,128)S(1)}, u32[]{:S(2)}, u32[]{:S(2)}) collective-permute-start(f32[3,8,8192]{2,1,0:T(8,128)S(1)} %get-tuple-element.42), channel_id=1, source_target_pairs={{0,2},{2,4},{3,1},{4,6},{5,3},{6,8},{7,5},{8,10},{9,7},{10,12},{11... | collective-permute-start | bytes 2359304 | tf_op jit(solution)/shard_map/ppermute | solution.py:370
  79.2 0.0 copy-done
  79.2 10.1 %early_steps.1 = (f32[8,32768]{1,0:T(8,128)}, f32[8,32768]{1,0:T(8,128)}, f32[3,6,8,1024]{3,2,1,0:T(8,128)S(1)}, f32[2,4,8,1024]{3,2,1,0:T(8,128)S(1)}, f32[2,4,8,1024]{3,2,1,0:T(8,128)S(1)}) custom-call(s32[1]{0:T(128)} %bitcast.here_ref, f32[3,8,8192]{2,1,0:T(8,128)S(1)} %get-tuple-element.43.edge_ref, f32[3,8,16384]{2,1,0:T(8,128)S(1)} %get-tuple-element.44.stay_ref, ...), custom_call_target="tpu_custom_call" | custom-call | flops 1000000 | bytes 20971520 | tf_op jit(solution)/shard_map/early_steps/pallas_call | solution.py:444
  89.4 0.0 collective-permute-done.2.far_ref
  89.4 6.0 %collective-permute-done.8.back_ref = f32[3,8,8192]{2,1,0:T(8,128)S(1)} collective-permute-done((f32[3,8,8192]{2,1,0:T(8,128)S(1)}, f32[3,8,8192]{2,1,0:T(8,128)S(1)}, u32[]{:S(2)}, u32[]{:S(2)}) %collective-permute-start.8) | collective-permute-done | bytes 786464 | tf_op jit(solution)/shard_map/ppermute | solution.py:370
  95.4 5.6 %late_steps.1 = (f32[8,32768]{1,0:T(8,128)}, f32[8,32768]{1,0:T(8,128)}) custom-call(s32[1]{0:T(128)} %bitcast.here_ref, f32[3,8,8192]{2,1,0:T(8,128)S(1)} %get-tuple-element.30.stay_ref, f32[3,8,8192]{2,1,0:T(8,128)S(1)} %collective-permute-done.2.far_ref, ...), custom_call_target="tpu_custom_call", output_to_operand_aliasing={{0}: (8, {}), {1}: (9, {})} | custom-call | flops 1000000 | bytes 8388608 | tf_op jit(solution)/shard_map/late_steps/pallas_call | solution.py:457
Async XLA Ops:
  0.6 12.1 %copy-start.1 = (s32[16]{0:T(128)S(1)}, s32[16]{0:T(128)}, u32[]{:S(2)}) copy-start(s32[16]{0:T(128)} %slot_ref.3) | copy-start | bytes 196
  3.8 8.9 %collective-permute-start.3 = (f32[3,8,32768]{2,1,0:T(8,128)S(1)}, f32[3,8,32768]{2,1,0:T(8,128)S(1)}, u32[]{:S(2)}, u32[]{:S(2)}) collective-permute-start(f32[3,8,32768]{2,1,0:T(8,128)S(1)} %get-tuple-element.34), channel_id=1, source_target_pairs={{0,1},{1,0},{2,3},{3,2},{4,5},{5,4},{6,7},{7,6},{8,9},{9,8},{10,11... | collective-permute-start | bytes 9437192 | tf_op jit(solution)/shard_map/ppermute | solution.py:370
  3.9 12.8 %collective-permute-start = (f32[3,8,32768]{2,1,0:T(8,128)S(1)}, f32[3,8,32768]{2,1,0:T(8,128)S(1)}, u32[]{:S(2)}, u32[]{:S(2)}) collective-permute-start(f32[3,8,32768]{2,1,0:T(8,128)S(1)} %get-tuple-element.29), channel_id=1, source_target_pairs={{0,1},{1,0},{2,3},{3,2},{4,5},{5,4},{6,7},{7,6},{8,9},{9,8},{10,11... | collective-permute-start | bytes 9437192 | tf_op jit(solution)/shard_map/ppermute | solution.py:370
  4.4 44.7 %collective-permute-start.1 = (f32[3,8,24576]{2,1,0:T(8,128)S(1)}, f32[3,8,24576]{2,1,0:T(8,128)S(1)}, u32[]{:S(2)}, u32[]{:S(2)}) collective-permute-start(f32[3,8,24576]{2,1,0:T(8,128)S(1)} %get-tuple-element.32), channel_id=1, source_target_pairs={{1,3},{2,0},{3,5},{4,2},{5,7},{6,4},{7,9},{8,6},{9,11},{10,8},{11,... | collective-permute-start | bytes 7077896 | tf_op jit(solution)/shard_map/ppermute | solution.py:370
  14.8 26.6 %collective-permute-start.4 = (f32[3,8,8192]{2,1,0:T(8,128)S(1)}, f32[3,8,8192]{2,1,0:T(8,128)S(1)}, u32[]{:S(2)}, u32[]{:S(2)}) collective-permute-start(f32[3,8,8192]{2,1,0:T(8,128)S(1)} %get-tuple-element.37), channel_id=1, source_target_pairs={{0,2},{2,4},{3,1},{4,6},{5,3},{6,8},{7,5},{8,10},{9,7},{10,12},{11... | collective-permute-start | bytes 2359304 | tf_op jit(solution)/shard_map/ppermute | solution.py:370
  18.7 60.5 %copy-start = (s32[8,6]{1,0:T(8,128)S(1)}, s32[8,6]{1,0:T(8,128)}, u32[]{:S(2)}) copy-start(s32[8,6]{1,0:T(8,128)} %nbr_ref.3) | copy-start | bytes 580
  41.4 36.0 %collective-permute-start.5 = (f32[3,8,16384]{2,1,0:T(8,128)S(1)}, f32[3,8,16384]{2,1,0:T(8,128)S(1)}, u32[]{:S(2)}, u32[]{:S(2)}) collective-permute-start(f32[3,8,16384]{2,1,0:T(8,128)S(1)} %get-tuple-element.39), channel_id=1, source_target_pairs={{0,2},{2,4},{3,1},{4,6},{5,3},{6,8},{7,5},{8,10},{9,7},{10,12},{11... | collective-permute-start | bytes 4718600 | tf_op jit(solution)/shard_map/ppermute | solution.py:370
  49.3 15.5 %collective-permute-start.6 = (f32[3,8,3072]{2,1,0:T(8,128)S(1)}, f32[3,8,3072]{2,1,0:T(8,128)S(1)}, u32[]{:S(2)}, u32[]{:S(2)}) collective-permute-start(f32[3,8,3072]{2,1,0:T(8,128)S(1)} %get-tuple-element.40), channel_id=1, source_target_pairs={{0,1},{1,2},{2,3},{3,4},{4,5},{5,6},{6,7},{7,8},{8,9},{9,10},{10,1... | collective-permute-start | bytes 884744 | tf_op jit(solution)/shard_map/ppermute | solution.py:370
  51.2 15.3 %collective-permute-start.7 = (f32[3,8,3072]{2,1,0:T(8,128)S(1)}, f32[3,8,3072]{2,1,0:T(8,128)S(1)}, u32[]{:S(2)}, u32[]{:S(2)}) collective-permute-start(f32[3,8,3072]{2,1,0:T(8,128)S(1)} %get-tuple-element.41), channel_id=1, source_target_pairs={{1,0},{2,1},{3,2},{4,3},{5,4},{6,5},{7,6},{8,7},{9,8},{10,9},{11,1... | collective-permute-start | bytes 884744 | tf_op jit(solution)/shard_map/ppermute | solution.py:370
  59.1 30.3 %collective-permute-start.2 = (f32[3,8,8192]{2,1,0:T(8,128)S(1)}, f32[3,8,8192]{2,1,0:T(8,128)S(1)}, u32[]{:S(2)}, u32[]{:S(2)}) collective-permute-start(f32[3,8,8192]{2,1,0:T(8,128)S(1)} %get-tuple-element.33), channel_id=1, source_target_pairs={{1,3},{2,0},{3,5},{4,2},{5,7},{6,4},{7,9},{8,6},{9,11},{10,8},{11,... | collective-permute-start | bytes 2359304 | tf_op jit(solution)/shard_map/ppermute | solution.py:370
  77.3 18.1 %collective-permute-start.8 = (f32[3,8,8192]{2,1,0:T(8,128)S(1)}, f32[3,8,8192]{2,1,0:T(8,128)S(1)}, u32[]{:S(2)}, u32[]{:S(2)}) collective-permute-start(f32[3,8,8192]{2,1,0:T(8,128)S(1)} %get-tuple-element.42), channel_id=1, source_target_pairs={{0,2},{2,4},{3,1},{4,6},{5,3},{6,8},{7,5},{8,10},{9,7},{10,12},{11... | collective-permute-start | bytes 2359304 | tf_op jit(solution)/shard_map/ppermute | solution.py:370

commit v3 on v2

--- a/solution.py
+++ b/solution.py
@@ -117,15 +117,19 @@
         fill(i, late_ref, (i - first_steps) * CHUNK)
 
 
-def add_rows(masks, amount, old_refs, add_ref, part_refs):
-    edge_ref, mid_ref, late_ref = part_refs
-    high = CHUNK_PLANES + MID + LATE
-    for out_ref, out_plane, plane, count in (
-        (edge_ref, 0, 0, CHUNK_PLANES),
-        (edge_ref, CHUNK_PLANES, high, CHUNK_PLANES),
-        (mid_ref, 0, CHUNK_PLANES, MID),
-        (late_ref, 0, CHUNK_PLANES + MID, LATE),
-    ):
+TOP = CHUNK_PLANES + MID + LATE
+PARTS = (2 * CHUNK_PLANES, MID, LATE)
+HALVES = (2 * CHUNK_PLANES, MID // 2, MID // 2, LATE // 2, LATE // 2)
+
+
+def add_rows(masks, amount, old_refs, add_ref, part_refs, sizes):
+    edge_ref, *rest = part_refs
+    spans = [(edge_ref, 0, 0, CHUNK_PLANES), (edge_ref, CHUNK_PLANES, TOP, CHUNK_PLANES)]
+    first = CHUNK_PLANES
+    for part_ref, size in zip(rest, sizes[1:]):
+        spans.append((part_ref, 0, first, size))
+        first += size
+    for out_ref, out_plane, plane, count in spans:
 
         @pl.loop(0, count // 2)
         def _(i):
@@ -139,13 +143,13 @@
 def relay_kernel(here_ref, slot_ref, phi_ref, conc_ref, mob_ref, merge_ref, *part_refs):
     here = here_ref[0]
     amount, masks = windows(slot_ref, here)
-    add_rows(masks(-2 * side_of(here)), amount, (phi_ref, conc_ref, mob_ref), merge_ref, part_refs)
+    add_rows(masks(-2 * side_of(here)), amount, (phi_ref, conc_ref, mob_ref), merge_ref, part_refs, HALVES)
 
 
 def stay_kernel(here_ref, slot_ref, phi_ref, conc_ref, mob_ref, final_ref, *part_refs):
     here = here_ref[0]
     amount, masks = windows(slot_ref, here)
-    add_rows(masks(0), amount, (phi_ref, conc_ref, mob_ref), final_ref, part_refs)
+    add_rows(masks(0), amount, (phi_ref, conc_ref, mob_ref), final_ref, part_refs, PARTS)
 
 
 def face_kernel(stay_ref, far_ref, back_ref, edge_ref, low_ref, high_ref):
@@ -251,14 +255,13 @@
 def place(states, planes, at, *parts):
     for f, ref in enumerate(states):
 
-        @pl.loop(0, planes)
-        def _(x):
-            for v in range(VREGS):
-                lanes = pl.ds(pl.multiple_of(x * FACE + v * LANES, LANES), LANES)
-                value = parts[0][f, :, lanes]
-                for part in parts[1:]:
-                    value = value + part[f, :, lanes]
-                ref[x + at, :, pl.ds(v * LANES, LANES)] = value
+        @pl.loop(0, planes // 2)
+        def _(i):
+            for u in range(2):
+                x = 2 * i + u
+                for v in range(VREGS):
+                    value = sum(part[f, :, lanes_at((x + first) * FACE, v)] for part, first in parts)
+                    ref[x + at, :, pl.ds(v * LANES, LANES)] = value
 
 
 MID_AT = HALO + CHUNK_PLANES
@@ -267,18 +270,21 @@
 
 
 def early_kernel(
-    here_ref, edge_ref, stay_ref, far_ref, back_ref, below_ref, above_ref, nbr_ref,
+    here_ref, edge_ref, stay_ref, far_ref, back_low_ref, back_high_ref, below_ref, above_ref, nbr_ref,
     phase_ref, solute_ref, kept0_ref, kept1_ref, kept2_ref,
     phi0, conc0, mob, phi1, conc1, phi2, conc2,
 ):
     st = Stencil(here_ref[0], nbr_ref[...])
+    back_refs = (back_low_ref, back_high_ref)
     states = (phi0, conc0, mob)
     for f, ref in enumerate(states):
         for d in range(2 * CHUNK_PLANES):
             at = HALO + d if d < CHUNK_PLANES else TOP_AT + d - CHUNK_PLANES
             for v in range(VREGS):
                 ref[at, :, pl.ds(v * LANES, LANES)] = edge_ref[f, :, pl.ds(d * FACE + v * LANES, LANES)]
-    place(states, MID, MID_AT, stay_ref, far_ref.at[:, :, pl.ds(2 * CHUNK, MID * FACE)], back_ref)
+    for n, back_ref in enumerate(back_refs):
+        done = n * MID // 2
+        place(states, MID // 2, MID_AT + done, (stay_ref, done), (far_ref, 2 * CHUNK_PLANES + done), (back_ref, 0))
     for f, ref in enumerate(states):
         for d in range(HALO):
             for v in range(VREGS):
@@ -312,11 +318,12 @@
 
 
 def late_kernel(
-    here_ref, stay_ref, far_ref, back_ref, nbr_ref, kept0_ref, kept1_ref, kept2_ref, _phase_in, _solute_in,
+    here_ref, stay_ref, far_ref, back_low_ref, back_high_ref, nbr_ref, kept0_ref, kept1_ref, kept2_ref, _phase_in, _solute_in,
     phase_hbm, solute_hbm,
     phi0, conc0, mob, phi1, conc1, phi2, conc2, phase_ref, solute_ref, sems,
 ):
     st = Stencil(here_ref[0], nbr_ref[...])
+    back_refs = (back_low_ref, back_high_ref)
     states = (phi0, conc0, mob)
     first, last = LATE_AT - BACK, TOP_AT - BACK
     for f, ref in enumerate(states):
@@ -328,7 +335,9 @@
     for f, ref in enumerate((phi2, conc2)):
         for n, x in enumerate((first - 4, first - 3, last + 2, last + 3)):
             ref[x] = kept2_ref[f, n]
-    place(states, LATE, first, stay_ref, far_ref, back_ref)
+    for n, back_ref in enumerate(back_refs):
+        done = n * LATE // 2
+        place(states, LATE // 2, first + done, (stay_ref, done), (far_ref, done), (back_ref, 0))
     st.sweep(first - 1, last + 1, 5, (phi0, conc0), mob, (phi1, conc1))
     st.sweep(first - 2, last + 2, 4, (phi1, conc1), mob, (phi2, conc2))
     st.sweep(first - 3, last + 3, 7, (phi2, conc2), mob, (phase_ref, solute_ref), first - 3)
@@ -395,12 +404,11 @@
     merge_got = sent(merge, partner)
     final_got = sent(final, partner)
 
-    three_parts = [shaped(2 * CHUNK_PLANES), shaped(MID), shaped(LATE)]
-    back_edge, back_mid, back_late = pl.pallas_call(
+    back_edge, *back_mid, back_late_low, back_late_high = pl.pallas_call(
         relay_kernel,
         in_specs=[SMEM, SMEM] + [VMEM] * 4,
-        out_specs=[VMEM] * 3,
-        out_shape=three_parts,
+        out_specs=[VMEM] * len(HALVES),
+        out_shape=[shaped(size) for size in HALVES],
         compiler_params=PARAMS,
         cost_estimate=cost(6 * MB),
         name="relay",
@@ -411,12 +419,12 @@
         stay_kernel,
         in_specs=[SMEM, SMEM] + [VMEM] * 4,
         out_specs=[VMEM] * 3,
-        out_shape=three_parts,
+        out_shape=[shaped(size) for size in PARTS],
         compiler_params=PARAMS,
         cost_estimate=cost(6 * MB),
         name="stay",
     )(here, new_global_slot, *olds, final_got)
-    back_mid_got = sent(after(back_mid, back_edge_got, stay_edge), back_route)
+    back_mid_got = [sent(after(half, back_edge_got, stay_edge), back_route) for half in back_mid]
     far_late_got = sent(after(far_late, far_first_got), far_route)
 
     edges = pl.BlockSpec((FIELDS, CAP, 2 * CHUNK), lambda i: (0, 0, 0))
@@ -433,7 +441,8 @@
     )(stay_edge, far_first_got, back_edge_got)
     below = sent(high, [(p, p + 1) for p in devices])
     above = sent(low, [(p, p - 1) for p in devices])
-    back_late_got = sent(after(back_late, back_mid_got, below, above), back_route)
+    back_late = (back_late_low, back_late_high)
+    back_late_got = [sent(after(half, *back_mid_got, below, above), back_route) for half in back_late]
 
     state = pltpu.VMEM((EXT, CAP, FACE), jnp.float32)
     whole = jax.ShapeDtypeStruct((CAP, CELLS), jnp.float32)
@@ -443,28 +452,28 @@
 
     phase, solute, kept0, kept1, kept2 = pl.pallas_call(
         early_kernel,
-        in_specs=[SMEM] + [VMEM] * 7,
+        in_specs=[SMEM] + [VMEM] * 8,
         out_specs=[VMEM] * 5,
         out_shape=[whole, whole, kept(3, 6), kept(2, 4), kept(2, 4)],
         scratch_shapes=[state] * 7,
         compiler_params=PARAMS,
         cost_estimate=cost(20 * MB),
         name="early_steps",
-    )(here, edge, stay_mid, far_first_got, back_mid_got, below, above, neighbors)
+    )(here, edge, stay_mid, far_first_got, *back_mid_got, below, above, neighbors)
 
     state = pltpu.VMEM((LATE_PLANES, CAP, FACE), jnp.float32)
     rows_out = pltpu.VMEM((CAP, OUT_PLANES * FACE), jnp.float32)
     phase, solute = pl.pallas_call(
         late_kernel,
-        in_specs=[SMEM] + [VMEM] * 7 + [HBM] * 2,
+        in_specs=[SMEM] + [VMEM] * 8 + [HBM] * 2,
         out_specs=[HBM] * 2,
         out_shape=[whole, whole],
         scratch_shapes=[state] * 7 + [rows_out] * 2 + [pltpu.SemaphoreType.DMA((2,))],
-        input_output_aliases={8: 0, 9: 1},
+        input_output_aliases={9: 0, 10: 1},
         compiler_params=PARAMS,
         cost_estimate=cost(8 * MB),
         name="late_steps",
-    )(here, stay_late, far_late_got, back_late_got, neighbors, kept0, kept1, kept2, phase, solute)
+    )(here, stay_late, far_late_got, *back_late_got, neighbors, kept0, kept1, kept2, phase, solute)
     return phase, solute
 
 

time: 101 us -> 103 us (1.020)
  starting transfers between devices: 28.8 us -> 36.8 us
  waiting for transfers between devices: 48.4 us -> 42.1 us
    ppermute x9 -> x11, starting transfers between devices: 28.8 us -> 36.8 us  [sent(): lax.ppermute(block, 'blk', [(p, q) for p, q in route if 0 <= q < count])]
    ppermute x9 -> x11, waiting for transfers between devices: 48.4 us -> 42.1 us  [sent(): lax.ppermute(block, 'blk', [(p, q) for p, q in route if 0 <= q < count])]
  transfers between devices with their start and end apart: 9 -> 11, of which waited for: 6 -> 5; matrix products, arithmetic and copies ran while one was open for 0% -> 0% of each run, Pallas kernels for 14% -> 14%
where the time goes in v3:
time: 103 us
  waiting for transfers between devices  42.1 us (41%)
  starting transfers between devices  36.8 us (36%)
  Pallas kernels  23.3 us (23%)
    ppermute x11, waiting for transfers between devices, sent(): lax.ppermute(block, 'blk', [(p, q) for p, q in route if 0 <= q < count])  42.1 us
    ppermute x11, starting transfers between devices, sent(): lax.ppermute(block, 'blk', [(p, q) for p, q in route if 0 <= q < count])  36.8 us
    pallas_call x1, Pallas kernels, on_device(): pl.pallas_call(early_kernel, in_specs=[SMEM] + [VMEM] * 8, out_specs=[VME...  10.4 us
    pallas_call x1, Pallas kernels, on_device(): pl.pallas_call(late_kernel, in_specs=[SMEM] + [VMEM] * 8 + [HBM] * 2, out...  5.55 us
    pallas_call x1, Pallas kernels, on_device(): pl.pallas_call(pack_kernel, in_specs=[SMEM, HBM, HBM, HBM, HBM], out_spec...  3.19 us
  transfers between devices with their start and end apart: 11, of which 5 were waited for; matrix products, arithmetic and copies ran while one was open for 0% of the time, Pallas kernels for 14%

profile of v3, /device:TPU:24, one launch (start us, length us, event | category | flops | bytes accessed | tf_op | source)
XLA Modules:
  0.0 103.1 jit_solution(2167143014767568995)
XLA Ops:
  0.6 0.0 copy-start.1
  0.6 3.2 %pack.1 = (f32[16,32768]{1,0:T(8,128)S(1)}, f32[16,32768]{1,0:T(8,128)S(1)}, f32[16,32768]{1,0:T(8,128)S(1)}, f32[3,8,32768]{2,1,0:T(8,128)S(1)}, f32[3,8,32768]...) custom-call(s32[1]{0:T(128)} %bitcast.here_ref, s32[16]{0:T(128)} %slot_ref.3, ...), custom_call_target="tpu_custom_call" | custom-call | flops 1000000 | bytes 6291456 | tf_op jit(solution)/shard_map/pack/pallas_call | solution.py:393
  3.8 0.1 collective-permute-start.3
  3.9 0.5 collective-permute-start
  4.4 8.3 %collective-permute-start.1 = (f32[3,8,24576]{2,1,0:T(8,128)S(1)}, f32[3,8,24576]{2,1,0:T(8,128)S(1)}, u32[]{:S(2)}, u32[]{:S(2)}) collective-permute-start(f32[3,8,24576]{2,1,0:T(8,128)S(1)} %get-tuple-element.36), channel_id=1, source_target_pairs={{1,3},{2,0},{3,5},{4,2},{5,7},{6,4},{7,9},{8,6},{9,11},{10,8},{11,... | collective-permute-start | bytes 7077896 | tf_op jit(solution)/shard_map/ppermute | solution.py:379
  12.7 0.0 collective-permute-done.3.merge_ref
  12.8 0.0 copy-done.1
  12.8 2.0 %relay.1 = (f32[3,8,8192]{2,1,0:T(8,128)S(1)}, f32[3,8,8192]{2,1,0:T(8,128)S(1)}, f32[3,8,8192]{2,1,0:T(8,128)S(1)}, f32[3,8,4096]{2,1,0:T(8,128)S(1)}, f32[3,8,4096]{2,1,0:T(8,128)S(1)}) custom-call(s32[1]{0:T(128)} %bitcast.here_ref, s32[16]{0:T(128)S(1)} %copy-done.1, f32[16,32768]{1,0:T(8,128)S(1)} %get-tuple-element.30.phi_ref, ...), custom_call_target="tpu_custom_call" | custom-call | flops 1000000 | bytes 6291456 | tf_op jit(solution)/shard_map/relay/pallas_call | solution.py:407
  14.8 1.9 %collective-permute-start.4 = (f32[3,8,8192]{2,1,0:T(8,128)S(1)}, f32[3,8,8192]{2,1,0:T(8,128)S(1)}, u32[]{:S(2)}, u32[]{:S(2)}) collective-permute-start(f32[3,8,8192]{2,1,0:T(8,128)S(1)} %get-tuple-element.41), channel_id=1, source_target_pairs={{0,2},{2,4},{3,1},{4,6},{5,3},{6,8},{7,5},{8,10},{9,7},{10,12},{11... | collective-permute-start | bytes 2359304 | tf_op jit(solution)/shard_map/ppermute | solution.py:379
  16.7 0.0 collective-permute-done.final_ref
  16.7 2.0 %stay.1 = (f32[3,8,8192]{2,1,0:T(8,128)S(1)}, f32[3,8,16384]{2,1,0:T(8,128)S(1)}, f32[3,8,8192]{2,1,0:T(8,128)S(1)}) custom-call(s32[1]{0:T(128)} %bitcast.here_ref, s32[16]{0:T(128)S(1)} %copy-done.1, f32[16,32768]{1,0:T(8,128)S(1)} %get-tuple-element.30.phi_ref, f32[16,32768]{1,0:T(8,128)S(1)} %get-tuple-element.31.conc_ref, ...), custom_call_target="tpu_custom_call" | custom-call | flops 1000000 | bytes 6291456 | tf_op jit(solution)/shard_map/stay/pallas_call | solution.py:418
  18.7 0.0 copy-start
  18.7 22.6 %collective-permute-done.4.back_ref = f32[3,8,8192]{2,1,0:T(8,128)S(1)} collective-permute-done((f32[3,8,8192]{2,1,0:T(8,128)S(1)}, f32[3,8,8192]{2,1,0:T(8,128)S(1)}, u32[]{:S(2)}, u32[]{:S(2)}) %collective-permute-start.4) | collective-permute-done | bytes 786464 | tf_op jit(solution)/shard_map/ppermute | solution.py:379
  41.4 1.9 %collective-permute-start.5 = (f32[3,8,8192]{2,1,0:T(8,128)S(1)}, f32[3,8,8192]{2,1,0:T(8,128)S(1)}, u32[]{:S(2)}, u32[]{:S(2)}) collective-permute-start(f32[3,8,8192]{2,1,0:T(8,128)S(1)} %get-tuple-element.43), channel_id=1, source_target_pairs={{0,2},{2,4},{3,1},{4,6},{5,3},{6,8},{7,5},{8,10},{9,7},{10,12},{11... | collective-permute-start | bytes 2359304 | tf_op jit(solution)/shard_map/ppermute | solution.py:379
  43.3 1.9 %collective-permute-start.6 = (f32[3,8,8192]{2,1,0:T(8,128)S(1)}, f32[3,8,8192]{2,1,0:T(8,128)S(1)}, u32[]{:S(2)}, u32[]{:S(2)}) collective-permute-start(f32[3,8,8192]{2,1,0:T(8,128)S(1)} %get-tuple-element.45), channel_id=1, source_target_pairs={{0,2},{2,4},{3,1},{4,6},{5,3},{6,8},{7,5},{8,10},{9,7},{10,12},{11... | collective-permute-start | bytes 2359304 | tf_op jit(solution)/shard_map/ppermute | solution.py:379
  45.2 3.9 %collective-permute-done.1.far_ref = f32[3,8,24576]{2,1,0:T(8,128)S(1)} collective-permute-done((f32[3,8,24576]{2,1,0:T(8,128)S(1)}, f32[3,8,24576]{2,1,0:T(8,128)S(1)}, u32[]{:S(2)}, u32[]{:S(2)}) %collective-permute-start.1) | collective-permute-done | bytes 2359328 | tf_op jit(solution)/shard_map/ppermute | solution.py:379
  49.1 8.6 %collective-permute-start.2 = (f32[3,8,8192]{2,1,0:T(8,128)S(1)}, f32[3,8,8192]{2,1,0:T(8,128)S(1)}, u32[]{:S(2)}, u32[]{:S(2)}) collective-permute-start(f32[3,8,8192]{2,1,0:T(8,128)S(1)} %get-tuple-element.37), channel_id=1, source_target_pairs={{1,3},{2,0},{3,5},{4,2},{5,7},{6,4},{7,9},{8,6},{9,11},{10,8},{11,... | collective-permute-start | bytes 2359304 | tf_op jit(solution)/shard_map/ppermute | solution.py:379
  57.7 0.2 faces.1
  57.9 1.9 %collective-permute-start.7 = (f32[3,8,3072]{2,1,0:T(8,128)S(1)}, f32[3,8,3072]{2,1,0:T(8,128)S(1)}, u32[]{:S(2)}, u32[]{:S(2)}) collective-permute-start(f32[3,8,3072]{2,1,0:T(8,128)S(1)} %get-tuple-element.46), channel_id=1, source_target_pairs={{0,1},{1,2},{2,3},{3,4},{4,5},{5,6},{6,7},{7,8},{8,9},{9,10},{10,1... | collective-permute-start | bytes 884744 | tf_op jit(solution)/shard_map/ppermute | solution.py:379
  59.8 7.9 %collective-permute-start.8 = (f32[3,8,3072]{2,1,0:T(8,128)S(1)}, f32[3,8,3072]{2,1,0:T(8,128)S(1)}, u32[]{:S(2)}, u32[]{:S(2)}) collective-permute-start(f32[3,8,3072]{2,1,0:T(8,128)S(1)} %get-tuple-element.47), channel_id=1, source_target_pairs={{1,0},{2,1},{3,2},{4,3},{5,4},{6,5},{7,6},{8,7},{9,8},{10,9},{11,1... | collective-permute-start | bytes 884744 | tf_op jit(solution)/shard_map/ppermute | solution.py:379
  67.7 11.7 %collective-permute-done.7.below_ref = f32[3,8,3072]{2,1,0:T(8,128)S(1)} collective-permute-done((f32[3,8,3072]{2,1,0:T(8,128)S(1)}, f32[3,8,3072]{2,1,0:T(8,128)S(1)}, u32[]{:S(2)}, u32[]{:S(2)}) %collective-permute-start.7) | collective-permute-done | bytes 294944 | tf_op jit(solution)/shard_map/ppermute | solution.py:379
  79.4 0.0 collective-permute-done.8.above_ref
  79.4 0.0 collective-permute-done.5.back_low_ref
  79.4 0.1 collective-permute-done.6.back_high_ref
  79.5 1.9 %collective-permute-start.9 = (f32[3,8,4096]{2,1,0:T(8,128)S(1)}, f32[3,8,4096]{2,1,0:T(8,128)S(1)}, u32[]{:S(2)}, u32[]{:S(2)}) collective-permute-start(f32[3,8,4096]{2,1,0:T(8,128)S(1)} %get-tuple-element.48), channel_id=1, source_target_pairs={{0,2},{2,4},{3,1},{4,6},{5,3},{6,8},{7,5},{8,10},{9,7},{10,12},{11... | collective-permute-start | bytes 1179656 | tf_op jit(solution)/shard_map/ppermute | solution.py:379
  81.4 1.9 %collective-permute-start.10 = (f32[3,8,4096]{2,1,0:T(8,128)S(1)}, f32[3,8,4096]{2,1,0:T(8,128)S(1)}, u32[]{:S(2)}, u32[]{:S(2)}) collective-permute-start(f32[3,8,4096]{2,1,0:T(8,128)S(1)} %get-tuple-element.50), channel_id=1, source_target_pairs={{0,2},{2,4},{3,1},{4,6},{5,3},{6,8},{7,5},{8,10},{9,7},{10,12},{11... | collective-permute-start | bytes 1179656 | tf_op jit(solution)/shard_map/ppermute | solution.py:379
  83.3 0.0 copy-done
  83.3 10.4 %early_steps.1 = (f32[8,32768]{1,0:T(8,128)}, f32[8,32768]{1,0:T(8,128)}, f32[3,6,8,1024]{3,2,1,0:T(8,128)S(1)}, f32[2,4,8,1024]{3,2,1,0:T(8,128)S(1)}, f32[2,4,8,1024]{3,2,1,0:T(8,128)S(1)}) custom-call(s32[1]{0:T(128)} %bitcast.here_ref, f32[3,8,8192]{2,1,0:T(8,128)S(1)} %get-tuple-element.51.edge_ref, f32[3,8,16384]{2,1,0:T(8,128)S(1)} %get-tuple-element.52.stay_ref, ...), custom_call_target="tpu_custom_call" | custom-call | flops 1000000 | bytes 20971520 | tf_op jit(solution)/shard_map/early_steps/pallas_call | solution.py:453
  93.8 0.0 collective-permute-done.2.far_ref
  93.8 0.0 collective-permute-done.9.back_low_ref
  93.8 3.8 %collective-permute-done.10.back_high_ref = f32[3,8,4096]{2,1,0:T(8,128)S(1)} collective-permute-done((f32[3,8,4096]{2,1,0:T(8,128)S(1)}, f32[3,8,4096]{2,1,0:T(8,128)S(1)}, u32[]{:S(2)}, u32[]{:S(2)}) %collective-permute-start.10) | collective-permute-done | bytes 393248 | tf_op jit(solution)/shard_map/ppermute | solution.py:379
  97.6 5.6 %late_steps.1 = (f32[8,32768]{1,0:T(8,128)}, f32[8,32768]{1,0:T(8,128)}) custom-call(s32[1]{0:T(128)} %bitcast.here_ref, f32[3,8,8192]{2,1,0:T(8,128)S(1)} %get-tuple-element.34.stay_ref, f32[3,8,8192]{2,1,0:T(8,128)S(1)} %collective-permute-done.2.far_ref, ...), custom_call_target="tpu_custom_call", output_to_operand_aliasing={{0}: (9, {}), {1}: (10, {})} | custom-call | flops 1000000 | bytes 8388608 | tf_op jit(solution)/shard_map/late_steps/pallas_call | solution.py:466
Async XLA Ops:
  0.6 12.1 %copy-start.1 = (s32[16]{0:T(128)S(1)}, s32[16]{0:T(128)}, u32[]{:S(2)}) copy-start(s32[16]{0:T(128)} %slot_ref.3) | copy-start | bytes 196
  3.8 8.9 %collective-permute-start.3 = (f32[3,8,32768]{2,1,0:T(8,128)S(1)}, f32[3,8,32768]{2,1,0:T(8,128)S(1)}, u32[]{:S(2)}, u32[]{:S(2)}) collective-permute-start(f32[3,8,32768]{2,1,0:T(8,128)S(1)} %get-tuple-element.38), channel_id=1, source_target_pairs={{0,1},{1,0},{2,3},{3,2},{4,5},{5,4},{6,7},{7,6},{8,9},{9,8},{10,11... | collective-permute-start | bytes 9437192 | tf_op jit(solution)/shard_map/ppermute | solution.py:379
  3.9 12.8 %collective-permute-start = (f32[3,8,32768]{2,1,0:T(8,128)S(1)}, f32[3,8,32768]{2,1,0:T(8,128)S(1)}, u32[]{:S(2)}, u32[]{:S(2)}) collective-permute-start(f32[3,8,32768]{2,1,0:T(8,128)S(1)} %get-tuple-element.33), channel_id=1, source_target_pairs={{0,1},{1,0},{2,3},{3,2},{4,5},{5,4},{6,7},{7,6},{8,9},{9,8},{10,11... | collective-permute-start | bytes 9437192 | tf_op jit(solution)/shard_map/ppermute | solution.py:379
  4.4 44.7 %collective-permute-start.1 = (f32[3,8,24576]{2,1,0:T(8,128)S(1)}, f32[3,8,24576]{2,1,0:T(8,128)S(1)}, u32[]{:S(2)}, u32[]{:S(2)}) collective-permute-start(f32[3,8,24576]{2,1,0:T(8,128)S(1)} %get-tuple-element.36), channel_id=1, source_target_pairs={{1,3},{2,0},{3,5},{4,2},{5,7},{6,4},{7,9},{8,6},{9,11},{10,8},{11,... | collective-permute-start | bytes 7077896 | tf_op jit(solution)/shard_map/ppermute | solution.py:379
  14.8 26.6 %collective-permute-start.4 = (f32[3,8,8192]{2,1,0:T(8,128)S(1)}, f32[3,8,8192]{2,1,0:T(8,128)S(1)}, u32[]{:S(2)}, u32[]{:S(2)}) collective-permute-start(f32[3,8,8192]{2,1,0:T(8,128)S(1)} %get-tuple-element.41), channel_id=1, source_target_pairs={{0,2},{2,4},{3,1},{4,6},{5,3},{6,8},{7,5},{8,10},{9,7},{10,12},{11... | collective-permute-start | bytes 2359304 | tf_op jit(solution)/shard_map/ppermute | solution.py:379
  18.7 64.6 %copy-start = (s32[8,6]{1,0:T(8,128)S(1)}, s32[8,6]{1,0:T(8,128)}, u32[]{:S(2)}) copy-start(s32[8,6]{1,0:T(8,128)} %nbr_ref.3) | copy-start | bytes 580
  41.4 38.0 %collective-permute-start.5 = (f32[3,8,8192]{2,1,0:T(8,128)S(1)}, f32[3,8,8192]{2,1,0:T(8,128)S(1)}, u32[]{:S(2)}, u32[]{:S(2)}) collective-permute-start(f32[3,8,8192]{2,1,0:T(8,128)S(1)} %get-tuple-element.43), channel_id=1, source_target_pairs={{0,2},{2,4},{3,1},{4,6},{5,3},{6,8},{7,5},{8,10},{9,7},{10,12},{11... | collective-permute-start | bytes 2359304 | tf_op jit(solution)/shard_map/ppermute | solution.py:379
  43.3 36.2 %collective-permute-start.6 = (f32[3,8,8192]{2,1,0:T(8,128)S(1)}, f32[3,8,8192]{2,1,0:T(8,128)S(1)}, u32[]{:S(2)}, u32[]{:S(2)}) collective-permute-start(f32[3,8,8192]{2,1,0:T(8,128)S(1)} %get-tuple-element.45), channel_id=1, source_target_pairs={{0,2},{2,4},{3,1},{4,6},{5,3},{6,8},{7,5},{8,10},{9,7},{10,12},{11... | collective-permute-start | bytes 2359304 | tf_op jit(solution)/shard_map/ppermute | solution.py:379
  49.1 44.7 %collective-permute-start.2 = (f32[3,8,8192]{2,1,0:T(8,128)S(1)}, f32[3,8,8192]{2,1,0:T(8,128)S(1)}, u32[]{:S(2)}, u32[]{:S(2)}) collective-permute-start(f32[3,8,8192]{2,1,0:T(8,128)S(1)} %get-tuple-element.37), channel_id=1, source_target_pairs={{1,3},{2,0},{3,5},{4,2},{5,7},{6,4},{7,9},{8,6},{9,11},{10,8},{11,... | collective-permute-start | bytes 2359304 | tf_op jit(solution)/shard_map/ppermute | solution.py:379
  57.9 21.5 %collective-permute-start.7 = (f32[3,8,3072]{2,1,0:T(8,128)S(1)}, f32[3,8,3072]{2,1,0:T(8,128)S(1)}, u32[]{:S(2)}, u32[]{:S(2)}) collective-permute-start(f32[3,8,3072]{2,1,0:T(8,128)S(1)} %get-tuple-element.46), channel_id=1, source_target_pairs={{0,1},{1,2},{2,3},{3,4},{4,5},{5,6},{6,7},{7,8},{8,9},{9,10},{10,1... | collective-permute-start | bytes 884744 | tf_op jit(solution)/shard_map/ppermute | solution.py:379
  59.8 19.6 %collective-permute-start.8 = (f32[3,8,3072]{2,1,0:T(8,128)S(1)}, f32[3,8,3072]{2,1,0:T(8,128)S(1)}, u32[]{:S(2)}, u32[]{:S(2)}) collective-permute-start(f32[3,8,3072]{2,1,0:T(8,128)S(1)} %get-tuple-element.47), channel_id=1, source_target_pairs={{1,0},{2,1},{3,2},{4,3},{5,4},{6,5},{7,6},{8,7},{9,8},{10,9},{11,1... | collective-permute-start | bytes 884744 | tf_op jit(solution)/shard_map/ppermute | solution.py:379
  79.5 14.3 %collective-permute-start.9 = (f32[3,8,4096]{2,1,0:T(8,128)S(1)}, f32[3,8,4096]{2,1,0:T(8,128)S(1)}, u32[]{:S(2)}, u32[]{:S(2)}) collective-permute-start(f32[3,8,4096]{2,1,0:T(8,128)S(1)} %get-tuple-element.48), channel_id=1, source_target_pairs={{0,2},{2,4},{3,1},{4,6},{5,3},{6,8},{7,5},{8,10},{9,7},{10,12},{11... | collective-permute-start | bytes 1179656 | tf_op jit(solution)/shard_map/ppermute | solution.py:379
  81.4 16.2 %collective-permute-start.10 = (f32[3,8,4096]{2,1,0:T(8,128)S(1)}, f32[3,8,4096]{2,1,0:T(8,128)S(1)}, u32[]{:S(2)}, u32[]{:S(2)}) collective-permute-start(f32[3,8,4096]{2,1,0:T(8,128)S(1)} %get-tuple-element.50), channel_id=1, source_target_pairs={{0,2},{2,4},{3,1},{4,6},{5,3},{6,8},{7,5},{8,10},{9,7},{10,12},{11... | collective-permute-start | bytes 1179656 | tf_op jit(solution)/shard_map/ppermute | solution.py:379

commit v4 on v2

--- a/solution.py
+++ b/solution.py
@@ -19,7 +19,7 @@
 CHUNKS = EDGE // CHUNK_PLANES
 LANES = 128
 EXT = EDGE + 2 * HALO
-MID = 16
+MID = 20
 LATE = EDGE - 2 * CHUNK_PLANES - MID
 MID_CHUNKS = MID // CHUNK_PLANES
 LATE_CHUNKS = LATE // CHUNK_PLANES
@@ -288,11 +288,11 @@
                 ref[d, :, lanes] = jnp.where(st.has_below_x, st.rows(below_ref[f, :, part], st.below_x), mirror_low)
                 mirror_high = ref[EDGE + HALO - 1 - d, :, lanes]
                 ref[EDGE + HALO + d, :, lanes] = jnp.where(st.has_above_x, st.rows(above_ref[f, :, part], st.above_x), mirror_high)
-    st.sweep(1, LATE_AT - 1, 4, (phi0, conc0), mob, (phi1, conc1))
+    st.sweep(1, LATE_AT - 1, 5, (phi0, conc0), mob, (phi1, conc1))
     st.sweep(TOP_AT + 1, EXT - 1, 5, (phi0, conc0), mob, (phi1, conc1))
     st.sweep(2, LATE_AT - 2, 4, (phi1, conc1), mob, (phi2, conc2))
     st.sweep(TOP_AT + 2, EXT - 2, 3, (phi1, conc1), mob, (phi2, conc2))
-    st.sweep(HALO, LATE_AT - 3, 4, (phi2, conc2), mob, (phase_ref, solute_ref), HALO)
+    st.sweep(HALO, LATE_AT - 3, 3, (phi2, conc2), mob, (phase_ref, solute_ref), HALO)
     st.sweep(TOP_AT + 3, EXT - 3, 1, (phi2, conc2), mob, (phase_ref, solute_ref), HALO)
     for f, ref in enumerate(states):
         for n, x in enumerate((*range(LATE_AT - 3, LATE_AT), *range(TOP_AT, TOP_AT + 3))):
@@ -329,9 +329,9 @@
         for n, x in enumerate((first - 4, first - 3, last + 2, last + 3)):
             ref[x] = kept2_ref[f, n]
     place(states, LATE, first, stay_ref, far_ref, back_ref)
-    st.sweep(first - 1, last + 1, 5, (phi0, conc0), mob, (phi1, conc1))
+    st.sweep(first - 1, last + 1, 6, (phi0, conc0), mob, (phi1, conc1))
     st.sweep(first - 2, last + 2, 4, (phi1, conc1), mob, (phi2, conc2))
-    st.sweep(first - 3, last + 3, 7, (phi2, conc2), mob, (phase_ref, solute_ref), first - 3)
+    st.sweep(first - 3, last + 3, 5, (phi2, conc2), mob, (phase_ref, solute_ref), first - 3)
     copies = []
     for n, (ref, hbm) in enumerate(((phase_ref, phase_hbm), (solute_ref, solute_hbm))):
         lanes = pl.ds((OUT_FIRST - HALO) * FACE, OUT_PLANES * FACE)

time: 101 us -> 102 us (level)
  the two profiles are of different devices: /device:TPU:24 before, /device:TPU:25 now
where the time goes in v4:
time: 102 us; the launch traced here: 101 us
  starting transfers between devices  42.5 us (42%)
  waiting for transfers between devices  35.2 us (35%)
  Pallas kernels  23 us (23%)
    ppermute x9, starting transfers between devices, sent(): lax.ppermute(block, 'blk', [(p, q) for p, q in route if 0 <= q < count])  42.5 us
    ppermute x9, waiting for transfers between devices, sent(): lax.ppermute(block, 'blk', [(p, q) for p, q in route if 0 <= q < count])  35.2 us
    pallas_call x1, Pallas kernels, on_device(): pl.pallas_call(early_kernel, in_specs=[SMEM] + [VMEM] * 7, out_specs=[VME...  11.8 us
    pallas_call x1, Pallas kernels, on_device(): pl.pallas_call(late_kernel, in_specs=[SMEM] + [VMEM] * 7 + [HBM] * 2, out...  3.88 us
    pallas_call x1, Pallas kernels, on_device(): pl.pallas_call(pack_kernel, in_specs=[SMEM, HBM, HBM, HBM, HBM], out_spec...  3.11 us
  transfers between devices with their start and end apart: 9, of which 6 were waited for; matrix products, arithmetic and copies ran while one was open for 0% of the time, Pallas kernels for 16%

profile of v4, /device:TPU:25, one launch (start us, length us, event | category | flops | bytes accessed | tf_op | source)
XLA Modules:
  0.0 101.4 jit_solution(10059046092374578191)
XLA Ops:
  0.6 0.0 copy-start.1
  0.6 3.1 %pack.1 = (f32[16,32768]{1,0:T(8,128)S(1)}, f32[16,32768]{1,0:T(8,128)S(1)}, f32[16,32768]{1,0:T(8,128)S(1)}, f32[3,8,32768]{2,1,0:T(8,128)S(1)}, f32[3,8,32768]...) custom-call(s32[1]{0:T(128)} %bitcast.here_ref, s32[16]{0:T(128)} %slot_ref.3, ...), custom_call_target="tpu_custom_call" | custom-call | flops 1000000 | bytes 6291456 | tf_op jit(solution)/shard_map/pack/pallas_call | solution.py:384
  3.8 0.8 collective-permute-start.3
  4.5 0.1 collective-permute-start
  4.6 3.5 %collective-permute-start.1 = (f32[3,8,28672]{2,1,0:T(8,128)S(1)}, f32[3,8,28672]{2,1,0:T(8,128)S(1)}, u32[]{:S(2)}, u32[]{:S(2)}) collective-permute-start(f32[3,8,28672]{2,1,0:T(8,128)S(1)} %get-tuple-element.32), channel_id=1, source_target_pairs={{1,3},{2,0},{3,5},{4,2},{5,7},{6,4},{7,9},{8,6},{9,11},{10,8},{11,... | collective-permute-start | bytes 8257544 | tf_op jit(solution)/shard_map/ppermute | solution.py:370
  8.2 1.7 %collective-permute-done.3.merge_ref = f32[3,8,32768]{2,1,0:T(8,128)S(1)} collective-permute-done((f32[3,8,32768]{2,1,0:T(8,128)S(1)}, f32[3,8,32768]{2,1,0:T(8,128)S(1)}, u32[]{:S(2)}, u32[]{:S(2)}) %collective-permute-start.3) | collective-permute-done | bytes 3145760 | tf_op jit(solution)/shard_map/ppermute | solution.py:370
  9.8 0.0 copy-done.1
  9.8 2.0 %relay.1 = (f32[3,8,8192]{2,1,0:T(8,128)S(1)}, f32[3,8,20480]{2,1,0:T(8,128)S(1)}, f32[3,8,4096]{2,1,0:T(8,128)S(1)}) custom-call(s32[1]{0:T(128)} %bitcast.here_ref, s32[16]{0:T(128)S(1)} %copy-done.1, f32[16,32768]{1,0:T(8,128)S(1)} %get-tuple-element.26.phi_ref, f32[16,32768]{1,0:T(8,128)S(1)} %get-tuple-element.27.conc_ref, ...), custom_call_target="tpu_custom_call" | custom-call | flops 1000000 | bytes 6291456 | tf_op jit(solution)/shard_map/relay/pallas_call | solution.py:399
  11.8 8.0 %collective-permute-start.4 = (f32[3,8,8192]{2,1,0:T(8,128)S(1)}, f32[3,8,8192]{2,1,0:T(8,128)S(1)}, u32[]{:S(2)}, u32[]{:S(2)}) collective-permute-start(f32[3,8,8192]{2,1,0:T(8,128)S(1)} %get-tuple-element.37), channel_id=1, source_target_pairs={{0,2},{2,4},{3,1},{4,6},{5,3},{6,8},{7,5},{8,10},{9,7},{10,12},{11... | collective-permute-start | bytes 2359304 | tf_op jit(solution)/shard_map/ppermute | solution.py:370
  19.9 0.0 collective-permute-done.final_ref
  19.9 2.0 %stay.1 = (f32[3,8,8192]{2,1,0:T(8,128)S(1)}, f32[3,8,20480]{2,1,0:T(8,128)S(1)}, f32[3,8,4096]{2,1,0:T(8,128)S(1)}) custom-call(s32[1]{0:T(128)} %bitcast.here_ref, s32[16]{0:T(128)S(1)} %copy-done.1, f32[16,32768]{1,0:T(8,128)S(1)} %get-tuple-element.26.phi_ref, f32[16,32768]{1,0:T(8,128)S(1)} %get-tuple-element.27.conc_ref, ...), custom_call_target="tpu_custom_call" | custom-call | flops 1000000 | bytes 6291456 | tf_op jit(solution)/shard_map/stay/pallas_call | solution.py:410
  21.9 15.4 %collective-permute-done.4.back_ref = f32[3,8,8192]{2,1,0:T(8,128)S(1)} collective-permute-done((f32[3,8,8192]{2,1,0:T(8,128)S(1)}, f32[3,8,8192]{2,1,0:T(8,128)S(1)}, u32[]{:S(2)}, u32[]{:S(2)}) %collective-permute-start.4) | collective-permute-done | bytes 786464 | tf_op jit(solution)/shard_map/ppermute | solution.py:370
  37.3 0.0 copy-start
  37.3 8.4 %collective-permute-start.5 = (f32[3,8,20480]{2,1,0:T(8,128)S(1)}, f32[3,8,20480]{2,1,0:T(8,128)S(1)}, u32[]{:S(2)}, u32[]{:S(2)}) collective-permute-start(f32[3,8,20480]{2,1,0:T(8,128)S(1)} %get-tuple-element.39), channel_id=1, source_target_pairs={{0,2},{2,4},{3,1},{4,6},{5,3},{6,8},{7,5},{8,10},{9,7},{10,12},{11... | collective-permute-start | bytes 5898248 | tf_op jit(solution)/shard_map/ppermute | solution.py:370
  45.7 6.5 %collective-permute-done.1.far_ref = f32[3,8,28672]{2,1,0:T(8,128)S(1)} collective-permute-done((f32[3,8,28672]{2,1,0:T(8,128)S(1)}, f32[3,8,28672]{2,1,0:T(8,128)S(1)}, u32[]{:S(2)}, u32[]{:S(2)}) %collective-permute-start.1) | collective-permute-done | bytes 2752544 | tf_op jit(solution)/shard_map/ppermute | solution.py:370
  52.2 0.2 faces.1
  52.3 9.4 %collective-permute-start.6 = (f32[3,8,3072]{2,1,0:T(8,128)S(1)}, f32[3,8,3072]{2,1,0:T(8,128)S(1)}, u32[]{:S(2)}, u32[]{:S(2)}) collective-permute-start(f32[3,8,3072]{2,1,0:T(8,128)S(1)} %get-tuple-element.40), channel_id=1, source_target_pairs={{0,1},{1,2},{2,3},{3,4},{4,5},{5,6},{6,7},{7,8},{8,9},{9,10},{10,1... | collective-permute-start | bytes 884744 | tf_op jit(solution)/shard_map/ppermute | solution.py:370
  61.7 1.9 %collective-permute-start.7 = (f32[3,8,3072]{2,1,0:T(8,128)S(1)}, f32[3,8,3072]{2,1,0:T(8,128)S(1)}, u32[]{:S(2)}, u32[]{:S(2)}) collective-permute-start(f32[3,8,3072]{2,1,0:T(8,128)S(1)} %get-tuple-element.41), channel_id=1, source_target_pairs={{1,0},{2,1},{3,2},{4,3},{5,4},{6,5},{7,6},{8,7},{9,8},{10,9},{11,1... | collective-permute-start | bytes 884744 | tf_op jit(solution)/shard_map/ppermute | solution.py:370
  63.6 2.0 %collective-permute-start.2 = (f32[3,8,4096]{2,1,0:T(8,128)S(1)}, f32[3,8,4096]{2,1,0:T(8,128)S(1)}, u32[]{:S(2)}, u32[]{:S(2)}) collective-permute-start(f32[3,8,4096]{2,1,0:T(8,128)S(1)} %get-tuple-element.33), channel_id=1, source_target_pairs={{1,3},{2,0},{3,5},{4,2},{5,7},{6,4},{7,9},{8,6},{9,11},{10,8},{11,... | collective-permute-start | bytes 1179656 | tf_op jit(solution)/shard_map/ppermute | solution.py:370
  65.7 2.9 %collective-permute-done.6.below_ref = f32[3,8,3072]{2,1,0:T(8,128)S(1)} collective-permute-done((f32[3,8,3072]{2,1,0:T(8,128)S(1)}, f32[3,8,3072]{2,1,0:T(8,128)S(1)}, u32[]{:S(2)}, u32[]{:S(2)}) %collective-permute-start.6) | collective-permute-done | bytes 294944 | tf_op jit(solution)/shard_map/ppermute | solution.py:370
  68.6 3.7 %collective-permute-done.7.above_ref = f32[3,8,3072]{2,1,0:T(8,128)S(1)} collective-permute-done((f32[3,8,3072]{2,1,0:T(8,128)S(1)}, f32[3,8,3072]{2,1,0:T(8,128)S(1)}, u32[]{:S(2)}, u32[]{:S(2)}) %collective-permute-start.7) | collective-permute-done | bytes 294944 | tf_op jit(solution)/shard_map/ppermute | solution.py:370
  72.2 5.1 %collective-permute-done.5.back_ref = f32[3,8,20480]{2,1,0:T(8,128)S(1)} collective-permute-done((f32[3,8,20480]{2,1,0:T(8,128)S(1)}, f32[3,8,20480]{2,1,0:T(8,128)S(1)}, u32[]{:S(2)}, u32[]{:S(2)}) %collective-permute-start.5) | collective-permute-done | bytes 1966112 | tf_op jit(solution)/shard_map/ppermute | solution.py:370
  77.3 8.3 %collective-permute-start.8 = (f32[3,8,4096]{2,1,0:T(8,128)S(1)}, f32[3,8,4096]{2,1,0:T(8,128)S(1)}, u32[]{:S(2)}, u32[]{:S(2)}) collective-permute-start(f32[3,8,4096]{2,1,0:T(8,128)S(1)} %get-tuple-element.42), channel_id=1, source_target_pairs={{0,2},{2,4},{3,1},{4,6},{5,3},{6,8},{7,5},{8,10},{9,7},{10,12},{11... | collective-permute-start | bytes 1179656 | tf_op jit(solution)/shard_map/ppermute | solution.py:370
  85.6 0.0 copy-done
  85.6 11.8 %early_steps.1 = (f32[8,32768]{1,0:T(8,128)}, f32[8,32768]{1,0:T(8,128)}, f32[3,6,8,1024]{3,2,1,0:T(8,128)S(1)}, f32[2,4,8,1024]{3,2,1,0:T(8,128)S(1)}, f32[2,4,8,1024]{3,2,1,0:T(8,128)S(1)}) custom-call(s32[1]{0:T(128)} %bitcast.here_ref, f32[3,8,8192]{2,1,0:T(8,128)S(1)} %get-tuple-element.43.edge_ref, f32[3,8,20480]{2,1,0:T(8,128)S(1)} %get-tuple-element.44.stay_ref, ...), custom_call_target="tpu_custom_call" | custom-call | flops 1000000 | bytes 20971520 | tf_op jit(solution)/shard_map/early_steps/pallas_call | solution.py:444
  97.5 0.0 collective-permute-done.2.far_ref
  97.5 0.0 collective-permute-done.8.back_ref
  97.5 3.9 %late_steps.1 = (f32[8,32768]{1,0:T(8,128)}, f32[8,32768]{1,0:T(8,128)}) custom-call(s32[1]{0:T(128)} %bitcast.here_ref, f32[3,8,4096]{2,1,0:T(8,128)S(1)} %get-tuple-element.30.stay_ref, f32[3,8,4096]{2,1,0:T(8,128)S(1)} %collective-permute-done.2.far_ref, ...), custom_call_target="tpu_custom_call", output_to_operand_aliasing={{0}: (8, {}), {1}: (9, {})} | custom-call | flops 1000000 | bytes 8388608 | tf_op jit(solution)/shard_map/late_steps/pallas_call | solution.py:457
Async XLA Ops:
  0.6 9.2 %copy-start.1 = (s32[16]{0:T(128)S(1)}, s32[16]{0:T(128)}, u32[]{:S(2)}) copy-start(s32[16]{0:T(128)} %slot_ref.3) | copy-start | bytes 196
  3.8 6.0 %collective-permute-start.3 = (f32[3,8,32768]{2,1,0:T(8,128)S(1)}, f32[3,8,32768]{2,1,0:T(8,128)S(1)}, u32[]{:S(2)}, u32[]{:S(2)}) collective-permute-start(f32[3,8,32768]{2,1,0:T(8,128)S(1)} %get-tuple-element.34), channel_id=1, source_target_pairs={{0,1},{1,0},{2,3},{3,2},{4,5},{5,4},{6,7},{7,6},{8,9},{9,8},{10,11... | collective-permute-start | bytes 9437192 | tf_op jit(solution)/shard_map/ppermute | solution.py:370
  4.5 15.3 %collective-permute-start = (f32[3,8,32768]{2,1,0:T(8,128)S(1)}, f32[3,8,32768]{2,1,0:T(8,128)S(1)}, u32[]{:S(2)}, u32[]{:S(2)}) collective-permute-start(f32[3,8,32768]{2,1,0:T(8,128)S(1)} %get-tuple-element.29), channel_id=1, source_target_pairs={{0,1},{1,0},{2,3},{3,2},{4,5},{5,4},{6,7},{7,6},{8,9},{9,8},{10,11... | collective-permute-start | bytes 9437192 | tf_op jit(solution)/shard_map/ppermute | solution.py:370
  4.6 47.6 %collective-permute-start.1 = (f32[3,8,28672]{2,1,0:T(8,128)S(1)}, f32[3,8,28672]{2,1,0:T(8,128)S(1)}, u32[]{:S(2)}, u32[]{:S(2)}) collective-permute-start(f32[3,8,28672]{2,1,0:T(8,128)S(1)} %get-tuple-element.32), channel_id=1, source_target_pairs={{1,3},{2,0},{3,5},{4,2},{5,7},{6,4},{7,9},{8,6},{9,11},{10,8},{11,... | collective-permute-start | bytes 8257544 | tf_op jit(solution)/shard_map/ppermute | solution.py:370
  11.8 25.5 %collective-permute-start.4 = (f32[3,8,8192]{2,1,0:T(8,128)S(1)}, f32[3,8,8192]{2,1,0:T(8,128)S(1)}, u32[]{:S(2)}, u32[]{:S(2)}) collective-permute-start(f32[3,8,8192]{2,1,0:T(8,128)S(1)} %get-tuple-element.37), channel_id=1, source_target_pairs={{0,2},{2,4},{3,1},{4,6},{5,3},{6,8},{7,5},{8,10},{9,7},{10,12},{11... | collective-permute-start | bytes 2359304 | tf_op jit(solution)/shard_map/ppermute | solution.py:370
  37.3 48.4 %copy-start = (s32[8,6]{1,0:T(8,128)S(1)}, s32[8,6]{1,0:T(8,128)}, u32[]{:S(2)}) copy-start(s32[8,6]{1,0:T(8,128)} %nbr_ref.3) | copy-start | bytes 580
  37.3 40.1 %collective-permute-start.5 = (f32[3,8,20480]{2,1,0:T(8,128)S(1)}, f32[3,8,20480]{2,1,0:T(8,128)S(1)}, u32[]{:S(2)}, u32[]{:S(2)}) collective-permute-start(f32[3,8,20480]{2,1,0:T(8,128)S(1)} %get-tuple-element.39), channel_id=1, source_target_pairs={{0,2},{2,4},{3,1},{4,6},{5,3},{6,8},{7,5},{8,10},{9,7},{10,12},{11... | collective-permute-start | bytes 5898248 | tf_op jit(solution)/shard_map/ppermute | solution.py:370
  52.3 16.2 %collective-permute-start.6 = (f32[3,8,3072]{2,1,0:T(8,128)S(1)}, f32[3,8,3072]{2,1,0:T(8,128)S(1)}, u32[]{:S(2)}, u32[]{:S(2)}) collective-permute-start(f32[3,8,3072]{2,1,0:T(8,128)S(1)} %get-tuple-element.40), channel_id=1, source_target_pairs={{0,1},{1,2},{2,3},{3,4},{4,5},{5,6},{6,7},{7,8},{8,9},{9,10},{10,1... | collective-permute-start | bytes 884744 | tf_op jit(solution)/shard_map/ppermute | solution.py:370
  61.7 10.5 %collective-permute-start.7 = (f32[3,8,3072]{2,1,0:T(8,128)S(1)}, f32[3,8,3072]{2,1,0:T(8,128)S(1)}, u32[]{:S(2)}, u32[]{:S(2)}) collective-permute-start(f32[3,8,3072]{2,1,0:T(8,128)S(1)} %get-tuple-element.41), channel_id=1, source_target_pairs={{1,0},{2,1},{3,2},{4,3},{5,4},{6,5},{7,6},{8,7},{9,8},{10,9},{11,1... | collective-permute-start | bytes 884744 | tf_op jit(solution)/shard_map/ppermute | solution.py:370
  63.6 33.9 %collective-permute-start.2 = (f32[3,8,4096]{2,1,0:T(8,128)S(1)}, f32[3,8,4096]{2,1,0:T(8,128)S(1)}, u32[]{:S(2)}, u32[]{:S(2)}) collective-permute-start(f32[3,8,4096]{2,1,0:T(8,128)S(1)} %get-tuple-element.33), channel_id=1, source_target_pairs={{1,3},{2,0},{3,5},{4,2},{5,7},{6,4},{7,9},{8,6},{9,11},{10,8},{11,... | collective-permute-start | bytes 1179656 | tf_op jit(solution)/shard_map/ppermute | solution.py:370
  77.3 20.2 %collective-permute-start.8 = (f32[3,8,4096]{2,1,0:T(8,128)S(1)}, f32[3,8,4096]{2,1,0:T(8,128)S(1)}, u32[]{:S(2)}, u32[]{:S(2)}) collective-permute-start(f32[3,8,4096]{2,1,0:T(8,128)S(1)} %get-tuple-element.42), channel_id=1, source_target_pairs={{0,2},{2,4},{3,1},{4,6},{5,3},{6,8},{7,5},{8,10},{9,7},{10,12},{11... | collective-permute-start | bytes 1179656 | tf_op jit(solution)/shard_map/ppermute | solution.py:370

commit v5 on v3

--- a/solution.py
+++ b/solution.py
@@ -19,10 +19,9 @@
 CHUNKS = EDGE // CHUNK_PLANES
 LANES = 128
 EXT = EDGE + 2 * HALO
-MID = 16
-LATE = EDGE - 2 * CHUNK_PLANES - MID
-MID_CHUNKS = MID // CHUNK_PLANES
-LATE_CHUNKS = LATE // CHUNK_PLANES
+REST = EDGE - 2 * CHUNK_PLANES
+AHEAD = 20
+FIRST_STEPS = 2 + AHEAD // CHUNK_PLANES
 VREGS = FACE // LANES
 
 time_step = 0.15
@@ -102,34 +101,25 @@
                 final_ref[f, :, lanes] = picked(final, *rows)
                 out_ref[f, :, lanes_at(out_start, v)] = picked(far, *rows)
 
-    first_steps = 2 + MID_CHUNKS
-
-    @pl.loop(0, first_steps)
+    @pl.loop(0, FIRST_STEPS)
     def _(i):
         for copy in copies(i):
             copy.wait()
         fill(i, far_ref, i * CHUNK)
 
-    @pl.loop(first_steps, CHUNKS)
+    @pl.loop(FIRST_STEPS, CHUNKS)
     def _(i):
         for copy in copies(i):
             copy.wait()
-        fill(i, late_ref, (i - first_steps) * CHUNK)
-
-
-TOP = CHUNK_PLANES + MID + LATE
-PARTS = (2 * CHUNK_PLANES, MID, LATE)
-HALVES = (2 * CHUNK_PLANES, MID // 2, MID // 2, LATE // 2, LATE // 2)
-
-
-def add_rows(masks, amount, old_refs, add_ref, part_refs, sizes):
-    edge_ref, *rest = part_refs
-    spans = [(edge_ref, 0, 0, CHUNK_PLANES), (edge_ref, CHUNK_PLANES, TOP, CHUNK_PLANES)]
-    first = CHUNK_PLANES
-    for part_ref, size in zip(rest, sizes[1:]):
-        spans.append((part_ref, 0, first, size))
-        first += size
-    for out_ref, out_plane, plane, count in spans:
+        fill(i, late_ref, (i - FIRST_STEPS) * CHUNK)
+
+
+def add_rows(masks, amount, old_refs, add_ref, edge_ref, rest_ref):
+    for out_ref, out_plane, plane, count in (
+        (edge_ref, 0, 0, CHUNK_PLANES),
+        (edge_ref, CHUNK_PLANES, CHUNK_PLANES + REST, CHUNK_PLANES),
+        (rest_ref, 0, CHUNK_PLANES, REST),
+    ):
 
         @pl.loop(0, count // 2)
         def _(i):
@@ -143,13 +133,13 @@
 def relay_kernel(here_ref, slot_ref, phi_ref, conc_ref, mob_ref, merge_ref, *part_refs):
     here = here_ref[0]
     amount, masks = windows(slot_ref, here)
-    add_rows(masks(-2 * side_of(here)), amount, (phi_ref, conc_ref, mob_ref), merge_ref, part_refs, HALVES)
+    add_rows(masks(-2 * side_of(here)), amount, (phi_ref, conc_ref, mob_ref), merge_ref, *part_refs)
 
 
 def stay_kernel(here_ref, slot_ref, phi_ref, conc_ref, mob_ref, final_ref, *part_refs):
     here = here_ref[0]
     amount, masks = windows(slot_ref, here)
-    add_rows(masks(0), amount, (phi_ref, conc_ref, mob_ref), final_ref, part_refs, PARTS)
+    add_rows(masks(0), amount, (phi_ref, conc_ref, mob_ref), final_ref, *part_refs)
 
 
 def face_kernel(stay_ref, far_ref, back_ref, edge_ref, low_ref, high_ref):
@@ -264,28 +254,22 @@
                     ref[x + at, :, pl.ds(v * LANES, LANES)] = value
 
 
-MID_AT = HALO + CHUNK_PLANES
-LATE_AT = MID_AT + MID
-TOP_AT = LATE_AT + LATE
-
-
-def early_kernel(
-    here_ref, edge_ref, stay_ref, far_ref, back_low_ref, back_high_ref, below_ref, above_ref, nbr_ref,
+REST_AT = HALO + CHUNK_PLANES
+TOP_AT = REST_AT + REST
+
+
+def edge_kernel(
+    here_ref, edge_ref, below_ref, above_ref, nbr_ref,
     phase_ref, solute_ref, kept0_ref, kept1_ref, kept2_ref,
     phi0, conc0, mob, phi1, conc1, phi2, conc2,
 ):
     st = Stencil(here_ref[0], nbr_ref[...])
-    back_refs = (back_low_ref, back_high_ref)
     states = (phi0, conc0, mob)
     for f, ref in enumerate(states):
         for d in range(2 * CHUNK_PLANES):
             at = HALO + d if d < CHUNK_PLANES else TOP_AT + d - CHUNK_PLANES
             for v in range(VREGS):
                 ref[at, :, pl.ds(v * LANES, LANES)] = edge_ref[f, :, pl.ds(d * FACE + v * LANES, LANES)]
-    for n, back_ref in enumerate(back_refs):
-        done = n * MID // 2
-        place(states, MID // 2, MID_AT + done, (stay_ref, done), (far_ref, 2 * CHUNK_PLANES + done), (back_ref, 0))
-    for f, ref in enumerate(states):
         for d in range(HALO):
             for v in range(VREGS):
                 lanes = pl.ds(v * LANES, LANES)
@@ -294,38 +278,37 @@
                 ref[d, :, lanes] = jnp.where(st.has_below_x, st.rows(below_ref[f, :, part], st.below_x), mirror_low)
                 mirror_high = ref[EDGE + HALO - 1 - d, :, lanes]
                 ref[EDGE + HALO + d, :, lanes] = jnp.where(st.has_above_x, st.rows(above_ref[f, :, part], st.above_x), mirror_high)
-    st.sweep(1, LATE_AT - 1, 4, (phi0, conc0), mob, (phi1, conc1))
-    st.sweep(TOP_AT + 1, EXT - 1, 5, (phi0, conc0), mob, (phi1, conc1))
-    st.sweep(2, LATE_AT - 2, 4, (phi1, conc1), mob, (phi2, conc2))
-    st.sweep(TOP_AT + 2, EXT - 2, 3, (phi1, conc1), mob, (phi2, conc2))
-    st.sweep(HALO, LATE_AT - 3, 4, (phi2, conc2), mob, (phase_ref, solute_ref), HALO)
-    st.sweep(TOP_AT + 3, EXT - 3, 1, (phi2, conc2), mob, (phase_ref, solute_ref), HALO)
+    for first, last in ((1, REST_AT - 1), (TOP_AT + 1, EXT - 1)):
+        st.sweep(first, last, 5, (phi0, conc0), mob, (phi1, conc1))
+        st.sweep(first + 1, last - 1, 3, (phi1, conc1), mob, (phi2, conc2))
+        st.sweep(first + 2, last - 2, 1, (phi2, conc2), mob, (phase_ref, solute_ref), HALO)
     for f, ref in enumerate(states):
-        for n, x in enumerate((*range(LATE_AT - 3, LATE_AT), *range(TOP_AT, TOP_AT + 3))):
+        for n, x in enumerate((*range(REST_AT - 3, REST_AT), *range(TOP_AT, TOP_AT + 3))):
             kept0_ref[f, n] = ref[x]
     for f, ref in enumerate((phi1, conc1)):
-        for n, x in enumerate((LATE_AT - 3, LATE_AT - 2, TOP_AT + 1, TOP_AT + 2)):
+        for n, x in enumerate((REST_AT - 3, REST_AT - 2, TOP_AT + 1, TOP_AT + 2)):
             kept1_ref[f, n] = ref[x]
     for f, ref in enumerate((phi2, conc2)):
-        for n, x in enumerate((LATE_AT - 4, LATE_AT - 3, TOP_AT + 2, TOP_AT + 3)):
+        for n, x in enumerate((REST_AT - 4, REST_AT - 3, TOP_AT + 2, TOP_AT + 3)):
             kept2_ref[f, n] = ref[x]
 
 
-BACK = LATE_AT - 4
-LATE_PLANES = TOP_AT + 4 - BACK
-OUT_FIRST = LATE_AT - 3
+BACK = REST_AT - 4
+MAIN_PLANES = TOP_AT + 4 - BACK
+OUT_FIRST = REST_AT - 3
 OUT_PLANES = TOP_AT + 3 - OUT_FIRST
-
-
-def late_kernel(
-    here_ref, stay_ref, far_ref, back_low_ref, back_high_ref, nbr_ref, kept0_ref, kept1_ref, kept2_ref, _phase_in, _solute_in,
+PIECE = 6
+PIECES = OUT_PLANES // PIECE
+
+
+def main_kernel(
+    here_ref, stay_ref, far_ref, far_late_ref, back_ref, nbr_ref, kept0_ref, kept1_ref, kept2_ref, _phase_in, _solute_in,
     phase_hbm, solute_hbm,
     phi0, conc0, mob, phi1, conc1, phi2, conc2, phase_ref, solute_ref, sems,
 ):
     st = Stencil(here_ref[0], nbr_ref[...])
-    back_refs = (back_low_ref, back_high_ref)
     states = (phi0, conc0, mob)
-    first, last = LATE_AT - BACK, TOP_AT - BACK
+    first, last = REST_AT - BACK, TOP_AT - BACK
     for f, ref in enumerate(states):
         for n, x in enumerate((*range(first - 3, first), *range(last, last + 3))):
             ref[x] = kept0_ref[f, n]
@@ -335,18 +318,20 @@
     for f, ref in enumerate((phi2, conc2)):
         for n, x in enumerate((first - 4, first - 3, last + 2, last + 3)):
             ref[x] = kept2_ref[f, n]
-    for n, back_ref in enumerate(back_refs):
-        done = n * LATE // 2
-        place(states, LATE // 2, first + done, (stay_ref, done), (far_ref, done), (back_ref, 0))
+    place(states, AHEAD, first, (stay_ref, 0), (far_ref, 2 * CHUNK_PLANES), (back_ref, 0))
+    place(states, REST - AHEAD, first + AHEAD, (stay_ref, AHEAD), (far_late_ref, 0), (back_ref, AHEAD))
     st.sweep(first - 1, last + 1, 5, (phi0, conc0), mob, (phi1, conc1))
     st.sweep(first - 2, last + 2, 4, (phi1, conc1), mob, (phi2, conc2))
-    st.sweep(first - 3, last + 3, 7, (phi2, conc2), mob, (phase_ref, solute_ref), first - 3)
+    start = first - 3
     copies = []
-    for n, (ref, hbm) in enumerate(((phase_ref, phase_hbm), (solute_ref, solute_hbm))):
-        lanes = pl.ds((OUT_FIRST - HALO) * FACE, OUT_PLANES * FACE)
-        copies.append(pltpu.make_async_copy(ref, hbm.at[:, lanes], sems.at[n]))
-    for copy in copies:
-        copy.start()
+    for piece in range(PIECES):
+        at = start + piece * PIECE
+        st.sweep(at, at + PIECE, PIECE, (phi2, conc2), mob, (phase_ref, solute_ref), start)
+        source = pl.ds(piece * PIECE * FACE, PIECE * FACE)
+        target = pl.ds((OUT_FIRST - HALO + piece * PIECE) * FACE, PIECE * FACE)
+        for n, (ref, hbm) in enumerate(((phase_ref, phase_hbm), (solute_ref, solute_hbm))):
+            copies.append(pltpu.make_async_copy(ref.at[:, source], hbm.at[:, target], sems.at[piece, n]))
+            copies[-1].start()
     for copy in copies:
         copy.wait()
 
@@ -394,7 +379,7 @@
         pack_kernel,
         in_specs=[SMEM, HBM, HBM, HBM, HBM],
         out_specs=[VMEM] * 7,
-        out_shape=[old_shape] * 3 + [shaped(EDGE)] * 2 + [shaped(2 * CHUNK_PLANES + MID), shaped(LATE)],
+        out_shape=[old_shape] * 3 + [shaped(EDGE)] * 2 + [shaped(2 * CHUNK_PLANES + AHEAD), shaped(REST - AHEAD)],
         scratch_shapes=[pltpu.SMEM((OLD,), jnp.int32), pltpu.SemaphoreType.DMA, pltpu.SemaphoreType.DMA((CHUNKS, FIELDS))],
         compiler_params=PARAMS,
         cost_estimate=cost(6 * MB),
@@ -404,27 +389,28 @@
     merge_got = sent(merge, partner)
     final_got = sent(final, partner)
 
-    back_edge, *back_mid, back_late_low, back_late_high = pl.pallas_call(
+    two_parts = [shaped(2 * CHUNK_PLANES), shaped(REST)]
+    back_edge, back_rest = pl.pallas_call(
         relay_kernel,
         in_specs=[SMEM, SMEM] + [VMEM] * 4,
-        out_specs=[VMEM] * len(HALVES),
-        out_shape=[shaped(size) for size in HALVES],
+        out_specs=[VMEM] * 2,
+        out_shape=two_parts,
         compiler_params=PARAMS,
         cost_estimate=cost(6 * MB),
         name="relay",
     )(here, new_global_slot, *olds, merge_got)
     back_edge_got = sent(back_edge, back_route)
 
-    stay_edge, stay_mid, stay_late = pl.pallas_call(
+    stay_edge, stay_rest = pl.pallas_call(
         stay_kernel,
         in_specs=[SMEM, SMEM] + [VMEM] * 4,
-        out_specs=[VMEM] * 3,
-        out_shape=[shaped(size) for size in PARTS],
+        out_specs=[VMEM] * 2,
+        out_shape=two_parts,
         compiler_params=PARAMS,
         cost_estimate=cost(6 * MB),
         name="stay",
     )(here, new_global_slot, *olds, final_got)
-    back_mid_got = [sent(after(half, back_edge_got, stay_edge), back_route) for half in back_mid]
+    back_rest_got = sent(after(back_rest, back_edge_got, stay_edge), back_route)
     far_late_got = sent(after(far_late, far_first_got), far_route)
 
     edges = pl.BlockSpec((FIELDS, CAP, 2 * CHUNK), lambda i: (0, 0, 0))
@@ -441,8 +427,6 @@
     )(stay_edge, far_first_got, back_edge_got)
     below = sent(high, [(p, p + 1) for p in devices])
     above = sent(low, [(p, p - 1) for p in devices])
-    back_late = (back_late_low, back_late_high)
-    back_late_got = [sent(after(half, *back_mid_got, below, above), back_route) for half in back_late]
 
     state = pltpu.VMEM((EXT, CAP, FACE), jnp.float32)
     whole = jax.ShapeDtypeStruct((CAP, CELLS), jnp.float32)
@@ -451,29 +435,29 @@
         return jax.ShapeDtypeStruct((fields, planes, CAP, FACE), jnp.float32)
 
     phase, solute, kept0, kept1, kept2 = pl.pallas_call(
-        early_kernel,
-        in_specs=[SMEM] + [VMEM] * 8,
+        edge_kernel,
+        in_specs=[SMEM] + [VMEM] * 4,
         out_specs=[VMEM] * 5,
         out_shape=[whole, whole, kept(3, 6), kept(2, 4), kept(2, 4)],
         scratch_shapes=[state] * 7,
         compiler_params=PARAMS,
-        cost_estimate=cost(20 * MB),
-        name="early_steps",
-    )(here, edge, stay_mid, far_first_got, *back_mid_got, below, above, neighbors)
-
-    state = pltpu.VMEM((LATE_PLANES, CAP, FACE), jnp.float32)
+        cost_estimate=cost(8 * MB),
+        name="edge_steps",
+    )(here, edge, below, above, neighbors)
+
+    state = pltpu.VMEM((MAIN_PLANES, CAP, FACE), jnp.float32)
     rows_out = pltpu.VMEM((CAP, OUT_PLANES * FACE), jnp.float32)
     phase, solute = pl.pallas_call(
-        late_kernel,
+        main_kernel,
         in_specs=[SMEM] + [VMEM] * 8 + [HBM] * 2,
         out_specs=[HBM] * 2,
         out_shape=[whole, whole],
-        scratch_shapes=[state] * 7 + [rows_out] * 2 + [pltpu.SemaphoreType.DMA((2,))],
+        scratch_shapes=[state] * 7 + [rows_out] * 2 + [pltpu.SemaphoreType.DMA((PIECES, 2))],
         input_output_aliases={9: 0, 10: 1},
         compiler_params=PARAMS,
-        cost_estimate=cost(8 * MB),
-        name="late_steps",
-    )(here, stay_late, far_late_got, *back_late_got, neighbors, kept0, kept1, kept2, phase, solute)
+        cost_estimate=cost(20 * MB),
+        name="main_steps",
+    )(here, stay_rest, far_first_got, far_late_got, back_rest_got, neighbors, kept0, kept1, kept2, phase, solute)
     return phase, solute
 
 

time: 103 us -> 99.2 us (0.963)
  starting transfers between devices: 36.8 us -> 31.1 us
  waiting for transfers between devices: 42.1 us -> 44.4 us
    ppermute x11 -> x8, starting transfers between devices: 36.8 us -> 31.1 us  [sent(): lax.ppermute(block, 'blk', [(p, q) for p, q in route if 0 <= q < count])]
    ppermute x11 -> x8, waiting for transfers between devices: 42.1 us -> 44.4 us  [sent(): lax.ppermute(block, 'blk', [(p, q) for p, q in route if 0 <= q < count])]
  transfers between devices with their start and end apart: 11 -> 8, of which waited for: 5 -> 4; matrix products, arithmetic and copies ran while one was open for 0% -> 0% of each run, Pallas kernels for 14% -> 8%
where the time goes in v5:
time: 99.2 us; the launch traced here: 98.7 us
  waiting for transfers between devices  44.4 us (45%)
  starting transfers between devices  31.1 us (31%)
  Pallas kernels  22.5 us (23%)
    ppermute x8, waiting for transfers between devices, sent(): lax.ppermute(block, 'blk', [(p, q) for p, q in route if 0 <= q < count])  44.4 us
    ppermute x8, starting transfers between devices, sent(): lax.ppermute(block, 'blk', [(p, q) for p, q in route if 0 <= q < count])  31.1 us
    pallas_call x1, Pallas kernels, on_device(): pl.pallas_call(main_kernel, in_specs=[SMEM] + [VMEM] * 8 + [HBM] * 2, out...  11.9 us
    pallas_call x1, Pallas kernels, on_device(): pl.pallas_call(edge_kernel, in_specs=[SMEM] + [VMEM] * 4, out_specs=[VMEM...  3.32 us
    pallas_call x1, Pallas kernels, on_device(): pl.pallas_call(pack_kernel, in_specs=[SMEM, HBM, HBM, HBM, HBM], out_spec...  3.11 us
    pallas_call x1, Pallas kernels, on_device(): pl.pallas_call(relay_kernel, in_specs=[SMEM, SMEM] + [VMEM] * 4, out_spec...  1.99 us
    pallas_call x1, Pallas kernels, on_device(): pl.pallas_call(stay_kernel, in_specs=[SMEM, SMEM] + [VMEM] * 4, out_specs...  1.99 us
  transfers between devices with their start and end apart: 8, of which 4 were waited for; matrix products, arithmetic and copies ran while one was open for 0% of the time, Pallas kernels for 8%

profile of v5, /device:TPU:24, one launch (start us, length us, event | category | flops | bytes accessed | tf_op | source)
XLA Modules:
  0.0 98.7 jit_solution(18120230082164916925)
XLA Ops:
  0.6 0.0 copy-start.1
  0.6 3.1 %pack.1 = (f32[16,32768]{1,0:T(8,128)S(1)}, f32[16,32768]{1,0:T(8,128)S(1)}, f32[16,32768]{1,0:T(8,128)S(1)}, f32[3,8,32768]{2,1,0:T(8,128)S(1)}, f32[3,8,32768]...) custom-call(s32[1]{0:T(128)} %bitcast.here_ref, s32[16]{0:T(128)} %slot_ref.3, ...), custom_call_target="tpu_custom_call" | custom-call | flops 1000000 | bytes 6291456 | tf_op jit(solution)/shard_map/pack/pallas_call | solution.py:378
  3.8 0.1 collective-permute-start.3
  3.9 0.5 collective-permute-start
  4.4 8.3 %collective-permute-start.1 = (f32[3,8,28672]{2,1,0:T(8,128)S(1)}, f32[3,8,28672]{2,1,0:T(8,128)S(1)}, u32[]{:S(2)}, u32[]{:S(2)}) collective-permute-start(f32[3,8,28672]{2,1,0:T(8,128)S(1)} %get-tuple-element.28), channel_id=1, source_target_pairs={{1,3},{2,0},{3,5},{4,2},{5,7},{6,4},{7,9},{8,6},{9,11},{10,8},{11,... | collective-permute-start | bytes 8257544 | tf_op jit(solution)/shard_map/ppermute | solution.py:364
  12.7 0.0 collective-permute-done.3.merge_ref
  12.7 0.0 copy-done.1
  12.7 2.0 %relay.1 = (f32[3,8,8192]{2,1,0:T(8,128)S(1)}, f32[3,8,24576]{2,1,0:T(8,128)S(1)}) custom-call(s32[1]{0:T(128)} %bitcast.here_ref, s32[16]{0:T(128)S(1)} %copy-done.1, f32[16,32768]{1,0:T(8,128)S(1)} %get-tuple-element.23.phi_ref, f32[16,32768]{1,0:T(8,128)S(1)} %get-tuple-element.24.conc_ref, f32[16,32768]{1,0:T(8,128)S(1)} %get-tuple-element.25.mob_ref, ...), custom_call_target="tpu_custom_call" | custom-call | flops 1000000 | bytes 6291456 | tf_op jit(solution)/shard_map/relay/pallas_call | solution.py:393
  14.7 1.9 %collective-permute-start.4 = (f32[3,8,8192]{2,1,0:T(8,128)S(1)}, f32[3,8,8192]{2,1,0:T(8,128)S(1)}, u32[]{:S(2)}, u32[]{:S(2)}) collective-permute-start(f32[3,8,8192]{2,1,0:T(8,128)S(1)} %get-tuple-element.33), channel_id=1, source_target_pairs={{0,2},{2,4},{3,1},{4,6},{5,3},{6,8},{7,5},{8,10},{9,7},{10,12},{11... | collective-permute-start | bytes 2359304 | tf_op jit(solution)/shard_map/ppermute | solution.py:364
  16.6 0.0 collective-permute-done.final_ref
  16.6 2.0 %stay.1 = (f32[3,8,8192]{2,1,0:T(8,128)S(1)}, f32[3,8,24576]{2,1,0:T(8,128)S(1)}) custom-call(s32[1]{0:T(128)} %bitcast.here_ref, s32[16]{0:T(128)S(1)} %copy-done.1, f32[16,32768]{1,0:T(8,128)S(1)} %get-tuple-element.23.phi_ref, f32[16,32768]{1,0:T(8,128)S(1)} %get-tuple-element.24.conc_ref, f32[16,32768]{1,0:T(8,128)S(1)} %get-tuple-element.25.mob_ref, ...), custom_call_target="tpu_custom_call" | custom-call | flops 1000000 | bytes 6291456 | tf_op jit(solution)/shard_map/stay/pallas_call | solution.py:404
  18.6 0.0 copy-start
  18.6 22.6 %collective-permute-done.4.back_ref = f32[3,8,8192]{2,1,0:T(8,128)S(1)} collective-permute-done((f32[3,8,8192]{2,1,0:T(8,128)S(1)}, f32[3,8,8192]{2,1,0:T(8,128)S(1)}, u32[]{:S(2)}, u32[]{:S(2)}) %collective-permute-start.4) | collective-permute-done | bytes 786464 | tf_op jit(solution)/shard_map/ppermute | solution.py:364
  41.3 1.9 %collective-permute-start.5 = (f32[3,8,24576]{2,1,0:T(8,128)S(1)}, f32[3,8,24576]{2,1,0:T(8,128)S(1)}, u32[]{:S(2)}, u32[]{:S(2)}) collective-permute-start(f32[3,8,24576]{2,1,0:T(8,128)S(1)} %get-tuple-element.35), channel_id=1, source_target_pairs={{0,2},{2,4},{3,1},{4,6},{5,3},{6,8},{7,5},{8,10},{9,7},{10,12},{11... | collective-permute-start | bytes 7077896 | tf_op jit(solution)/shard_map/ppermute | solution.py:364
  43.2 14.3 %collective-permute-done.1.far_ref = f32[3,8,28672]{2,1,0:T(8,128)S(1)} collective-permute-done((f32[3,8,28672]{2,1,0:T(8,128)S(1)}, f32[3,8,28672]{2,1,0:T(8,128)S(1)}, u32[]{:S(2)}, u32[]{:S(2)}) %collective-permute-start.1) | collective-permute-done | bytes 2752544 | tf_op jit(solution)/shard_map/ppermute | solution.py:364
  57.5 8.6 %collective-permute-start.2 = (f32[3,8,4096]{2,1,0:T(8,128)S(1)}, f32[3,8,4096]{2,1,0:T(8,128)S(1)}, u32[]{:S(2)}, u32[]{:S(2)}) collective-permute-start(f32[3,8,4096]{2,1,0:T(8,128)S(1)} %get-tuple-element.30), channel_id=1, source_target_pairs={{1,3},{2,0},{3,5},{4,2},{5,7},{6,4},{7,9},{8,6},{9,11},{10,8},{11,... | collective-permute-start | bytes 1179656 | tf_op jit(solution)/shard_map/ppermute | solution.py:364
  66.1 0.2 faces.1
  66.2 1.9 %collective-permute-start.6 = (f32[3,8,3072]{2,1,0:T(8,128)S(1)}, f32[3,8,3072]{2,1,0:T(8,128)S(1)}, u32[]{:S(2)}, u32[]{:S(2)}) collective-permute-start(f32[3,8,3072]{2,1,0:T(8,128)S(1)} %get-tuple-element.37), channel_id=1, source_target_pairs={{0,1},{1,2},{2,3},{3,4},{4,5},{5,6},{6,7},{7,8},{8,9},{9,10},{10,1... | collective-permute-start | bytes 884744 | tf_op jit(solution)/shard_map/ppermute | solution.py:364
  68.2 7.9 %collective-permute-start.7 = (f32[3,8,3072]{2,1,0:T(8,128)S(1)}, f32[3,8,3072]{2,1,0:T(8,128)S(1)}, u32[]{:S(2)}, u32[]{:S(2)}) collective-permute-start(f32[3,8,3072]{2,1,0:T(8,128)S(1)} %get-tuple-element.38), channel_id=1, source_target_pairs={{1,0},{2,1},{3,2},{4,3},{5,4},{6,5},{7,6},{8,7},{9,8},{10,9},{11,1... | collective-permute-start | bytes 884744 | tf_op jit(solution)/shard_map/ppermute | solution.py:364
  76.0 5.7 %collective-permute-done.6.below_ref = f32[3,8,3072]{2,1,0:T(8,128)S(1)} collective-permute-done((f32[3,8,3072]{2,1,0:T(8,128)S(1)}, f32[3,8,3072]{2,1,0:T(8,128)S(1)}, u32[]{:S(2)}, u32[]{:S(2)}) %collective-permute-start.6) | collective-permute-done | bytes 294944 | tf_op jit(solution)/shard_map/ppermute | solution.py:364
  81.7 1.8 %collective-permute-done.7.above_ref = f32[3,8,3072]{2,1,0:T(8,128)S(1)} collective-permute-done((f32[3,8,3072]{2,1,0:T(8,128)S(1)}, f32[3,8,3072]{2,1,0:T(8,128)S(1)}, u32[]{:S(2)}, u32[]{:S(2)}) %collective-permute-start.7) | collective-permute-done | bytes 294944 | tf_op jit(solution)/shard_map/ppermute | solution.py:364
  83.5 0.0 copy-done
  83.5 3.3 %edge_steps.1 = (f32[8,32768]{1,0:T(8,128)}, f32[8,32768]{1,0:T(8,128)}, f32[3,6,8,1024]{3,2,1,0:T(8,128)S(1)}, f32[2,4,8,1024]{3,2,1,0:T(8,128)S(1)}, f32[2,4,8,1024]{3,2,1,0:T(8,128)S(1)}) custom-call(s32[1]{0:T(128)} %bitcast.here_ref, f32[3,8,8192]{2,1,0:T(8,128)S(1)} %get-tuple-element.36.edge_ref, f32[3,8,3072]{2,1,0:T(8,128)S(1)} %collective-permute-done.6.below_ref, ...), custom_call_target="tpu_custom_call" | custom-call | flops 1000000 | bytes 8388608 | tf_op jit(solution)/shard_map/edge_steps/pallas_call | solution.py:437
  86.8 0.0 collective-permute-done.2.far_late_ref
  86.8 0.0 collective-permute-done.5.back_ref
  86.8 11.9 %main_steps.1 = (f32[8,32768]{1,0:T(8,128)}, f32[8,32768]{1,0:T(8,128)}) custom-call(s32[1]{0:T(128)} %bitcast.here_ref, f32[3,8,24576]{2,1,0:T(8,128)S(1)} %get-tuple-element.27.stay_ref, f32[3,8,28672]{2,1,0:T(8,128)S(1)} %collective-permute-done.1.far_ref, ...), custom_call_target="tpu_custom_call", output_to_operand_aliasing={{0}: (9, {}), {1}: (10, {})} | custom-call | flops 1000000 | bytes 20971520 | tf_op jit(solution)/shard_map/main_steps/pallas_call | solution.py:450
Async XLA Ops:
  0.6 12.1 %copy-start.1 = (s32[16]{0:T(128)S(1)}, s32[16]{0:T(128)}, u32[]{:S(2)}) copy-start(s32[16]{0:T(128)} %slot_ref.3) | copy-start | bytes 196
  3.8 8.9 %collective-permute-start.3 = (f32[3,8,32768]{2,1,0:T(8,128)S(1)}, f32[3,8,32768]{2,1,0:T(8,128)S(1)}, u32[]{:S(2)}, u32[]{:S(2)}) collective-permute-start(f32[3,8,32768]{2,1,0:T(8,128)S(1)} %get-tuple-element.31), channel_id=1, source_target_pairs={{0,1},{1,0},{2,3},{3,2},{4,5},{5,4},{6,7},{7,6},{8,9},{9,8},{10,11... | collective-permute-start | bytes 9437192 | tf_op jit(solution)/shard_map/ppermute | solution.py:364
  3.9 12.8 %collective-permute-start = (f32[3,8,32768]{2,1,0:T(8,128)S(1)}, f32[3,8,32768]{2,1,0:T(8,128)S(1)}, u32[]{:S(2)}, u32[]{:S(2)}) collective-permute-start(f32[3,8,32768]{2,1,0:T(8,128)S(1)} %get-tuple-element.26), channel_id=1, source_target_pairs={{0,1},{1,0},{2,3},{3,2},{4,5},{5,4},{6,7},{7,6},{8,9},{9,8},{10,11... | collective-permute-start | bytes 9437192 | tf_op jit(solution)/shard_map/ppermute | solution.py:364
  4.4 53.1 %collective-permute-start.1 = (f32[3,8,28672]{2,1,0:T(8,128)S(1)}, f32[3,8,28672]{2,1,0:T(8,128)S(1)}, u32[]{:S(2)}, u32[]{:S(2)}) collective-permute-start(f32[3,8,28672]{2,1,0:T(8,128)S(1)} %get-tuple-element.28), channel_id=1, source_target_pairs={{1,3},{2,0},{3,5},{4,2},{5,7},{6,4},{7,9},{8,6},{9,11},{10,8},{11,... | collective-permute-start | bytes 8257544 | tf_op jit(solution)/shard_map/ppermute | solution.py:364
  14.7 26.6 %collective-permute-start.4 = (f32[3,8,8192]{2,1,0:T(8,128)S(1)}, f32[3,8,8192]{2,1,0:T(8,128)S(1)}, u32[]{:S(2)}, u32[]{:S(2)}) collective-permute-start(f32[3,8,8192]{2,1,0:T(8,128)S(1)} %get-tuple-element.33), channel_id=1, source_target_pairs={{0,2},{2,4},{3,1},{4,6},{5,3},{6,8},{7,5},{8,10},{9,7},{10,12},{11... | collective-permute-start | bytes 2359304 | tf_op jit(solution)/shard_map/ppermute | solution.py:364
  18.6 64.8 %copy-start = (s32[8,6]{1,0:T(8,128)S(1)}, s32[8,6]{1,0:T(8,128)}, u32[]{:S(2)}) copy-start(s32[8,6]{1,0:T(8,128)} %nbr_ref.3) | copy-start | bytes 580
  41.3 45.5 %collective-permute-start.5 = (f32[3,8,24576]{2,1,0:T(8,128)S(1)}, f32[3,8,24576]{2,1,0:T(8,128)S(1)}, u32[]{:S(2)}, u32[]{:S(2)}) collective-permute-start(f32[3,8,24576]{2,1,0:T(8,128)S(1)} %get-tuple-element.35), channel_id=1, source_target_pairs={{0,2},{2,4},{3,1},{4,6},{5,3},{6,8},{7,5},{8,10},{9,7},{10,12},{11... | collective-permute-start | bytes 7077896 | tf_op jit(solution)/shard_map/ppermute | solution.py:364
  57.5 29.3 %collective-permute-start.2 = (f32[3,8,4096]{2,1,0:T(8,128)S(1)}, f32[3,8,4096]{2,1,0:T(8,128)S(1)}, u32[]{:S(2)}, u32[]{:S(2)}) collective-permute-start(f32[3,8,4096]{2,1,0:T(8,128)S(1)} %get-tuple-element.30), channel_id=1, source_target_pairs={{1,3},{2,0},{3,5},{4,2},{5,7},{6,4},{7,9},{8,6},{9,11},{10,8},{11,... | collective-permute-start | bytes 1179656 | tf_op jit(solution)/shard_map/ppermute | solution.py:364
  66.2 15.5 %collective-permute-start.6 = (f32[3,8,3072]{2,1,0:T(8,128)S(1)}, f32[3,8,3072]{2,1,0:T(8,128)S(1)}, u32[]{:S(2)}, u32[]{:S(2)}) collective-permute-start(f32[3,8,3072]{2,1,0:T(8,128)S(1)} %get-tuple-element.37), channel_id=1, source_target_pairs={{0,1},{1,2},{2,3},{3,4},{4,5},{5,6},{6,7},{7,8},{8,9},{9,10},{10,1... | collective-permute-start | bytes 884744 | tf_op jit(solution)/shard_map/ppermute | solution.py:364
  68.2 15.3 %collective-permute-start.7 = (f32[3,8,3072]{2,1,0:T(8,128)S(1)}, f32[3,8,3072]{2,1,0:T(8,128)S(1)}, u32[]{:S(2)}, u32[]{:S(2)}) collective-permute-start(f32[3,8,3072]{2,1,0:T(8,128)S(1)} %get-tuple-element.38), channel_id=1, source_target_pairs={{1,0},{2,1},{3,2},{4,3},{5,4},{6,5},{7,6},{8,7},{9,8},{10,9},{11,1... | collective-permute-start | bytes 884744 | tf_op jit(solution)/shard_map/ppermute | solution.py:364

commit v6 on v5

--- a/solution.py
+++ b/solution.py
@@ -20,8 +20,6 @@
 LANES = 128
 EXT = EDGE + 2 * HALO
 REST = EDGE - 2 * CHUNK_PLANES
-AHEAD = 20
-FIRST_STEPS = 2 + AHEAD // CHUNK_PLANES
 VREGS = FACE // LANES
 
 time_step = 0.15
@@ -68,7 +66,7 @@
 
 def pack_kernel(
     here_ref, slot_hbm, phi_hbm, conc_hbm, mob_hbm,
-    phi_ref, conc_ref, mob_ref, merge_ref, final_ref, far_ref, late_ref,
+    phi_ref, conc_ref, mob_ref, merge_ref, final_ref, far_ref,
     slot_ref, slot_sem, sems,
 ):
     olds = tuple(zip((phi_hbm, conc_hbm, mob_hbm), (phi_ref, conc_ref, mob_ref)))
@@ -91,7 +89,7 @@
     amount, masks = windows(slot_ref, here)
     far, merge, final = masks(2 * side), masks(side), masks(-side)
 
-    def fill(i, out_ref, out_start):
+    def fill(i):
         start = chunk_at(i) * CHUNK
         for f, (_, ref) in enumerate(olds):
             for v in range(CHUNK // LANES):
@@ -99,19 +97,13 @@
                 rows = aligned(ref, lanes, amount)
                 merge_ref[f, :, lanes] = picked(merge, *rows)
                 final_ref[f, :, lanes] = picked(final, *rows)
-                out_ref[f, :, lanes_at(out_start, v)] = picked(far, *rows)
-
-    @pl.loop(0, FIRST_STEPS)
+                far_ref[f, :, lanes_at(i * CHUNK, v)] = picked(far, *rows)
+
+    @pl.loop(0, CHUNKS)
     def _(i):
         for copy in copies(i):
             copy.wait()
-        fill(i, far_ref, i * CHUNK)
-
-    @pl.loop(FIRST_STEPS, CHUNKS)
-    def _(i):
-        for copy in copies(i):
-            copy.wait()
-        fill(i, late_ref, (i - FIRST_STEPS) * CHUNK)
+        fill(i)
 
 
 def add_rows(masks, amount, old_refs, add_ref, edge_ref, rest_ref):
@@ -180,14 +172,11 @@
     def rows(x, index):
         return jnp.take_along_axis(x, index, axis=0, mode="promise_in_bounds")
 
-    def laplacian(self, ref, x):
-        centre = [ref[x, :, pl.ds(v * LANES, LANES)] for v in range(VREGS)]
+    def across_y(self, centre):
         lower = [pltpu.roll(c, EDGE, 1) for c in centre]
         upper = [pltpu.roll(c, LANES - EDGE, 1) for c in centre]
         out = []
-        for v in range(VREGS):
-            c = centre[v]
-            lanes = pl.ds(v * LANES, LANES)
+        for v, c in enumerate(centre):
             if v:
                 from_lower = lower[v - 1]
             else:
@@ -196,17 +185,33 @@
                 from_upper = upper[v + 1]
             else:
                 from_upper = jnp.where(self.has_above_y, self.rows(upper[0], self.above_y), c)
-            prev_y = jnp.where(self.y_first, from_lower, lower[v])
-            next_y = jnp.where(self.y_last, from_upper, upper[v])
-            prev_z = jnp.where(self.z_first, pltpu.roll(self.rows(c, self.below_z), LANES - EDGE + 1, 1), pltpu.roll(c, 1, 1))
-            next_z = jnp.where(self.z_last, pltpu.roll(self.rows(c, self.above_z), EDGE - 1, 1), pltpu.roll(c, LANES - 1, 1))
-            total = (ref[x - 1, :, lanes] + ref[x + 1, :, lanes]) + (prev_y + next_y) + (prev_z + next_z)
-            out.append(total - 6.0 * c)
-        return out, centre
+            out.append(jnp.where(self.y_first, from_lower, lower[v]) + jnp.where(self.y_last, from_upper, upper[v]))
+        return out
+
+    def across_z(self, phi, conc):
+        phi_prev, conc_prev = pltpu.roll(phi, 1, 1), pltpu.roll(conc, 1, 1)
+        phi_next, conc_next = pltpu.roll(phi, LANES - 1, 1), pltpu.roll(conc, LANES - 1, 1)
+        below = self.rows(jnp.where(self.z_first, conc_prev, phi), self.below_z)
+        above = self.rows(jnp.where(self.z_last, conc_next, phi), self.above_z)
+        phi_prev = jnp.where(self.z_first, pltpu.roll(below, LANES - EDGE + 1, 1), phi_prev)
+        conc_prev = jnp.where(self.z_first, pltpu.roll(below, LANES - EDGE, 1), conc_prev)
+        phi_next = jnp.where(self.z_last, pltpu.roll(above, EDGE - 1, 1), phi_next)
+        conc_next = jnp.where(self.z_last, pltpu.roll(above, EDGE, 1), conc_next)
+        return phi_prev + phi_next, conc_prev + conc_next
 
     def advance(self, phi_ref, conc_ref, mob_ref, x, store):
-        lapl_phi, phis = self.laplacian(phi_ref, x)
-        lapl_conc, concs = self.laplacian(conc_ref, x)
+        lanes = [pl.ds(v * LANES, LANES) for v in range(VREGS)]
+        phis, concs = ([ref[x, :, part] for part in lanes] for ref in (phi_ref, conc_ref))
+        phi_y, conc_y = self.across_y(phis), self.across_y(concs)
+        lapl_phi, lapl_conc = [], []
+        for v in range(VREGS):
+            phi_z, conc_z = self.across_z(phis[v], concs[v])
+            for out, ref, c, in_y, in_z in (
+                (lapl_phi, phi_ref, phis[v], phi_y[v], phi_z),
+                (lapl_conc, conc_ref, concs[v], conc_y[v], conc_z),
+            ):
+                total = (ref[x - 1, :, lanes[v]] + ref[x + 1, :, lanes[v]]) + in_y + in_z
+                out.append(total - 6.0 * c)
         for v in range(VREGS):
             phi, conc = phis[v], concs[v]
             square = phi * phi
@@ -302,7 +307,7 @@
 
 
 def main_kernel(
-    here_ref, stay_ref, far_ref, far_late_ref, back_ref, nbr_ref, kept0_ref, kept1_ref, kept2_ref, _phase_in, _solute_in,
+    here_ref, stay_ref, far_ref, back_ref, nbr_ref, kept0_ref, kept1_ref, kept2_ref, _phase_in, _solute_in,
     phase_hbm, solute_hbm,
     phi0, conc0, mob, phi1, conc1, phi2, conc2, phase_ref, solute_ref, sems,
 ):
@@ -318,8 +323,7 @@
     for f, ref in enumerate((phi2, conc2)):
         for n, x in enumerate((first - 4, first - 3, last + 2, last + 3)):
             ref[x] = kept2_ref[f, n]
-    place(states, AHEAD, first, (stay_ref, 0), (far_ref, 2 * CHUNK_PLANES), (back_ref, 0))
-    place(states, REST - AHEAD, first + AHEAD, (stay_ref, AHEAD), (far_late_ref, 0), (back_ref, AHEAD))
+    place(states, REST, first, (stay_ref, 0), (far_ref, 2 * CHUNK_PLANES), (back_ref, 0))
     st.sweep(first - 1, last + 1, 5, (phi0, conc0), mob, (phi1, conc1))
     st.sweep(first - 2, last + 2, 4, (phi1, conc1), mob, (phi2, conc2))
     start = first - 3
@@ -375,17 +379,17 @@
 
     slots_hbm = pltpu.with_memory_space_constraint(new_global_slot, pltpu.HBM)
     old_shape = jax.ShapeDtypeStruct((OLD, CELLS), jnp.float32)
-    *olds, merge, final, far_first, far_late = pl.pallas_call(
+    *olds, merge, final, far_all = pl.pallas_call(
         pack_kernel,
         in_specs=[SMEM, HBM, HBM, HBM, HBM],
-        out_specs=[VMEM] * 7,
-        out_shape=[old_shape] * 3 + [shaped(EDGE)] * 2 + [shaped(2 * CHUNK_PLANES + AHEAD), shaped(REST - AHEAD)],
+        out_specs=[VMEM] * 6,
+        out_shape=[old_shape] * 3 + [shaped(EDGE)] * 3,
         scratch_shapes=[pltpu.SMEM((OLD,), jnp.int32), pltpu.SemaphoreType.DMA, pltpu.SemaphoreType.DMA((CHUNKS, FIELDS))],
         compiler_params=PARAMS,
         cost_estimate=cost(6 * MB),
         name="pack",
     )(here, slots_hbm, *olds)
-    far_first_got = sent(far_first, far_route)
+    far_got = sent(far_all, far_route)
     merge_got = sent(merge, partner)
     final_got = sent(final, partner)
 
@@ -411,7 +415,6 @@
         name="stay",
     )(here, new_global_slot, *olds, final_got)
     back_rest_got = sent(after(back_rest, back_edge_got, stay_edge), back_route)
-    far_late_got = sent(after(far_late, far_first_got), far_route)
 
     edges = pl.BlockSpec((FIELDS, CAP, 2 * CHUNK), lambda i: (0, 0, 0))
     faces = pl.BlockSpec((FIELDS, CAP, HALO * FACE), lambda i: (0, 0, 0))
@@ -424,7 +427,7 @@
         compiler_params=PARAMS,
         cost_estimate=cost(3 * MB),
         name="faces",
-    )(stay_edge, far_first_got, back_edge_got)
+    )(stay_edge, far_got, back_edge_got)
     below = sent(high, [(p, p + 1) for p in devices])
     above = sent(low, [(p, p - 1) for p in devices])
 
@@ -449,15 +452,15 @@
     rows_out = pltpu.VMEM((CAP, OUT_PLANES * FACE), jnp.float32)
     phase, solute = pl.pallas_call(
         main_kernel,
-        in_specs=[SMEM] + [VMEM] * 8 + [HBM] * 2,
+        in_specs=[SMEM] + [VMEM] * 7 + [HBM] * 2,
         out_specs=[HBM] * 2,
         out_shape=[whole, whole],
         scratch_shapes=[state] * 7 + [rows_out] * 2 + [pltpu.SemaphoreType.DMA((PIECES, 2))],
-        input_output_aliases={9: 0, 10: 1},
+        input_output_aliases={8: 0, 9: 1},
         compiler_params=PARAMS,
         cost_estimate=cost(20 * MB),
         name="main_steps",
-    )(here, stay_rest, far_first_got, far_late_got, back_rest_got, neighbors, kept0, kept1, kept2, phase, solute)
+    )(here, stay_rest, far_got, back_rest_got, neighbors, kept0, kept1, kept2, phase, solute)
     return phase, solute
 
 

time: 99.2 us -> 141 us (1.42)
  Pallas kernels: 22.5 us -> 64.1 us
  starting transfers between devices: 31.1 us -> 22.6 us
  waiting for transfers between devices: 44.4 us -> 52.5 us
    pallas_call x1, Pallas kernels: 11.9 us -> 45.2 us  [on_device(): pl.pallas_call(main_kernel, in_specs=[SMEM] + [VMEM] * 7 + [HBM] * 2, out...]
    ppermute x8 -> x7, starting transfers between devices: 31.1 us -> 22.6 us  [sent(): lax.ppermute(block, 'blk', [(p, q) for p, q in route if 0 <= q < count])]
    pallas_call x1, Pallas kernels: 3.32 us -> 11.6 us  [on_device(): pl.pallas_call(edge_kernel, in_specs=[SMEM] + [VMEM] * 4, out_specs=[VMEM...]
    ppermute x8 -> x7, waiting for transfers between devices: 44.4 us -> 52.5 us  [sent(): lax.ppermute(block, 'blk', [(p, q) for p, q in route if 0 <= q < count])]
  transfers between devices with their start and end apart: 8 -> 7, of which waited for: 4 -> 4; matrix products, arithmetic and copies ran while one was open for 0% -> 0% of each run, Pallas kernels for 8% -> 11%
where the time goes in v6:
time: 141 us; the launch traced here: 140 us
  Pallas kernels  64.1 us (45%)
  waiting for transfers between devices  52.5 us (37%)
  starting transfers between devices  22.6 us (16%)
    ppermute x7, waiting for transfers between devices, sent(): lax.ppermute(block, 'blk', [(p, q) for p, q in route if 0 <= q < count])  52.5 us
    pallas_call x1, Pallas kernels, on_device(): pl.pallas_call(main_kernel, in_specs=[SMEM] + [VMEM] * 7 + [HBM] * 2, out...  45.2 us
    ppermute x7, starting transfers between devices, sent(): lax.ppermute(block, 'blk', [(p, q) for p, q in route if 0 <= q < count])  22.6 us
    pallas_call x1, Pallas kernels, on_device(): pl.pallas_call(edge_kernel, in_specs=[SMEM] + [VMEM] * 4, out_specs=[VMEM...  11.6 us
    pallas_call x1, Pallas kernels, on_device(): pl.pallas_call(pack_kernel, in_specs=[SMEM, HBM, HBM, HBM, HBM], out_spec...  3.19 us
  transfers between devices with their start and end apart: 7, of which 4 were waited for; matrix products, arithmetic and copies ran while one was open for 0% of the time, Pallas kernels for 11%

profile of v6, /device:TPU:24, one launch (start us, length us, event | category | flops | bytes accessed | tf_op | source)
XLA Modules:
  0.0 140.0 jit_solution(13441833875144268854)
XLA Ops:
  0.6 0.0 copy-start.1
  0.6 3.2 %pack.1 = (f32[16,32768]{1,0:T(8,128)S(1)}, f32[16,32768]{1,0:T(8,128)S(1)}, f32[16,32768]{1,0:T(8,128)S(1)}, f32[3,8,32768]{2,1,0:T(8,128)S(1)}, f32[3,8,32768]...) custom-call(s32[1]{0:T(128)} %bitcast.here_ref, s32[16]{0:T(128)} %slot_ref.3, f32[16,32768]{1,0:T(8,128)} %phi_hbm.1, ...), custom_call_target="tpu_custom_call" | custom-call | flops 1000000 | bytes 6291456 | tf_op jit(solution)/shard_map/pack/pallas_call | solution.py:382
  3.8 0.1 collective-permute-start.2
  3.9 0.5 collective-permute-start
  4.4 8.3 %collective-permute-start.1 = (f32[3,8,32768]{2,1,0:T(8,128)S(1)}, f32[3,8,32768]{2,1,0:T(8,128)S(1)}, u32[]{:S(2)}, u32[]{:S(2)}) collective-permute-start(f32[3,8,32768]{2,1,0:T(8,128)S(1)} %get-tuple-element.26), channel_id=1, source_target_pairs={{1,3},{2,0},{3,5},{4,2},{5,7},{6,4},{7,9},{8,6},{9,11},{10,8},{11,... | collective-permute-start | bytes 9437192 | tf_op jit(solution)/shard_map/ppermute | solution.py:368
  12.8 0.0 collective-permute-done.2.merge_ref
  12.8 0.0 copy-done.1
  12.8 2.0 %relay.1 = (f32[3,8,8192]{2,1,0:T(8,128)S(1)}, f32[3,8,24576]{2,1,0:T(8,128)S(1)}) custom-call(s32[1]{0:T(128)} %bitcast.here_ref, s32[16]{0:T(128)S(1)} %copy-done.1, f32[16,32768]{1,0:T(8,128)S(1)} %get-tuple-element.21.phi_ref, f32[16,32768]{1,0:T(8,128)S(1)} %get-tuple-element.22.conc_ref, f32[16,32768]{1,0:T(8,128)S(1)} %get-tuple-element.23.mob_ref, ...), custom_call_target="tpu_custom_call" | custom-call | flops 1000000 | bytes 6291456 | tf_op jit(solution)/shard_map/relay/pallas_call | solution.py:397
  14.8 1.9 %collective-permute-start.3 = (f32[3,8,8192]{2,1,0:T(8,128)S(1)}, f32[3,8,8192]{2,1,0:T(8,128)S(1)}, u32[]{:S(2)}, u32[]{:S(2)}) collective-permute-start(f32[3,8,8192]{2,1,0:T(8,128)S(1)} %get-tuple-element.29), channel_id=1, source_target_pairs={{0,2},{2,4},{3,1},{4,6},{5,3},{6,8},{7,5},{8,10},{9,7},{10,12},{11... | collective-permute-start | bytes 2359304 | tf_op jit(solution)/shard_map/ppermute | solution.py:368
  16.7 0.0 collective-permute-done.final_ref
  16.7 2.0 %stay.1 = (f32[3,8,8192]{2,1,0:T(8,128)S(1)}, f32[3,8,24576]{2,1,0:T(8,128)S(1)}) custom-call(s32[1]{0:T(128)} %bitcast.here_ref, s32[16]{0:T(128)S(1)} %copy-done.1, f32[16,32768]{1,0:T(8,128)S(1)} %get-tuple-element.21.phi_ref, f32[16,32768]{1,0:T(8,128)S(1)} %get-tuple-element.22.conc_ref, f32[16,32768]{1,0:T(8,128)S(1)} %get-tuple-element.23.mob_ref, ...), custom_call_target="tpu_custom_call" | custom-call | flops 1000000 | bytes 6291456 | tf_op jit(solution)/shard_map/stay/pallas_call | solution.py:408
  18.7 22.7 %collective-permute-done.3.back_ref = f32[3,8,8192]{2,1,0:T(8,128)S(1)} collective-permute-done((f32[3,8,8192]{2,1,0:T(8,128)S(1)}, f32[3,8,8192]{2,1,0:T(8,128)S(1)}, u32[]{:S(2)}, u32[]{:S(2)}) %collective-permute-start.3) | collective-permute-done | bytes 786464 | tf_op jit(solution)/shard_map/ppermute | solution.py:368
  41.4 0.0 copy-start
  41.4 2.0 %collective-permute-start.4 = (f32[3,8,24576]{2,1,0:T(8,128)S(1)}, f32[3,8,24576]{2,1,0:T(8,128)S(1)}, u32[]{:S(2)}, u32[]{:S(2)}) collective-permute-start(f32[3,8,24576]{2,1,0:T(8,128)S(1)} %get-tuple-element.31), channel_id=1, source_target_pairs={{0,2},{2,4},{3,1},{4,6},{5,3},{6,8},{7,5},{8,10},{9,7},{10,12},{11... | collective-permute-start | bytes 7077896 | tf_op jit(solution)/shard_map/ppermute | solution.py:368
  43.4 22.4 %collective-permute-done.1.far_ref = f32[3,8,32768]{2,1,0:T(8,128)S(1)} collective-permute-done((f32[3,8,32768]{2,1,0:T(8,128)S(1)}, f32[3,8,32768]{2,1,0:T(8,128)S(1)}, u32[]{:S(2)}, u32[]{:S(2)}) %collective-permute-start.1) | collective-permute-done | bytes 3145760 | tf_op jit(solution)/shard_map/ppermute | solution.py:368
  65.8 0.2 faces.1
  66.0 1.9 %collective-permute-start.5 = (f32[3,8,3072]{2,1,0:T(8,128)S(1)}, f32[3,8,3072]{2,1,0:T(8,128)S(1)}, u32[]{:S(2)}, u32[]{:S(2)}) collective-permute-start(f32[3,8,3072]{2,1,0:T(8,128)S(1)} %get-tuple-element.33), channel_id=1, source_target_pairs={{0,1},{1,2},{2,3},{3,4},{4,5},{5,6},{6,7},{7,8},{8,9},{9,10},{10,1... | collective-permute-start | bytes 884744 | tf_op jit(solution)/shard_map/ppermute | solution.py:368
  67.9 7.9 %collective-permute-start.6 = (f32[3,8,3072]{2,1,0:T(8,128)S(1)}, f32[3,8,3072]{2,1,0:T(8,128)S(1)}, u32[]{:S(2)}, u32[]{:S(2)}) collective-permute-start(f32[3,8,3072]{2,1,0:T(8,128)S(1)} %get-tuple-element.34), channel_id=1, source_target_pairs={{1,0},{2,1},{3,2},{4,3},{5,4},{6,5},{7,6},{8,7},{9,8},{10,9},{11,1... | collective-permute-start | bytes 884744 | tf_op jit(solution)/shard_map/ppermute | solution.py:368
  75.8 5.7 %collective-permute-done.5.below_ref = f32[3,8,3072]{2,1,0:T(8,128)S(1)} collective-permute-done((f32[3,8,3072]{2,1,0:T(8,128)S(1)}, f32[3,8,3072]{2,1,0:T(8,128)S(1)}, u32[]{:S(2)}, u32[]{:S(2)}) %collective-permute-start.5) | collective-permute-done | bytes 294944 | tf_op jit(solution)/shard_map/ppermute | solution.py:368
  81.5 1.8 %collective-permute-done.6.above_ref = f32[3,8,3072]{2,1,0:T(8,128)S(1)} collective-permute-done((f32[3,8,3072]{2,1,0:T(8,128)S(1)}, f32[3,8,3072]{2,1,0:T(8,128)S(1)}, u32[]{:S(2)}, u32[]{:S(2)}) %collective-permute-start.6) | collective-permute-done | bytes 294944 | tf_op jit(solution)/shard_map/ppermute | solution.py:368
  83.2 0.0 copy-done
  83.2 11.6 %edge_steps.1 = (f32[8,32768]{1,0:T(8,128)}, f32[8,32768]{1,0:T(8,128)}, f32[3,6,8,1024]{3,2,1,0:T(8,128)S(1)}, f32[2,4,8,1024]{3,2,1,0:T(8,128)S(1)}, f32[2,4,8,1024]{3,2,1,0:T(8,128)S(1)}) custom-call(s32[1]{0:T(128)} %bitcast.here_ref, f32[3,8,8192]{2,1,0:T(8,128)S(1)} %get-tuple-element.32.edge_ref, f32[3,8,3072]{2,1,0:T(8,128)S(1)} %collective-permute-done.5.below_ref, ...), custom_call_target="tpu_custom_call" | custom-call | flops 1000000 | bytes 8388608 | tf_op jit(solution)/shard_map/edge_steps/pallas_call | solution.py:440
  94.9 0.0 collective-permute-done.4.back_ref
  94.9 45.2 %main_steps.1 = (f32[8,32768]{1,0:T(8,128)}, f32[8,32768]{1,0:T(8,128)}) custom-call(s32[1]{0:T(128)} %bitcast.here_ref, f32[3,8,24576]{2,1,0:T(8,128)S(1)} %get-tuple-element.25.stay_ref, f32[3,8,32768]{2,1,0:T(8,128)S(1)} %collective-permute-done.1.far_ref, ...), custom_call_target="tpu_custom_call", output_to_operand_aliasing={{0}: (8, {}), {1}: (9, {})} | custom-call | flops 1000000 | bytes 20971520 | tf_op jit(solution)/shard_map/main_steps/pallas_call | solution.py:453
Async XLA Ops:
  0.6 12.1 %copy-start.1 = (s32[16]{0:T(128)S(1)}, s32[16]{0:T(128)}, u32[]{:S(2)}) copy-start(s32[16]{0:T(128)} %slot_ref.3) | copy-start | bytes 196
  3.8 8.9 %collective-permute-start.2 = (f32[3,8,32768]{2,1,0:T(8,128)S(1)}, f32[3,8,32768]{2,1,0:T(8,128)S(1)}, u32[]{:S(2)}, u32[]{:S(2)}) collective-permute-start(f32[3,8,32768]{2,1,0:T(8,128)S(1)} %get-tuple-element.27), channel_id=1, source_target_pairs={{0,1},{1,0},{2,3},{3,2},{4,5},{5,4},{6,7},{7,6},{8,9},{9,8},{10,11... | collective-permute-start | bytes 9437192 | tf_op jit(solution)/shard_map/ppermute | solution.py:368
  3.9 12.8 %collective-permute-start = (f32[3,8,32768]{2,1,0:T(8,128)S(1)}, f32[3,8,32768]{2,1,0:T(8,128)S(1)}, u32[]{:S(2)}, u32[]{:S(2)}) collective-permute-start(f32[3,8,32768]{2,1,0:T(8,128)S(1)} %get-tuple-element.24), channel_id=1, source_target_pairs={{0,1},{1,0},{2,3},{3,2},{4,5},{5,4},{6,7},{7,6},{8,9},{9,8},{10,11... | collective-permute-start | bytes 9437192 | tf_op jit(solution)/shard_map/ppermute | solution.py:368
  4.4 61.4 %collective-permute-start.1 = (f32[3,8,32768]{2,1,0:T(8,128)S(1)}, f32[3,8,32768]{2,1,0:T(8,128)S(1)}, u32[]{:S(2)}, u32[]{:S(2)}) collective-permute-start(f32[3,8,32768]{2,1,0:T(8,128)S(1)} %get-tuple-element.26), channel_id=1, source_target_pairs={{1,3},{2,0},{3,5},{4,2},{5,7},{6,4},{7,9},{8,6},{9,11},{10,8},{11,... | collective-permute-start | bytes 9437192 | tf_op jit(solution)/shard_map/ppermute | solution.py:368
  14.8 26.6 %collective-permute-start.3 = (f32[3,8,8192]{2,1,0:T(8,128)S(1)}, f32[3,8,8192]{2,1,0:T(8,128)S(1)}, u32[]{:S(2)}, u32[]{:S(2)}) collective-permute-start(f32[3,8,8192]{2,1,0:T(8,128)S(1)} %get-tuple-element.29), channel_id=1, source_target_pairs={{0,2},{2,4},{3,1},{4,6},{5,3},{6,8},{7,5},{8,10},{9,7},{10,12},{11... | collective-permute-start | bytes 2359304 | tf_op jit(solution)/shard_map/ppermute | solution.py:368
  41.4 41.9 %copy-start = (s32[8,6]{1,0:T(8,128)S(1)}, s32[8,6]{1,0:T(8,128)}, u32[]{:S(2)}) copy-start(s32[8,6]{1,0:T(8,128)} %nbr_ref.3) | copy-start | bytes 580
  41.4 53.5 %collective-permute-start.4 = (f32[3,8,24576]{2,1,0:T(8,128)S(1)}, f32[3,8,24576]{2,1,0:T(8,128)S(1)}, u32[]{:S(2)}, u32[]{:S(2)}) collective-permute-start(f32[3,8,24576]{2,1,0:T(8,128)S(1)} %get-tuple-element.31), channel_id=1, source_target_pairs={{0,2},{2,4},{3,1},{4,6},{5,3},{6,8},{7,5},{8,10},{9,7},{10,12},{11... | collective-permute-start | bytes 7077896 | tf_op jit(solution)/shard_map/ppermute | solution.py:368
  66.0 15.5 %collective-permute-start.5 = (f32[3,8,3072]{2,1,0:T(8,128)S(1)}, f32[3,8,3072]{2,1,0:T(8,128)S(1)}, u32[]{:S(2)}, u32[]{:S(2)}) collective-permute-start(f32[3,8,3072]{2,1,0:T(8,128)S(1)} %get-tuple-element.33), channel_id=1, source_target_pairs={{0,1},{1,2},{2,3},{3,4},{4,5},{5,6},{6,7},{7,8},{8,9},{9,10},{10,1... | collective-permute-start | bytes 884744 | tf_op jit(solution)/shard_map/ppermute | solution.py:368
  67.9 15.3 %collective-permute-start.6 = (f32[3,8,3072]{2,1,0:T(8,128)S(1)}, f32[3,8,3072]{2,1,0:T(8,128)S(1)}, u32[]{:S(2)}, u32[]{:S(2)}) collective-permute-start(f32[3,8,3072]{2,1,0:T(8,128)S(1)} %get-tuple-element.34), channel_id=1, source_target_pairs={{1,0},{2,1},{3,2},{4,3},{5,4},{6,5},{7,6},{8,7},{9,8},{10,9},{11,1... | collective-permute-start | bytes 884744 | tf_op jit(solution)/shard_map/ppermute | solution.py:368

commit v7 on v5

--- a/solution.py
+++ b/solution.py
@@ -297,7 +297,7 @@
 MAIN_PLANES = TOP_AT + 4 - BACK
 OUT_FIRST = REST_AT - 3
 OUT_PLANES = TOP_AT + 3 - OUT_FIRST
-PIECE = 6
+PIECE = 10
 PIECES = OUT_PLANES // PIECE
 
 
@@ -320,8 +320,8 @@
             ref[x] = kept2_ref[f, n]
     place(states, AHEAD, first, (stay_ref, 0), (far_ref, 2 * CHUNK_PLANES), (back_ref, 0))
     place(states, REST - AHEAD, first + AHEAD, (stay_ref, AHEAD), (far_late_ref, 0), (back_ref, AHEAD))
-    st.sweep(first - 1, last + 1, 5, (phi0, conc0), mob, (phi1, conc1))
-    st.sweep(first - 2, last + 2, 4, (phi1, conc1), mob, (phi2, conc2))
+    st.sweep(first - 1, last + 1, REST + 2, (phi0, conc0), mob, (phi1, conc1))
+    st.sweep(first - 2, last + 2, REST + 4, (phi1, conc1), mob, (phi2, conc2))
     start = first - 3
     copies = []
     for piece in range(PIECES):
@@ -411,7 +411,6 @@
         name="stay",
     )(here, new_global_slot, *olds, final_got)
     back_rest_got = sent(after(back_rest, back_edge_got, stay_edge), back_route)
-    far_late_got = sent(after(far_late, far_first_got), far_route)
 
     edges = pl.BlockSpec((FIELDS, CAP, 2 * CHUNK), lambda i: (0, 0, 0))
     faces = pl.BlockSpec((FIELDS, CAP, HALO * FACE), lambda i: (0, 0, 0))
@@ -427,6 +426,7 @@
     )(stay_edge, far_first_got, back_edge_got)
     below = sent(high, [(p, p + 1) for p in devices])
     above = sent(low, [(p, p - 1) for p in devices])
+    far_late_got = sent(after(far_late, below, above), far_route)
 
     state = pltpu.VMEM((EXT, CAP, FACE), jnp.float32)
     whole = jax.ShapeDtypeStruct((CAP, CELLS), jnp.float32)

time: 99.2 us -> 99.8 us (level)
  the two profiles are of different devices: /device:TPU:24 before, /device:TPU:25 now
where the time goes in v7:
time: 99.8 us; the launch traced here: 99.5 us
  waiting for transfers between devices  42.9 us (43%)
  starting transfers between devices  34.1 us (34%)
  Pallas kernels  21.6 us (22%)
    ppermute x8, waiting for transfers between devices, sent(): lax.ppermute(block, 'blk', [(p, q) for p, q in route if 0 <= q < count])  42.9 us
    ppermute x8, starting transfers between devices, sent(): lax.ppermute(block, 'blk', [(p, q) for p, q in route if 0 <= q < count])  34.1 us
    pallas_call x1, Pallas kernels, on_device(): pl.pallas_call(main_kernel, in_specs=[SMEM] + [VMEM] * 8 + [HBM] * 2, out...  11 us
    pallas_call x1, Pallas kernels, on_device(): pl.pallas_call(edge_kernel, in_specs=[SMEM] + [VMEM] * 4, out_specs=[VMEM...  3.32 us
    pallas_call x1, Pallas kernels, on_device(): pl.pallas_call(pack_kernel, in_specs=[SMEM, HBM, HBM, HBM, HBM], out_spec...  3.11 us
  transfers between devices with their start and end apart: 8, of which 6 were waited for; matrix products, arithmetic and copies ran while one was open for 0% of the time, Pallas kernels for 7%

profile of v7, /device:TPU:25, one launch (start us, length us, event | category | flops | bytes accessed | tf_op | source)
XLA Modules:
  0.0 99.5 jit_solution(10316944788369394907)
XLA Ops:
  0.6 0.0 copy-start.1
  0.6 3.1 %pack.1 = (f32[16,32768]{1,0:T(8,128)S(1)}, f32[16,32768]{1,0:T(8,128)S(1)}, f32[16,32768]{1,0:T(8,128)S(1)}, f32[3,8,32768]{2,1,0:T(8,128)S(1)}, f32[3,8,32768]...) custom-call(s32[1]{0:T(128)} %bitcast.here_ref, s32[16]{0:T(128)} %slot_ref.3, ...), custom_call_target="tpu_custom_call" | custom-call | flops 1000000 | bytes 6291456 | tf_op jit(solution)/shard_map/pack/pallas_call | solution.py:378
  3.8 0.8 collective-permute-start.2
  4.5 0.1 collective-permute-start
  4.6 3.5 %collective-permute-start.1 = (f32[3,8,28672]{2,1,0:T(8,128)S(1)}, f32[3,8,28672]{2,1,0:T(8,128)S(1)}, u32[]{:S(2)}, u32[]{:S(2)}) collective-permute-start(f32[3,8,28672]{2,1,0:T(8,128)S(1)} %get-tuple-element.28), channel_id=1, source_target_pairs={{1,3},{2,0},{3,5},{4,2},{5,7},{6,4},{7,9},{8,6},{9,11},{10,8},{11,... | collective-permute-start | bytes 8257544 | tf_op jit(solution)/shard_map/ppermute | solution.py:364
  8.2 1.7 %collective-permute-done.2.merge_ref = f32[3,8,32768]{2,1,0:T(8,128)S(1)} collective-permute-done((f32[3,8,32768]{2,1,0:T(8,128)S(1)}, f32[3,8,32768]{2,1,0:T(8,128)S(1)}, u32[]{:S(2)}, u32[]{:S(2)}) %collective-permute-start.2) | collective-permute-done | bytes 3145760 | tf_op jit(solution)/shard_map/ppermute | solution.py:364
  9.8 0.0 copy-done.1
  9.8 2.0 %relay.1 = (f32[3,8,8192]{2,1,0:T(8,128)S(1)}, f32[3,8,24576]{2,1,0:T(8,128)S(1)}) custom-call(s32[1]{0:T(128)} %bitcast.here_ref, s32[16]{0:T(128)S(1)} %copy-done.1, f32[16,32768]{1,0:T(8,128)S(1)} %get-tuple-element.23.phi_ref, f32[16,32768]{1,0:T(8,128)S(1)} %get-tuple-element.24.conc_ref, f32[16,32768]{1,0:T(8,128)S(1)} %get-tuple-element.25.mob_ref, ...), custom_call_target="tpu_custom_call" | custom-call | flops 1000000 | bytes 6291456 | tf_op jit(solution)/shard_map/relay/pallas_call | solution.py:393
  11.8 8.0 %collective-permute-start.3 = (f32[3,8,8192]{2,1,0:T(8,128)S(1)}, f32[3,8,8192]{2,1,0:T(8,128)S(1)}, u32[]{:S(2)}, u32[]{:S(2)}) collective-permute-start(f32[3,8,8192]{2,1,0:T(8,128)S(1)} %get-tuple-element.32), channel_id=1, source_target_pairs={{0,2},{2,4},{3,1},{4,6},{5,3},{6,8},{7,5},{8,10},{9,7},{10,12},{11... | collective-permute-start | bytes 2359304 | tf_op jit(solution)/shard_map/ppermute | solution.py:364
  19.9 0.0 collective-permute-done.final_ref
  19.9 2.0 %stay.1 = (f32[3,8,8192]{2,1,0:T(8,128)S(1)}, f32[3,8,24576]{2,1,0:T(8,128)S(1)}) custom-call(s32[1]{0:T(128)} %bitcast.here_ref, s32[16]{0:T(128)S(1)} %copy-done.1, f32[16,32768]{1,0:T(8,128)S(1)} %get-tuple-element.23.phi_ref, f32[16,32768]{1,0:T(8,128)S(1)} %get-tuple-element.24.conc_ref, f32[16,32768]{1,0:T(8,128)S(1)} %get-tuple-element.25.mob_ref, ...), custom_call_target="tpu_custom_call" | custom-call | flops 1000000 | bytes 6291456 | tf_op jit(solution)/shard_map/stay/pallas_call | solution.py:404
  21.9 0.0 copy-start
  21.9 15.4 %collective-permute-done.3.back_ref = f32[3,8,8192]{2,1,0:T(8,128)S(1)} collective-permute-done((f32[3,8,8192]{2,1,0:T(8,128)S(1)}, f32[3,8,8192]{2,1,0:T(8,128)S(1)}, u32[]{:S(2)}, u32[]{:S(2)}) %collective-permute-start.3) | collective-permute-done | bytes 786464 | tf_op jit(solution)/shard_map/ppermute | solution.py:364
  37.3 8.3 %collective-permute-start.7 = (f32[3,8,24576]{2,1,0:T(8,128)S(1)}, f32[3,8,24576]{2,1,0:T(8,128)S(1)}, u32[]{:S(2)}, u32[]{:S(2)}) collective-permute-start(f32[3,8,24576]{2,1,0:T(8,128)S(1)} %get-tuple-element.37), channel_id=1, source_target_pairs={{0,2},{2,4},{3,1},{4,6},{5,3},{6,8},{7,5},{8,10},{9,7},{10,12},{11... | collective-permute-start | bytes 7077896 | tf_op jit(solution)/shard_map/ppermute | solution.py:364
  45.6 6.7 %collective-permute-done.1.far_ref = f32[3,8,28672]{2,1,0:T(8,128)S(1)} collective-permute-done((f32[3,8,28672]{2,1,0:T(8,128)S(1)}, f32[3,8,28672]{2,1,0:T(8,128)S(1)}, u32[]{:S(2)}, u32[]{:S(2)}) %collective-permute-start.1) | collective-permute-done | bytes 2752544 | tf_op jit(solution)/shard_map/ppermute | solution.py:364
  52.3 0.2 faces.1
  52.5 9.4 %collective-permute-start.4 = (f32[3,8,3072]{2,1,0:T(8,128)S(1)}, f32[3,8,3072]{2,1,0:T(8,128)S(1)}, u32[]{:S(2)}, u32[]{:S(2)}) collective-permute-start(f32[3,8,3072]{2,1,0:T(8,128)S(1)} %get-tuple-element.33), channel_id=1, source_target_pairs={{0,1},{1,2},{2,3},{3,4},{4,5},{5,6},{6,7},{7,8},{8,9},{9,10},{10,1... | collective-permute-start | bytes 884744 | tf_op jit(solution)/shard_map/ppermute | solution.py:364
  61.8 1.9 %collective-permute-start.5 = (f32[3,8,3072]{2,1,0:T(8,128)S(1)}, f32[3,8,3072]{2,1,0:T(8,128)S(1)}, u32[]{:S(2)}, u32[]{:S(2)}) collective-permute-start(f32[3,8,3072]{2,1,0:T(8,128)S(1)} %get-tuple-element.34), channel_id=1, source_target_pairs={{1,0},{2,1},{3,2},{4,3},{5,4},{6,5},{7,6},{8,7},{9,8},{10,9},{11,1... | collective-permute-start | bytes 884744 | tf_op jit(solution)/shard_map/ppermute | solution.py:364
  63.8 4.9 %collective-permute-done.4.below_ref = f32[3,8,3072]{2,1,0:T(8,128)S(1)} collective-permute-done((f32[3,8,3072]{2,1,0:T(8,128)S(1)}, f32[3,8,3072]{2,1,0:T(8,128)S(1)}, u32[]{:S(2)}, u32[]{:S(2)}) %collective-permute-start.4) | collective-permute-done | bytes 294944 | tf_op jit(solution)/shard_map/ppermute | solution.py:364
  68.7 4.7 %collective-permute-done.5.above_ref = f32[3,8,3072]{2,1,0:T(8,128)S(1)} collective-permute-done((f32[3,8,3072]{2,1,0:T(8,128)S(1)}, f32[3,8,3072]{2,1,0:T(8,128)S(1)}, u32[]{:S(2)}, u32[]{:S(2)}) %collective-permute-start.5) | collective-permute-done | bytes 294944 | tf_op jit(solution)/shard_map/ppermute | solution.py:364
  73.4 2.1 %collective-permute-start.6 = (f32[3,8,4096]{2,1,0:T(8,128)S(1)}, f32[3,8,4096]{2,1,0:T(8,128)S(1)}, u32[]{:S(2)}, u32[]{:S(2)}) collective-permute-start(f32[3,8,4096]{2,1,0:T(8,128)S(1)} %get-tuple-element.35), channel_id=1, source_target_pairs={{1,3},{2,0},{3,5},{4,2},{5,7},{6,4},{7,9},{8,6},{9,11},{10,8},{11,... | collective-permute-start | bytes 1179656 | tf_op jit(solution)/shard_map/ppermute | solution.py:364
  75.5 0.0 copy-done
  75.5 3.3 %edge_steps.1 = (f32[8,32768]{1,0:T(8,128)}, f32[8,32768]{1,0:T(8,128)}, f32[3,6,8,1024]{3,2,1,0:T(8,128)S(1)}, f32[2,4,8,1024]{3,2,1,0:T(8,128)S(1)}, f32[2,4,8,1024]{3,2,1,0:T(8,128)S(1)}) custom-call(s32[1]{0:T(128)} %bitcast.here_ref, f32[3,8,8192]{2,1,0:T(8,128)S(1)} %get-tuple-element.38.edge_ref, f32[3,8,3072]{2,1,0:T(8,128)S(1)} %collective-permute-done.4.below_ref, ...), custom_call_target="tpu_custom_call" | custom-call | flops 1000000 | bytes 8388608 | tf_op jit(solution)/shard_map/edge_steps/pallas_call | solution.py:437
  78.8 9.5 %collective-permute-done.6.far_late_ref = f32[3,8,4096]{2,1,0:T(8,128)S(1)} collective-permute-done((f32[3,8,4096]{2,1,0:T(8,128)S(1)}, f32[3,8,4096]{2,1,0:T(8,128)S(1)}, u32[]{:S(2)}, u32[]{:S(2)}) %collective-permute-start.6) | collective-permute-done | bytes 393248 | tf_op jit(solution)/shard_map/ppermute | solution.py:364
  88.3 0.0 collective-permute-done.7.back_ref
  88.3 11.0 %main_steps.1 = (f32[8,32768]{1,0:T(8,128)}, f32[8,32768]{1,0:T(8,128)}) custom-call(s32[1]{0:T(128)} %bitcast.here_ref, f32[3,8,24576]{2,1,0:T(8,128)S(1)} %get-tuple-element.27.stay_ref, f32[3,8,28672]{2,1,0:T(8,128)S(1)} %collective-permute-done.1.far_ref, ...), custom_call_target="tpu_custom_call", output_to_operand_aliasing={{0}: (9, {}), {1}: (10, {})} | custom-call | flops 1000000 | bytes 20971520 | tf_op jit(solution)/shard_map/main_steps/pallas_call | solution.py:450
Async XLA Ops:
  0.6 9.2 %copy-start.1 = (s32[16]{0:T(128)S(1)}, s32[16]{0:T(128)}, u32[]{:S(2)}) copy-start(s32[16]{0:T(128)} %slot_ref.3) | copy-start | bytes 196
  3.8 6.0 %collective-permute-start.2 = (f32[3,8,32768]{2,1,0:T(8,128)S(1)}, f32[3,8,32768]{2,1,0:T(8,128)S(1)}, u32[]{:S(2)}, u32[]{:S(2)}) collective-permute-start(f32[3,8,32768]{2,1,0:T(8,128)S(1)} %get-tuple-element.31), channel_id=1, source_target_pairs={{0,1},{1,0},{2,3},{3,2},{4,5},{5,4},{6,7},{7,6},{8,9},{9,8},{10,11... | collective-permute-start | bytes 9437192 | tf_op jit(solution)/shard_map/ppermute | solution.py:364
  4.5 15.3 %collective-permute-start = (f32[3,8,32768]{2,1,0:T(8,128)S(1)}, f32[3,8,32768]{2,1,0:T(8,128)S(1)}, u32[]{:S(2)}, u32[]{:S(2)}) collective-permute-start(f32[3,8,32768]{2,1,0:T(8,128)S(1)} %get-tuple-element.26), channel_id=1, source_target_pairs={{0,1},{1,0},{2,3},{3,2},{4,5},{5,4},{6,7},{7,6},{8,9},{9,8},{10,11... | collective-permute-start | bytes 9437192 | tf_op jit(solution)/shard_map/ppermute | solution.py:364
  4.6 47.7 %collective-permute-start.1 = (f32[3,8,28672]{2,1,0:T(8,128)S(1)}, f32[3,8,28672]{2,1,0:T(8,128)S(1)}, u32[]{:S(2)}, u32[]{:S(2)}) collective-permute-start(f32[3,8,28672]{2,1,0:T(8,128)S(1)} %get-tuple-element.28), channel_id=1, source_target_pairs={{1,3},{2,0},{3,5},{4,2},{5,7},{6,4},{7,9},{8,6},{9,11},{10,8},{11,... | collective-permute-start | bytes 8257544 | tf_op jit(solution)/shard_map/ppermute | solution.py:364
  11.8 25.5 %collective-permute-start.3 = (f32[3,8,8192]{2,1,0:T(8,128)S(1)}, f32[3,8,8192]{2,1,0:T(8,128)S(1)}, u32[]{:S(2)}, u32[]{:S(2)}) collective-permute-start(f32[3,8,8192]{2,1,0:T(8,128)S(1)} %get-tuple-element.32), channel_id=1, source_target_pairs={{0,2},{2,4},{3,1},{4,6},{5,3},{6,8},{7,5},{8,10},{9,7},{10,12},{11... | collective-permute-start | bytes 2359304 | tf_op jit(solution)/shard_map/ppermute | solution.py:364
  21.9 53.6 %copy-start = (s32[8,6]{1,0:T(8,128)S(1)}, s32[8,6]{1,0:T(8,128)}, u32[]{:S(2)}) copy-start(s32[8,6]{1,0:T(8,128)} %nbr_ref.3) | copy-start | bytes 580
  37.3 51.1 %collective-permute-start.7 = (f32[3,8,24576]{2,1,0:T(8,128)S(1)}, f32[3,8,24576]{2,1,0:T(8,128)S(1)}, u32[]{:S(2)}, u32[]{:S(2)}) collective-permute-start(f32[3,8,24576]{2,1,0:T(8,128)S(1)} %get-tuple-element.37), channel_id=1, source_target_pairs={{0,2},{2,4},{3,1},{4,6},{5,3},{6,8},{7,5},{8,10},{9,7},{10,12},{11... | collective-permute-start | bytes 7077896 | tf_op jit(solution)/shard_map/ppermute | solution.py:364
  52.5 16.2 %collective-permute-start.4 = (f32[3,8,3072]{2,1,0:T(8,128)S(1)}, f32[3,8,3072]{2,1,0:T(8,128)S(1)}, u32[]{:S(2)}, u32[]{:S(2)}) collective-permute-start(f32[3,8,3072]{2,1,0:T(8,128)S(1)} %get-tuple-element.33), channel_id=1, source_target_pairs={{0,1},{1,2},{2,3},{3,4},{4,5},{5,6},{6,7},{7,8},{8,9},{9,10},{10,1... | collective-permute-start | bytes 884744 | tf_op jit(solution)/shard_map/ppermute | solution.py:364
  61.8 11.6 %collective-permute-start.5 = (f32[3,8,3072]{2,1,0:T(8,128)S(1)}, f32[3,8,3072]{2,1,0:T(8,128)S(1)}, u32[]{:S(2)}, u32[]{:S(2)}) collective-permute-start(f32[3,8,3072]{2,1,0:T(8,128)S(1)} %get-tuple-element.34), channel_id=1, source_target_pairs={{1,0},{2,1},{3,2},{4,3},{5,4},{6,5},{7,6},{8,7},{9,8},{10,9},{11,1... | collective-permute-start | bytes 884744 | tf_op jit(solution)/shard_map/ppermute | solution.py:364
  73.4 14.9 %collective-permute-start.6 = (f32[3,8,4096]{2,1,0:T(8,128)S(1)}, f32[3,8,4096]{2,1,0:T(8,128)S(1)}, u32[]{:S(2)}, u32[]{:S(2)}) collective-permute-start(f32[3,8,4096]{2,1,0:T(8,128)S(1)} %get-tuple-element.35), channel_id=1, source_target_pairs={{1,3},{2,0},{3,5},{4,2},{5,7},{6,4},{7,9},{8,6},{9,11},{10,8},{11,... | collective-permute-start | bytes 1179656 | tf_op jit(solution)/shard_map/ppermute | solution.py:364

commit v8 on v7

--- a/solution.py
+++ b/solution.py
@@ -20,8 +20,6 @@
 LANES = 128
 EXT = EDGE + 2 * HALO
 REST = EDGE - 2 * CHUNK_PLANES
-AHEAD = 20
-FIRST_STEPS = 2 + AHEAD // CHUNK_PLANES
 VREGS = FACE // LANES
 
 time_step = 0.15
@@ -68,7 +66,7 @@
 
 def pack_kernel(
     here_ref, slot_hbm, phi_hbm, conc_hbm, mob_hbm,
-    phi_ref, conc_ref, mob_ref, merge_ref, final_ref, far_ref, late_ref,
+    phi_ref, conc_ref, mob_ref, merge_ref, final_ref, far_ref,
     slot_ref, slot_sem, sems,
 ):
     olds = tuple(zip((phi_hbm, conc_hbm, mob_hbm), (phi_ref, conc_ref, mob_ref)))
@@ -91,7 +89,7 @@
     amount, masks = windows(slot_ref, here)
     far, merge, final = masks(2 * side), masks(side), masks(-side)
 
-    def fill(i, out_ref, out_start):
+    def fill(i):
         start = chunk_at(i) * CHUNK
         for f, (_, ref) in enumerate(olds):
             for v in range(CHUNK // LANES):
@@ -99,19 +97,13 @@
                 rows = aligned(ref, lanes, amount)
                 merge_ref[f, :, lanes] = picked(merge, *rows)
                 final_ref[f, :, lanes] = picked(final, *rows)
-                out_ref[f, :, lanes_at(out_start, v)] = picked(far, *rows)
-
-    @pl.loop(0, FIRST_STEPS)
+                far_ref[f, :, lanes_at(i * CHUNK, v)] = picked(far, *rows)
+
+    @pl.loop(0, CHUNKS)
     def _(i):
         for copy in copies(i):
             copy.wait()
-        fill(i, far_ref, i * CHUNK)
-
-    @pl.loop(FIRST_STEPS, CHUNKS)
-    def _(i):
-        for copy in copies(i):
-            copy.wait()
-        fill(i, late_ref, (i - FIRST_STEPS) * CHUNK)
+        fill(i)
 
 
 def add_rows(masks, amount, old_refs, add_ref, edge_ref, rest_ref):
@@ -302,7 +294,7 @@
 
 
 def main_kernel(
-    here_ref, stay_ref, far_ref, far_late_ref, back_ref, nbr_ref, kept0_ref, kept1_ref, kept2_ref, _phase_in, _solute_in,
+    here_ref, stay_ref, far_ref, back_ref, nbr_ref, kept0_ref, kept1_ref, kept2_ref, _phase_in, _solute_in,
     phase_hbm, solute_hbm,
     phi0, conc0, mob, phi1, conc1, phi2, conc2, phase_ref, solute_ref, sems,
 ):
@@ -318,8 +310,7 @@
     for f, ref in enumerate((phi2, conc2)):
         for n, x in enumerate((first - 4, first - 3, last + 2, last + 3)):
             ref[x] = kept2_ref[f, n]
-    place(states, AHEAD, first, (stay_ref, 0), (far_ref, 2 * CHUNK_PLANES), (back_ref, 0))
-    place(states, REST - AHEAD, first + AHEAD, (stay_ref, AHEAD), (far_late_ref, 0), (back_ref, AHEAD))
+    place(states, REST, first, (stay_ref, 0), (far_ref, 2 * CHUNK_PLANES), (back_ref, 0))
     st.sweep(first - 1, last + 1, REST + 2, (phi0, conc0), mob, (phi1, conc1))
     st.sweep(first - 2, last + 2, REST + 4, (phi1, conc1), mob, (phi2, conc2))
     start = first - 3
@@ -375,17 +366,17 @@
 
     slots_hbm = pltpu.with_memory_space_constraint(new_global_slot, pltpu.HBM)
     old_shape = jax.ShapeDtypeStruct((OLD, CELLS), jnp.float32)
-    *olds, merge, final, far_first, far_late = pl.pallas_call(
+    *olds, merge, final, far_all = pl.pallas_call(
         pack_kernel,
         in_specs=[SMEM, HBM, HBM, HBM, HBM],
-        out_specs=[VMEM] * 7,
-        out_shape=[old_shape] * 3 + [shaped(EDGE)] * 2 + [shaped(2 * CHUNK_PLANES + AHEAD), shaped(REST - AHEAD)],
+        out_specs=[VMEM] * 6,
+        out_shape=[old_shape] * 3 + [shaped(EDGE)] * 3,
         scratch_shapes=[pltpu.SMEM((OLD,), jnp.int32), pltpu.SemaphoreType.DMA, pltpu.SemaphoreType.DMA((CHUNKS, FIELDS))],
         compiler_params=PARAMS,
         cost_estimate=cost(6 * MB),
         name="pack",
     )(here, slots_hbm, *olds)
-    far_first_got = sent(far_first, far_route)
+    far_got = sent(far_all, far_route)
     merge_got = sent(merge, partner)
     final_got = sent(final, partner)
 
@@ -423,10 +414,9 @@
         compiler_params=PARAMS,
         cost_estimate=cost(3 * MB),
         name="faces",
-    )(stay_edge, far_first_got, back_edge_got)
+    )(stay_edge, far_got, back_edge_got)
     below = sent(high, [(p, p + 1) for p in devices])
     above = sent(low, [(p, p - 1) for p in devices])
-    far_late_got = sent(after(far_late, below, above), far_route)
 
     state = pltpu.VMEM((EXT, CAP, FACE), jnp.float32)
     whole = jax.ShapeDtypeStruct((CAP, CELLS), jnp.float32)
@@ -449,15 +439,15 @@
     rows_out = pltpu.VMEM((CAP, OUT_PLANES * FACE), jnp.float32)
     phase, solute = pl.pallas_call(
         main_kernel,
-        in_specs=[SMEM] + [VMEM] * 8 + [HBM] * 2,
+        in_specs=[SMEM] + [VMEM] * 7 + [HBM] * 2,
         out_specs=[HBM] * 2,
         out_shape=[whole, whole],
         scratch_shapes=[state] * 7 + [rows_out] * 2 + [pltpu.SemaphoreType.DMA((PIECES, 2))],
-        input_output_aliases={9: 0, 10: 1},
+        input_output_aliases={8: 0, 9: 1},
         compiler_params=PARAMS,
         cost_estimate=cost(20 * MB),
         name="main_steps",
-    )(here, stay_rest, far_first_got, far_late_got, back_rest_got, neighbors, kept0, kept1, kept2, phase, solute)
+    )(here, stay_rest, far_got, back_rest_got, neighbors, kept0, kept1, kept2, phase, solute)
     return phase, solute
 
 

time: 99.8 us -> 98.3 us (0.985)
  the two profiles are of different devices: /device:TPU:25 before, /device:TPU:24 now
where the time goes in v8:
time: 98.3 us; the launch traced here: 97.8 us
  waiting for transfers between devices  52.3 us (53%)
  starting transfers between devices  22.8 us (23%)
  Pallas kernels  21.7 us (22%)
    ppermute x7, waiting for transfers between devices, sent(): lax.ppermute(block, 'blk', [(p, q) for p, q in route if 0 <= q < count])  52.3 us
    ppermute x7, starting transfers between devices, sent(): lax.ppermute(block, 'blk', [(p, q) for p, q in route if 0 <= q < count])  22.8 us
    pallas_call x1, Pallas kernels, on_device(): pl.pallas_call(main_kernel, in_specs=[SMEM] + [VMEM] * 7 + [HBM] * 2, out...  11 us
    pallas_call x1, Pallas kernels, on_device(): pl.pallas_call(edge_kernel, in_specs=[SMEM] + [VMEM] * 4, out_specs=[VMEM...  3.34 us
    pallas_call x1, Pallas kernels, on_device(): pl.pallas_call(pack_kernel, in_specs=[SMEM, HBM, HBM, HBM, HBM], out_spec...  3.19 us
    pallas_call x1, Pallas kernels, on_device(): pl.pallas_call(relay_kernel, in_specs=[SMEM, SMEM] + [VMEM] * 4, out_spec...  1.99 us
    pallas_call x1, Pallas kernels, on_device(): pl.pallas_call(stay_kernel, in_specs=[SMEM, SMEM] + [VMEM] * 4, out_specs...  1.99 us
  transfers between devices with their start and end apart: 7, of which 4 were waited for; matrix products, arithmetic and copies ran while one was open for 0% of the time, Pallas kernels for 8%

profile of v8, /device:TPU:24, one launch (start us, length us, event | category | flops | bytes accessed | tf_op | source)
XLA Modules:
  0.0 97.8 jit_solution(11960654543719985566)
XLA Ops:
  0.6 0.0 copy-start.1
  0.6 3.2 %pack.1 = (f32[16,32768]{1,0:T(8,128)S(1)}, f32[16,32768]{1,0:T(8,128)S(1)}, f32[16,32768]{1,0:T(8,128)S(1)}, f32[3,8,32768]{2,1,0:T(8,128)S(1)}, f32[3,8,32768]...) custom-call(s32[1]{0:T(128)} %bitcast.here_ref, s32[16]{0:T(128)} %slot_ref.3, f32[16,32768]{1,0:T(8,128)} %phi_hbm.1, ...), custom_call_target="tpu_custom_call" | custom-call | flops 1000000 | bytes 6291456 | tf_op jit(solution)/shard_map/pack/pallas_call | solution.py:369
  3.8 0.1 collective-permute-start.2
  3.9 0.5 collective-permute-start
  4.4 8.3 %collective-permute-start.1 = (f32[3,8,32768]{2,1,0:T(8,128)S(1)}, f32[3,8,32768]{2,1,0:T(8,128)S(1)}, u32[]{:S(2)}, u32[]{:S(2)}) collective-permute-start(f32[3,8,32768]{2,1,0:T(8,128)S(1)} %get-tuple-element.26), channel_id=1, source_target_pairs={{1,3},{2,0},{3,5},{4,2},{5,7},{6,4},{7,9},{8,6},{9,11},{10,8},{11,... | collective-permute-start | bytes 9437192 | tf_op jit(solution)/shard_map/ppermute | solution.py:355
  12.8 0.0 collective-permute-done.2.merge_ref
  12.8 0.0 copy-done.1
  12.8 2.0 %relay.1 = (f32[3,8,8192]{2,1,0:T(8,128)S(1)}, f32[3,8,24576]{2,1,0:T(8,128)S(1)}) custom-call(s32[1]{0:T(128)} %bitcast.here_ref, s32[16]{0:T(128)S(1)} %copy-done.1, f32[16,32768]{1,0:T(8,128)S(1)} %get-tuple-element.21.phi_ref, f32[16,32768]{1,0:T(8,128)S(1)} %get-tuple-element.22.conc_ref, f32[16,32768]{1,0:T(8,128)S(1)} %get-tuple-element.23.mob_ref, ...), custom_call_target="tpu_custom_call" | custom-call | flops 1000000 | bytes 6291456 | tf_op jit(solution)/shard_map/relay/pallas_call | solution.py:384
  14.8 1.9 %collective-permute-start.3 = (f32[3,8,8192]{2,1,0:T(8,128)S(1)}, f32[3,8,8192]{2,1,0:T(8,128)S(1)}, u32[]{:S(2)}, u32[]{:S(2)}) collective-permute-start(f32[3,8,8192]{2,1,0:T(8,128)S(1)} %get-tuple-element.29), channel_id=1, source_target_pairs={{0,2},{2,4},{3,1},{4,6},{5,3},{6,8},{7,5},{8,10},{9,7},{10,12},{11... | collective-permute-start | bytes 2359304 | tf_op jit(solution)/shard_map/ppermute | solution.py:355
  16.7 0.0 collective-permute-done.final_ref
  16.7 2.0 %stay.1 = (f32[3,8,8192]{2,1,0:T(8,128)S(1)}, f32[3,8,24576]{2,1,0:T(8,128)S(1)}) custom-call(s32[1]{0:T(128)} %bitcast.here_ref, s32[16]{0:T(128)S(1)} %copy-done.1, f32[16,32768]{1,0:T(8,128)S(1)} %get-tuple-element.21.phi_ref, f32[16,32768]{1,0:T(8,128)S(1)} %get-tuple-element.22.conc_ref, f32[16,32768]{1,0:T(8,128)S(1)} %get-tuple-element.23.mob_ref, ...), custom_call_target="tpu_custom_call" | custom-call | flops 1000000 | bytes 6291456 | tf_op jit(solution)/shard_map/stay/pallas_call | solution.py:395
  18.7 22.7 %collective-permute-done.3.back_ref = f32[3,8,8192]{2,1,0:T(8,128)S(1)} collective-permute-done((f32[3,8,8192]{2,1,0:T(8,128)S(1)}, f32[3,8,8192]{2,1,0:T(8,128)S(1)}, u32[]{:S(2)}, u32[]{:S(2)}) %collective-permute-start.3) | collective-permute-done | bytes 786464 | tf_op jit(solution)/shard_map/ppermute | solution.py:355
  41.4 0.0 copy-start
  41.4 2.0 %collective-permute-start.4 = (f32[3,8,24576]{2,1,0:T(8,128)S(1)}, f32[3,8,24576]{2,1,0:T(8,128)S(1)}, u32[]{:S(2)}, u32[]{:S(2)}) collective-permute-start(f32[3,8,24576]{2,1,0:T(8,128)S(1)} %get-tuple-element.31), channel_id=1, source_target_pairs={{0,2},{2,4},{3,1},{4,6},{5,3},{6,8},{7,5},{8,10},{9,7},{10,12},{11... | collective-permute-start | bytes 7077896 | tf_op jit(solution)/shard_map/ppermute | solution.py:355
  43.4 22.4 %collective-permute-done.1.far_ref = f32[3,8,32768]{2,1,0:T(8,128)S(1)} collective-permute-done((f32[3,8,32768]{2,1,0:T(8,128)S(1)}, f32[3,8,32768]{2,1,0:T(8,128)S(1)}, u32[]{:S(2)}, u32[]{:S(2)}) %collective-permute-start.1) | collective-permute-done | bytes 3145760 | tf_op jit(solution)/shard_map/ppermute | solution.py:355
  65.8 0.2 faces.1
  66.0 1.9 %collective-permute-start.5 = (f32[3,8,3072]{2,1,0:T(8,128)S(1)}, f32[3,8,3072]{2,1,0:T(8,128)S(1)}, u32[]{:S(2)}, u32[]{:S(2)}) collective-permute-start(f32[3,8,3072]{2,1,0:T(8,128)S(1)} %get-tuple-element.33), channel_id=1, source_target_pairs={{0,1},{1,2},{2,3},{3,4},{4,5},{5,6},{6,7},{7,8},{8,9},{9,10},{10,1... | collective-permute-start | bytes 884744 | tf_op jit(solution)/shard_map/ppermute | solution.py:355
  67.9 8.0 %collective-permute-start.6 = (f32[3,8,3072]{2,1,0:T(8,128)S(1)}, f32[3,8,3072]{2,1,0:T(8,128)S(1)}, u32[]{:S(2)}, u32[]{:S(2)}) collective-permute-start(f32[3,8,3072]{2,1,0:T(8,128)S(1)} %get-tuple-element.34), channel_id=1, source_target_pairs={{1,0},{2,1},{3,2},{4,3},{5,4},{6,5},{7,6},{8,7},{9,8},{10,9},{11,1... | collective-permute-start | bytes 884744 | tf_op jit(solution)/shard_map/ppermute | solution.py:355
  76.0 5.5 %collective-permute-done.5.below_ref = f32[3,8,3072]{2,1,0:T(8,128)S(1)} collective-permute-done((f32[3,8,3072]{2,1,0:T(8,128)S(1)}, f32[3,8,3072]{2,1,0:T(8,128)S(1)}, u32[]{:S(2)}, u32[]{:S(2)}) %collective-permute-start.5) | collective-permute-done | bytes 294944 | tf_op jit(solution)/shard_map/ppermute | solution.py:355
  81.5 1.8 %collective-permute-done.6.above_ref = f32[3,8,3072]{2,1,0:T(8,128)S(1)} collective-permute-done((f32[3,8,3072]{2,1,0:T(8,128)S(1)}, f32[3,8,3072]{2,1,0:T(8,128)S(1)}, u32[]{:S(2)}, u32[]{:S(2)}) %collective-permute-start.6) | collective-permute-done | bytes 294944 | tf_op jit(solution)/shard_map/ppermute | solution.py:355
  83.2 0.0 copy-done
  83.2 3.3 %edge_steps.1 = (f32[8,32768]{1,0:T(8,128)}, f32[8,32768]{1,0:T(8,128)}, f32[3,6,8,1024]{3,2,1,0:T(8,128)S(1)}, f32[2,4,8,1024]{3,2,1,0:T(8,128)S(1)}, f32[2,4,8,1024]{3,2,1,0:T(8,128)S(1)}) custom-call(s32[1]{0:T(128)} %bitcast.here_ref, f32[3,8,8192]{2,1,0:T(8,128)S(1)} %get-tuple-element.32.edge_ref, f32[3,8,3072]{2,1,0:T(8,128)S(1)} %collective-permute-done.5.below_ref, ...), custom_call_target="tpu_custom_call" | custom-call | flops 1000000 | bytes 8388608 | tf_op jit(solution)/shard_map/edge_steps/pallas_call | solution.py:427
  86.6 0.0 collective-permute-done.4.back_ref
  86.6 11.0 %main_steps.1 = (f32[8,32768]{1,0:T(8,128)}, f32[8,32768]{1,0:T(8,128)}) custom-call(s32[1]{0:T(128)} %bitcast.here_ref, f32[3,8,24576]{2,1,0:T(8,128)S(1)} %get-tuple-element.25.stay_ref, f32[3,8,32768]{2,1,0:T(8,128)S(1)} %collective-permute-done.1.far_ref, ...), custom_call_target="tpu_custom_call", output_to_operand_aliasing={{0}: (8, {}), {1}: (9, {})} | custom-call | flops 1000000 | bytes 20971520 | tf_op jit(solution)/shard_map/main_steps/pallas_call | solution.py:440
Async XLA Ops:
  0.6 12.1 %copy-start.1 = (s32[16]{0:T(128)S(1)}, s32[16]{0:T(128)}, u32[]{:S(2)}) copy-start(s32[16]{0:T(128)} %slot_ref.3) | copy-start | bytes 196
  3.8 8.9 %collective-permute-start.2 = (f32[3,8,32768]{2,1,0:T(8,128)S(1)}, f32[3,8,32768]{2,1,0:T(8,128)S(1)}, u32[]{:S(2)}, u32[]{:S(2)}) collective-permute-start(f32[3,8,32768]{2,1,0:T(8,128)S(1)} %get-tuple-element.27), channel_id=1, source_target_pairs={{0,1},{1,0},{2,3},{3,2},{4,5},{5,4},{6,7},{7,6},{8,9},{9,8},{10,11... | collective-permute-start | bytes 9437192 | tf_op jit(solution)/shard_map/ppermute | solution.py:355
  3.9 12.8 %collective-permute-start = (f32[3,8,32768]{2,1,0:T(8,128)S(1)}, f32[3,8,32768]{2,1,0:T(8,128)S(1)}, u32[]{:S(2)}, u32[]{:S(2)}) collective-permute-start(f32[3,8,32768]{2,1,0:T(8,128)S(1)} %get-tuple-element.24), channel_id=1, source_target_pairs={{0,1},{1,0},{2,3},{3,2},{4,5},{5,4},{6,7},{7,6},{8,9},{9,8},{10,11... | collective-permute-start | bytes 9437192 | tf_op jit(solution)/shard_map/ppermute | solution.py:355
  4.4 61.4 %collective-permute-start.1 = (f32[3,8,32768]{2,1,0:T(8,128)S(1)}, f32[3,8,32768]{2,1,0:T(8,128)S(1)}, u32[]{:S(2)}, u32[]{:S(2)}) collective-permute-start(f32[3,8,32768]{2,1,0:T(8,128)S(1)} %get-tuple-element.26), channel_id=1, source_target_pairs={{1,3},{2,0},{3,5},{4,2},{5,7},{6,4},{7,9},{8,6},{9,11},{10,8},{11,... | collective-permute-start | bytes 9437192 | tf_op jit(solution)/shard_map/ppermute | solution.py:355
  14.8 26.6 %collective-permute-start.3 = (f32[3,8,8192]{2,1,0:T(8,128)S(1)}, f32[3,8,8192]{2,1,0:T(8,128)S(1)}, u32[]{:S(2)}, u32[]{:S(2)}) collective-permute-start(f32[3,8,8192]{2,1,0:T(8,128)S(1)} %get-tuple-element.29), channel_id=1, source_target_pairs={{0,2},{2,4},{3,1},{4,6},{5,3},{6,8},{7,5},{8,10},{9,7},{10,12},{11... | collective-permute-start | bytes 2359304 | tf_op jit(solution)/shard_map/ppermute | solution.py:355
  41.4 41.9 %copy-start = (s32[8,6]{1,0:T(8,128)S(1)}, s32[8,6]{1,0:T(8,128)}, u32[]{:S(2)}) copy-start(s32[8,6]{1,0:T(8,128)} %nbr_ref.3) | copy-start | bytes 580
  41.4 45.2 %collective-permute-start.4 = (f32[3,8,24576]{2,1,0:T(8,128)S(1)}, f32[3,8,24576]{2,1,0:T(8,128)S(1)}, u32[]{:S(2)}, u32[]{:S(2)}) collective-permute-start(f32[3,8,24576]{2,1,0:T(8,128)S(1)} %get-tuple-element.31), channel_id=1, source_target_pairs={{0,2},{2,4},{3,1},{4,6},{5,3},{6,8},{7,5},{8,10},{9,7},{10,12},{11... | collective-permute-start | bytes 7077896 | tf_op jit(solution)/shard_map/ppermute | solution.py:355
  66.0 15.5 %collective-permute-start.5 = (f32[3,8,3072]{2,1,0:T(8,128)S(1)}, f32[3,8,3072]{2,1,0:T(8,128)S(1)}, u32[]{:S(2)}, u32[]{:S(2)}) collective-permute-start(f32[3,8,3072]{2,1,0:T(8,128)S(1)} %get-tuple-element.33), channel_id=1, source_target_pairs={{0,1},{1,2},{2,3},{3,4},{4,5},{5,6},{6,7},{7,8},{8,9},{9,10},{10,1... | collective-permute-start | bytes 884744 | tf_op jit(solution)/shard_map/ppermute | solution.py:355
  67.9 15.3 %collective-permute-start.6 = (f32[3,8,3072]{2,1,0:T(8,128)S(1)}, f32[3,8,3072]{2,1,0:T(8,128)S(1)}, u32[]{:S(2)}, u32[]{:S(2)}) collective-permute-start(f32[3,8,3072]{2,1,0:T(8,128)S(1)} %get-tuple-element.34), channel_id=1, source_target_pairs={{1,0},{2,1},{3,2},{4,3},{5,4},{6,5},{7,6},{8,7},{9,8},{10,9},{11,1... | collective-permute-start | bytes 884744 | tf_op jit(solution)/shard_map/ppermute | solution.py:355

commit v9 on v7

--- a/solution.py
+++ b/solution.py
@@ -20,7 +20,7 @@
 LANES = 128
 EXT = EDGE + 2 * HALO
 REST = EDGE - 2 * CHUNK_PLANES
-AHEAD = 20
+AHEAD = 16
 FIRST_STEPS = 2 + AHEAD // CHUNK_PLANES
 VREGS = FACE // LANES
 
@@ -386,6 +386,7 @@
         name="pack",
     )(here, slots_hbm, *olds)
     far_first_got = sent(far_first, far_route)
+    far_late_got = sent(after(far_late, far_first_got), far_route)
     merge_got = sent(merge, partner)
     final_got = sent(final, partner)
 
@@ -426,7 +427,6 @@
     )(stay_edge, far_first_got, back_edge_got)
     below = sent(high, [(p, p + 1) for p in devices])
     above = sent(low, [(p, p - 1) for p in devices])
-    far_late_got = sent(after(far_late, below, above), far_route)
 
     state = pltpu.VMEM((EXT, CAP, FACE), jnp.float32)
     whole = jax.ShapeDtypeStruct((CAP, CELLS), jnp.float32)

time: 99.8 us -> 99.3 us (level)
  the two profiles are of different devices: /device:TPU:25 before, /device:TPU:24 now
where the time goes in v9:
time: 99.3 us; the launch traced here: 99.1 us
  waiting for transfers between devices  45.2 us (46%)
  starting transfers between devices  31.3 us (32%)
  Pallas kernels  21.7 us (22%)
    ppermute x8, waiting for transfers between devices, sent(): lax.ppermute(block, 'blk', [(p, q) for p, q in route if 0 <= q < count])  45.2 us
    ppermute x8, starting transfers between devices, sent(): lax.ppermute(block, 'blk', [(p, q) for p, q in route if 0 <= q < count])  31.3 us
    pallas_call x1, Pallas kernels, on_device(): pl.pallas_call(main_kernel, in_specs=[SMEM] + [VMEM] * 8 + [HBM] * 2, out...  11 us
    pallas_call x1, Pallas kernels, on_device(): pl.pallas_call(edge_kernel, in_specs=[SMEM] + [VMEM] * 4, out_specs=[VMEM...  3.32 us
    pallas_call x1, Pallas kernels, on_device(): pl.pallas_call(pack_kernel, in_specs=[SMEM, HBM, HBM, HBM, HBM], out_spec...  3.19 us
    pallas_call x1, Pallas kernels, on_device(): pl.pallas_call(relay_kernel, in_specs=[SMEM, SMEM] + [VMEM] * 4, out_spec...  1.99 us
  transfers between devices with their start and end apart: 8, of which 5 were waited for; matrix products, arithmetic and copies ran while one was open for 0% of the time, Pallas kernels for 8%

profile of v9, /device:TPU:24, one launch (start us, length us, event | category | flops | bytes accessed | tf_op | source)
XLA Modules:
  0.0 99.1 jit_solution(2596910456210763425)
XLA Ops:
  0.6 0.0 copy-start.1
  0.6 3.2 %pack.1 = (f32[16,32768]{1,0:T(8,128)S(1)}, f32[16,32768]{1,0:T(8,128)S(1)}, f32[16,32768]{1,0:T(8,128)S(1)}, f32[3,8,32768]{2,1,0:T(8,128)S(1)}, f32[3,8,32768]...) custom-call(s32[1]{0:T(128)} %bitcast.here_ref, s32[16]{0:T(128)} %slot_ref.3, ...), custom_call_target="tpu_custom_call" | custom-call | flops 1000000 | bytes 6291456 | tf_op jit(solution)/shard_map/pack/pallas_call | solution.py:378
  3.8 0.1 collective-permute-start.3
  3.9 0.5 collective-permute-start
  4.4 8.3 %collective-permute-start.1 = (f32[3,8,24576]{2,1,0:T(8,128)S(1)}, f32[3,8,24576]{2,1,0:T(8,128)S(1)}, u32[]{:S(2)}, u32[]{:S(2)}) collective-permute-start(f32[3,8,24576]{2,1,0:T(8,128)S(1)} %get-tuple-element.28), channel_id=1, source_target_pairs={{1,3},{2,0},{3,5},{4,2},{5,7},{6,4},{7,9},{8,6},{9,11},{10,8},{11,... | collective-permute-start | bytes 7077896 | tf_op jit(solution)/shard_map/ppermute | solution.py:364
  12.7 0.0 collective-permute-done.3.merge_ref
  12.8 0.0 copy-done.1
  12.8 2.0 %relay.1 = (f32[3,8,8192]{2,1,0:T(8,128)S(1)}, f32[3,8,24576]{2,1,0:T(8,128)S(1)}) custom-call(s32[1]{0:T(128)} %bitcast.here_ref, s32[16]{0:T(128)S(1)} %copy-done.1, f32[16,32768]{1,0:T(8,128)S(1)} %get-tuple-element.23.phi_ref, f32[16,32768]{1,0:T(8,128)S(1)} %get-tuple-element.24.conc_ref, f32[16,32768]{1,0:T(8,128)S(1)} %get-tuple-element.25.mob_ref, ...), custom_call_target="tpu_custom_call" | custom-call | flops 1000000 | bytes 6291456 | tf_op jit(solution)/shard_map/relay/pallas_call | solution.py:394
  14.8 1.9 %collective-permute-start.4 = (f32[3,8,8192]{2,1,0:T(8,128)S(1)}, f32[3,8,8192]{2,1,0:T(8,128)S(1)}, u32[]{:S(2)}, u32[]{:S(2)}) collective-permute-start(f32[3,8,8192]{2,1,0:T(8,128)S(1)} %get-tuple-element.33), channel_id=1, source_target_pairs={{0,2},{2,4},{3,1},{4,6},{5,3},{6,8},{7,5},{8,10},{9,7},{10,12},{11... | collective-permute-start | bytes 2359304 | tf_op jit(solution)/shard_map/ppermute | solution.py:364
  16.7 0.0 collective-permute-done.final_ref
  16.7 2.0 %stay.1 = (f32[3,8,8192]{2,1,0:T(8,128)S(1)}, f32[3,8,24576]{2,1,0:T(8,128)S(1)}) custom-call(s32[1]{0:T(128)} %bitcast.here_ref, s32[16]{0:T(128)S(1)} %copy-done.1, f32[16,32768]{1,0:T(8,128)S(1)} %get-tuple-element.23.phi_ref, f32[16,32768]{1,0:T(8,128)S(1)} %get-tuple-element.24.conc_ref, f32[16,32768]{1,0:T(8,128)S(1)} %get-tuple-element.25.mob_ref, ...), custom_call_target="tpu_custom_call" | custom-call | flops 1000000 | bytes 6291456 | tf_op jit(solution)/shard_map/stay/pallas_call | solution.py:405
  18.7 0.0 copy-start
  18.7 22.6 %collective-permute-done.4.back_ref = f32[3,8,8192]{2,1,0:T(8,128)S(1)} collective-permute-done((f32[3,8,8192]{2,1,0:T(8,128)S(1)}, f32[3,8,8192]{2,1,0:T(8,128)S(1)}, u32[]{:S(2)}, u32[]{:S(2)}) %collective-permute-start.4) | collective-permute-done | bytes 786464 | tf_op jit(solution)/shard_map/ppermute | solution.py:364
  41.4 1.9 %collective-permute-start.5 = (f32[3,8,24576]{2,1,0:T(8,128)S(1)}, f32[3,8,24576]{2,1,0:T(8,128)S(1)}, u32[]{:S(2)}, u32[]{:S(2)}) collective-permute-start(f32[3,8,24576]{2,1,0:T(8,128)S(1)} %get-tuple-element.35), channel_id=1, source_target_pairs={{0,2},{2,4},{3,1},{4,6},{5,3},{6,8},{7,5},{8,10},{9,7},{10,12},{11... | collective-permute-start | bytes 7077896 | tf_op jit(solution)/shard_map/ppermute | solution.py:364
  43.3 5.8 %collective-permute-done.1.far_ref = f32[3,8,24576]{2,1,0:T(8,128)S(1)} collective-permute-done((f32[3,8,24576]{2,1,0:T(8,128)S(1)}, f32[3,8,24576]{2,1,0:T(8,128)S(1)}, u32[]{:S(2)}, u32[]{:S(2)}) %collective-permute-start.1) | collective-permute-done | bytes 2359328 | tf_op jit(solution)/shard_map/ppermute | solution.py:364
  49.1 8.6 %collective-permute-start.2 = (f32[3,8,8192]{2,1,0:T(8,128)S(1)}, f32[3,8,8192]{2,1,0:T(8,128)S(1)}, u32[]{:S(2)}, u32[]{:S(2)}) collective-permute-start(f32[3,8,8192]{2,1,0:T(8,128)S(1)} %get-tuple-element.30), channel_id=1, source_target_pairs={{1,3},{2,0},{3,5},{4,2},{5,7},{6,4},{7,9},{8,6},{9,11},{10,8},{11,... | collective-permute-start | bytes 2359304 | tf_op jit(solution)/shard_map/ppermute | solution.py:364
  57.7 0.2 faces.1
  57.9 1.9 %collective-permute-start.6 = (f32[3,8,3072]{2,1,0:T(8,128)S(1)}, f32[3,8,3072]{2,1,0:T(8,128)S(1)}, u32[]{:S(2)}, u32[]{:S(2)}) collective-permute-start(f32[3,8,3072]{2,1,0:T(8,128)S(1)} %get-tuple-element.37), channel_id=1, source_target_pairs={{0,1},{1,2},{2,3},{3,4},{4,5},{5,6},{6,7},{7,8},{8,9},{9,10},{10,1... | collective-permute-start | bytes 884744 | tf_op jit(solution)/shard_map/ppermute | solution.py:364
  59.8 8.0 %collective-permute-start.7 = (f32[3,8,3072]{2,1,0:T(8,128)S(1)}, f32[3,8,3072]{2,1,0:T(8,128)S(1)}, u32[]{:S(2)}, u32[]{:S(2)}) collective-permute-start(f32[3,8,3072]{2,1,0:T(8,128)S(1)} %get-tuple-element.38), channel_id=1, source_target_pairs={{1,0},{2,1},{3,2},{4,3},{5,4},{6,5},{7,6},{8,7},{9,8},{10,9},{11,1... | collective-permute-start | bytes 884744 | tf_op jit(solution)/shard_map/ppermute | solution.py:364
  67.9 11.3 %collective-permute-done.6.below_ref = f32[3,8,3072]{2,1,0:T(8,128)S(1)} collective-permute-done((f32[3,8,3072]{2,1,0:T(8,128)S(1)}, f32[3,8,3072]{2,1,0:T(8,128)S(1)}, u32[]{:S(2)}, u32[]{:S(2)}) %collective-permute-start.6) | collective-permute-done | bytes 294944 | tf_op jit(solution)/shard_map/ppermute | solution.py:364
  79.1 2.9 %collective-permute-done.7.above_ref = f32[3,8,3072]{2,1,0:T(8,128)S(1)} collective-permute-done((f32[3,8,3072]{2,1,0:T(8,128)S(1)}, f32[3,8,3072]{2,1,0:T(8,128)S(1)}, u32[]{:S(2)}, u32[]{:S(2)}) %collective-permute-start.7) | collective-permute-done | bytes 294944 | tf_op jit(solution)/shard_map/ppermute | solution.py:364
  82.0 0.0 copy-done
  82.0 3.3 %edge_steps.1 = (f32[8,32768]{1,0:T(8,128)}, f32[8,32768]{1,0:T(8,128)}, f32[3,6,8,1024]{3,2,1,0:T(8,128)S(1)}, f32[2,4,8,1024]{3,2,1,0:T(8,128)S(1)}, f32[2,4,8,1024]{3,2,1,0:T(8,128)S(1)}) custom-call(s32[1]{0:T(128)} %bitcast.here_ref, f32[3,8,8192]{2,1,0:T(8,128)S(1)} %get-tuple-element.36.edge_ref, f32[3,8,3072]{2,1,0:T(8,128)S(1)} %collective-permute-done.6.below_ref, ...), custom_call_target="tpu_custom_call" | custom-call | flops 1000000 | bytes 8388608 | tf_op jit(solution)/shard_map/edge_steps/pallas_call | solution.py:437
  85.3 0.0 collective-permute-done.2.far_late_ref
  85.3 2.6 %collective-permute-done.5.back_ref = f32[3,8,24576]{2,1,0:T(8,128)S(1)} collective-permute-done((f32[3,8,24576]{2,1,0:T(8,128)S(1)}, f32[3,8,24576]{2,1,0:T(8,128)S(1)}, u32[]{:S(2)}, u32[]{:S(2)}) %collective-permute-start.5) | collective-permute-done | bytes 2359328 | tf_op jit(solution)/shard_map/ppermute | solution.py:364
  87.9 11.0 %main_steps.1 = (f32[8,32768]{1,0:T(8,128)}, f32[8,32768]{1,0:T(8,128)}) custom-call(s32[1]{0:T(128)} %bitcast.here_ref, f32[3,8,24576]{2,1,0:T(8,128)S(1)} %get-tuple-element.27.stay_ref, f32[3,8,24576]{2,1,0:T(8,128)S(1)} %collective-permute-done.1.far_ref, ...), custom_call_target="tpu_custom_call", output_to_operand_aliasing={{0}: (9, {}), {1}: (10, {})} | custom-call | flops 1000000 | bytes 20971520 | tf_op jit(solution)/shard_map/main_steps/pallas_call | solution.py:450
Async XLA Ops:
  0.6 12.1 %copy-start.1 = (s32[16]{0:T(128)S(1)}, s32[16]{0:T(128)}, u32[]{:S(2)}) copy-start(s32[16]{0:T(128)} %slot_ref.3) | copy-start | bytes 196
  3.8 8.9 %collective-permute-start.3 = (f32[3,8,32768]{2,1,0:T(8,128)S(1)}, f32[3,8,32768]{2,1,0:T(8,128)S(1)}, u32[]{:S(2)}, u32[]{:S(2)}) collective-permute-start(f32[3,8,32768]{2,1,0:T(8,128)S(1)} %get-tuple-element.31), channel_id=1, source_target_pairs={{0,1},{1,0},{2,3},{3,2},{4,5},{5,4},{6,7},{7,6},{8,9},{9,8},{10,11... | collective-permute-start | bytes 9437192 | tf_op jit(solution)/shard_map/ppermute | solution.py:364
  3.9 12.8 %collective-permute-start = (f32[3,8,32768]{2,1,0:T(8,128)S(1)}, f32[3,8,32768]{2,1,0:T(8,128)S(1)}, u32[]{:S(2)}, u32[]{:S(2)}) collective-permute-start(f32[3,8,32768]{2,1,0:T(8,128)S(1)} %get-tuple-element.26), channel_id=1, source_target_pairs={{0,1},{1,0},{2,3},{3,2},{4,5},{5,4},{6,7},{7,6},{8,9},{9,8},{10,11... | collective-permute-start | bytes 9437192 | tf_op jit(solution)/shard_map/ppermute | solution.py:364
  4.4 44.7 %collective-permute-start.1 = (f32[3,8,24576]{2,1,0:T(8,128)S(1)}, f32[3,8,24576]{2,1,0:T(8,128)S(1)}, u32[]{:S(2)}, u32[]{:S(2)}) collective-permute-start(f32[3,8,24576]{2,1,0:T(8,128)S(1)} %get-tuple-element.28), channel_id=1, source_target_pairs={{1,3},{2,0},{3,5},{4,2},{5,7},{6,4},{7,9},{8,6},{9,11},{10,8},{11,... | collective-permute-start | bytes 7077896 | tf_op jit(solution)/shard_map/ppermute | solution.py:364
  14.8 26.6 %collective-permute-start.4 = (f32[3,8,8192]{2,1,0:T(8,128)S(1)}, f32[3,8,8192]{2,1,0:T(8,128)S(1)}, u32[]{:S(2)}, u32[]{:S(2)}) collective-permute-start(f32[3,8,8192]{2,1,0:T(8,128)S(1)} %get-tuple-element.33), channel_id=1, source_target_pairs={{0,2},{2,4},{3,1},{4,6},{5,3},{6,8},{7,5},{8,10},{9,7},{10,12},{11... | collective-permute-start | bytes 2359304 | tf_op jit(solution)/shard_map/ppermute | solution.py:364
  18.7 63.3 %copy-start = (s32[8,6]{1,0:T(8,128)S(1)}, s32[8,6]{1,0:T(8,128)}, u32[]{:S(2)}) copy-start(s32[8,6]{1,0:T(8,128)} %nbr_ref.3) | copy-start | bytes 580
  41.4 46.5 %collective-permute-start.5 = (f32[3,8,24576]{2,1,0:T(8,128)S(1)}, f32[3,8,24576]{2,1,0:T(8,128)S(1)}, u32[]{:S(2)}, u32[]{:S(2)}) collective-permute-start(f32[3,8,24576]{2,1,0:T(8,128)S(1)} %get-tuple-element.35), channel_id=1, source_target_pairs={{0,2},{2,4},{3,1},{4,6},{5,3},{6,8},{7,5},{8,10},{9,7},{10,12},{11... | collective-permute-start | bytes 7077896 | tf_op jit(solution)/shard_map/ppermute | solution.py:364
  49.1 36.2 %collective-permute-start.2 = (f32[3,8,8192]{2,1,0:T(8,128)S(1)}, f32[3,8,8192]{2,1,0:T(8,128)S(1)}, u32[]{:S(2)}, u32[]{:S(2)}) collective-permute-start(f32[3,8,8192]{2,1,0:T(8,128)S(1)} %get-tuple-element.30), channel_id=1, source_target_pairs={{1,3},{2,0},{3,5},{4,2},{5,7},{6,4},{7,9},{8,6},{9,11},{10,8},{11,... | collective-permute-start | bytes 2359304 | tf_op jit(solution)/shard_map/ppermute | solution.py:364
  57.9 21.3 %collective-permute-start.6 = (f32[3,8,3072]{2,1,0:T(8,128)S(1)}, f32[3,8,3072]{2,1,0:T(8,128)S(1)}, u32[]{:S(2)}, u32[]{:S(2)}) collective-permute-start(f32[3,8,3072]{2,1,0:T(8,128)S(1)} %get-tuple-element.37), channel_id=1, source_target_pairs={{0,1},{1,2},{2,3},{3,4},{4,5},{5,6},{6,7},{7,8},{8,9},{9,10},{10,1... | collective-permute-start | bytes 884744 | tf_op jit(solution)/shard_map/ppermute | solution.py:364
  59.8 22.2 %collective-permute-start.7 = (f32[3,8,3072]{2,1,0:T(8,128)S(1)}, f32[3,8,3072]{2,1,0:T(8,128)S(1)}, u32[]{:S(2)}, u32[]{:S(2)}) collective-permute-start(f32[3,8,3072]{2,1,0:T(8,128)S(1)} %get-tuple-element.38), channel_id=1, source_target_pairs={{1,0},{2,1},{3,2},{4,3},{5,4},{6,5},{7,6},{8,7},{9,8},{10,9},{11,1... | collective-permute-start | bytes 884744 | tf_op jit(solution)/shard_map/ppermute | solution.py:364

commit v10 on v8

--- a/solution.py
+++ b/solution.py
@@ -134,6 +134,10 @@
     add_rows(masks(0), amount, (phi_ref, conc_ref, mob_ref), final_ref, *part_refs)
 
 
+LOW_PLANES = {(f, d): n for n, (f, d) in enumerate((f, d) for f in range(FIELDS) for d in range(HALO) if f < 2 or d < HALO - 1)}
+HIGH_PLANES = {(f, d): n for n, (f, d) in enumerate((f, d) for f in range(FIELDS) for d in range(HALO) if f < 2 or d > 0)}
+
+
 def face_kernel(stay_ref, far_ref, back_ref, edge_ref, low_ref, high_ref):
     first_high = (2 * CHUNK_PLANES - HALO) * FACE
     for f in range(FIELDS):
@@ -142,10 +146,11 @@
             value = stay_ref[f, :, lanes] + far_ref[f, :, lanes] + back_ref[f, :, lanes]
             edge_ref[f, :, lanes] = value
             at = v * LANES
-            if at < HALO * FACE:
-                low_ref[f, :, lanes] = value
-            if at >= first_high:
-                high_ref[f, :, pl.ds(at - first_high, LANES)] = value
+            part = pl.ds(at % FACE, LANES)
+            if (f, at // FACE) in LOW_PLANES:
+                low_ref[LOW_PLANES[f, at // FACE], :, part] = value
+            if (f, (at - first_high) // FACE) in HIGH_PLANES:
+                high_ref[HIGH_PLANES[f, (at - first_high) // FACE], :, part] = value
 
 
 class Stencil:
@@ -265,11 +270,14 @@
         for d in range(HALO):
             for v in range(VREGS):
                 lanes = pl.ds(v * LANES, LANES)
-                part = pl.ds(d * FACE + v * LANES, LANES)
-                mirror_low = ref[2 * HALO - 1 - d, :, lanes]
-                ref[d, :, lanes] = jnp.where(st.has_below_x, st.rows(below_ref[f, :, part], st.below_x), mirror_low)
-                mirror_high = ref[EDGE + HALO - 1 - d, :, lanes]
-                ref[EDGE + HALO + d, :, lanes] = jnp.where(st.has_above_x, st.rows(above_ref[f, :, part], st.above_x), mirror_high)
+                if (f, d) in HIGH_PLANES:
+                    mirror = ref[2 * HALO - 1 - d, :, lanes]
+                    taken = st.rows(below_ref[HIGH_PLANES[f, d], :, lanes], st.below_x)
+                    ref[d, :, lanes] = jnp.where(st.has_below_x, taken, mirror)
+                if (f, d) in LOW_PLANES:
+                    mirror = ref[EDGE + HALO - 1 - d, :, lanes]
+                    taken = st.rows(above_ref[LOW_PLANES[f, d], :, lanes], st.above_x)
+                    ref[EDGE + HALO + d, :, lanes] = jnp.where(st.has_above_x, taken, mirror)
     for first, last in ((1, REST_AT - 1), (TOP_AT + 1, EXT - 1)):
         st.sweep(first, last, 5, (phi0, conc0), mob, (phi1, conc1))
         st.sweep(first + 1, last - 1, 3, (phi1, conc1), mob, (phi2, conc2))
@@ -404,13 +412,13 @@
     back_rest_got = sent(after(back_rest, back_edge_got, stay_edge), back_route)
 
     edges = pl.BlockSpec((FIELDS, CAP, 2 * CHUNK), lambda i: (0, 0, 0))
-    faces = pl.BlockSpec((FIELDS, CAP, HALO * FACE), lambda i: (0, 0, 0))
+    faces = pl.BlockSpec((len(LOW_PLANES), CAP, FACE), lambda i: (0, 0, 0))
     edge, low, high = pl.pallas_call(
         face_kernel,
         grid=(1,),
         in_specs=[edges] * 3,
         out_specs=[edges, faces, faces],
-        out_shape=[shaped(2 * CHUNK_PLANES), shaped(HALO), shaped(HALO)],
+        out_shape=[shaped(2 * CHUNK_PLANES)] + [shaped(1, len(LOW_PLANES))] * 2,
         compiler_params=PARAMS,
         cost_estimate=cost(3 * MB),
         name="faces",

time: 98.3 us -> 97.6 us (level)
  no operation moved by 1% of the time
where the time goes in v10:
time: 97.6 us; the launch traced here: 97.1 us
  waiting for transfers between devices  51.6 us (53%)
  starting transfers between devices  22.8 us (23%)
  Pallas kernels  21.7 us (22%)
    ppermute x7, waiting for transfers between devices, sent(): lax.ppermute(block, 'blk', [(p, q) for p, q in route if 0 <= q < count])  51.6 us
    ppermute x7, starting transfers between devices, sent(): lax.ppermute(block, 'blk', [(p, q) for p, q in route if 0 <= q < count])  22.8 us
    pallas_call x1, Pallas kernels, on_device(): pl.pallas_call(main_kernel, in_specs=[SMEM] + [VMEM] * 7 + [HBM] * 2, out...  11 us
    pallas_call x1, Pallas kernels, on_device(): pl.pallas_call(edge_kernel, in_specs=[SMEM] + [VMEM] * 4, out_specs=[VMEM...  3.34 us
    pallas_call x1, Pallas kernels, on_device(): pl.pallas_call(pack_kernel, in_specs=[SMEM, HBM, HBM, HBM, HBM], out_spec...  3.19 us
    pallas_call x1, Pallas kernels, on_device(): pl.pallas_call(relay_kernel, in_specs=[SMEM, SMEM] + [VMEM] * 4, out_spec...  1.99 us
    pallas_call x1, Pallas kernels, on_device(): pl.pallas_call(stay_kernel, in_specs=[SMEM, SMEM] + [VMEM] * 4, out_specs...  1.99 us
  transfers between devices with their start and end apart: 7, of which 4 were waited for; matrix products, arithmetic and copies ran while one was open for 0% of the time, Pallas kernels for 8%

profile of v10, /device:TPU:24, one launch (start us, length us, event | category | flops | bytes accessed | tf_op | source)
XLA Modules:
  0.0 97.1 jit_solution(3570123800820072987)
XLA Ops:
  0.6 0.0 copy-start.1
  0.6 3.2 %pack.1 = (f32[16,32768]{1,0:T(8,128)S(1)}, f32[16,32768]{1,0:T(8,128)S(1)}, f32[16,32768]{1,0:T(8,128)S(1)}, f32[3,8,32768]{2,1,0:T(8,128)S(1)}, f32[3,8,32768]...) custom-call(s32[1]{0:T(128)} %bitcast.here_ref, s32[16]{0:T(128)} %slot_ref.3, f32[16,32768]{1,0:T(8,128)} %phi_hbm.1, ...), custom_call_target="tpu_custom_call" | custom-call | flops 1000000 | bytes 6291456 | tf_op jit(solution)/shard_map/pack/pallas_call | solution.py:377
  3.8 0.1 collective-permute-start.2
  3.9 0.5 collective-permute-start
  4.4 8.3 %collective-permute-start.1 = (f32[3,8,32768]{2,1,0:T(8,128)S(1)}, f32[3,8,32768]{2,1,0:T(8,128)S(1)}, u32[]{:S(2)}, u32[]{:S(2)}) collective-permute-start(f32[3,8,32768]{2,1,0:T(8,128)S(1)} %get-tuple-element.26), channel_id=1, source_target_pairs={{1,3},{2,0},{3,5},{4,2},{5,7},{6,4},{7,9},{8,6},{9,11},{10,8},{11,... | collective-permute-start | bytes 9437192 | tf_op jit(solution)/shard_map/ppermute | solution.py:363
  12.8 0.0 collective-permute-done.2.merge_ref
  12.8 0.0 copy-done.1
  12.8 2.0 %relay.1 = (f32[3,8,8192]{2,1,0:T(8,128)S(1)}, f32[3,8,24576]{2,1,0:T(8,128)S(1)}) custom-call(s32[1]{0:T(128)} %bitcast.here_ref, s32[16]{0:T(128)S(1)} %copy-done.1, f32[16,32768]{1,0:T(8,128)S(1)} %get-tuple-element.21.phi_ref, f32[16,32768]{1,0:T(8,128)S(1)} %get-tuple-element.22.conc_ref, f32[16,32768]{1,0:T(8,128)S(1)} %get-tuple-element.23.mob_ref, ...), custom_call_target="tpu_custom_call" | custom-call | flops 1000000 | bytes 6291456 | tf_op jit(solution)/shard_map/relay/pallas_call | solution.py:392
  14.8 1.9 %collective-permute-start.3 = (f32[3,8,8192]{2,1,0:T(8,128)S(1)}, f32[3,8,8192]{2,1,0:T(8,128)S(1)}, u32[]{:S(2)}, u32[]{:S(2)}) collective-permute-start(f32[3,8,8192]{2,1,0:T(8,128)S(1)} %get-tuple-element.29), channel_id=1, source_target_pairs={{0,2},{2,4},{3,1},{4,6},{5,3},{6,8},{7,5},{8,10},{9,7},{10,12},{11... | collective-permute-start | bytes 2359304 | tf_op jit(solution)/shard_map/ppermute | solution.py:363
  16.7 0.0 collective-permute-done.final_ref
  16.7 2.0 %stay.1 = (f32[3,8,8192]{2,1,0:T(8,128)S(1)}, f32[3,8,24576]{2,1,0:T(8,128)S(1)}) custom-call(s32[1]{0:T(128)} %bitcast.here_ref, s32[16]{0:T(128)S(1)} %copy-done.1, f32[16,32768]{1,0:T(8,128)S(1)} %get-tuple-element.21.phi_ref, f32[16,32768]{1,0:T(8,128)S(1)} %get-tuple-element.22.conc_ref, f32[16,32768]{1,0:T(8,128)S(1)} %get-tuple-element.23.mob_ref, ...), custom_call_target="tpu_custom_call" | custom-call | flops 1000000 | bytes 6291456 | tf_op jit(solution)/shard_map/stay/pallas_call | solution.py:403
  18.7 22.7 %collective-permute-done.3.back_ref = f32[3,8,8192]{2,1,0:T(8,128)S(1)} collective-permute-done((f32[3,8,8192]{2,1,0:T(8,128)S(1)}, f32[3,8,8192]{2,1,0:T(8,128)S(1)}, u32[]{:S(2)}, u32[]{:S(2)}) %collective-permute-start.3) | collective-permute-done | bytes 786464 | tf_op jit(solution)/shard_map/ppermute | solution.py:363
  41.4 0.0 copy-start
  41.4 2.0 %collective-permute-start.4 = (f32[3,8,24576]{2,1,0:T(8,128)S(1)}, f32[3,8,24576]{2,1,0:T(8,128)S(1)}, u32[]{:S(2)}, u32[]{:S(2)}) collective-permute-start(f32[3,8,24576]{2,1,0:T(8,128)S(1)} %get-tuple-element.31), channel_id=1, source_target_pairs={{0,2},{2,4},{3,1},{4,6},{5,3},{6,8},{7,5},{8,10},{9,7},{10,12},{11... | collective-permute-start | bytes 7077896 | tf_op jit(solution)/shard_map/ppermute | solution.py:363
  43.4 22.4 %collective-permute-done.1.far_ref = f32[3,8,32768]{2,1,0:T(8,128)S(1)} collective-permute-done((f32[3,8,32768]{2,1,0:T(8,128)S(1)}, f32[3,8,32768]{2,1,0:T(8,128)S(1)}, u32[]{:S(2)}, u32[]{:S(2)}) %collective-permute-start.1) | collective-permute-done | bytes 3145760 | tf_op jit(solution)/shard_map/ppermute | solution.py:363
  65.8 0.2 faces.1
  66.0 1.9 %collective-permute-start.5 = (f32[8,8,1024]{2,1,0:T(8,128)S(1)}, f32[8,8,1024]{2,1,0:T(8,128)S(1)}, u32[]{:S(2)}, u32[]{:S(2)}) collective-permute-start(f32[8,8,1024]{2,1,0:T(8,128)S(1)} %get-tuple-element.33), channel_id=1, source_target_pairs={{0,1},{1,2},{2,3},{3,4},{4,5},{5,6},{6,7},{7,8},{8,9},{9,10},{10,1... | collective-permute-start | bytes 786440 | tf_op jit(solution)/shard_map/ppermute | solution.py:363
  67.9 8.0 %collective-permute-start.6 = (f32[8,8,1024]{2,1,0:T(8,128)S(1)}, f32[8,8,1024]{2,1,0:T(8,128)S(1)}, u32[]{:S(2)}, u32[]{:S(2)}) collective-permute-start(f32[8,8,1024]{2,1,0:T(8,128)S(1)} %get-tuple-element.34), channel_id=1, source_target_pairs={{1,0},{2,1},{3,2},{4,3},{5,4},{6,5},{7,6},{8,7},{9,8},{10,9},{11,1... | collective-permute-start | bytes 786440 | tf_op jit(solution)/shard_map/ppermute | solution.py:363
  76.0 4.8 %collective-permute-done.5.below_ref = f32[8,8,1024]{2,1,0:T(8,128)S(1)} collective-permute-done((f32[8,8,1024]{2,1,0:T(8,128)S(1)}, f32[8,8,1024]{2,1,0:T(8,128)S(1)}, u32[]{:S(2)}, u32[]{:S(2)}) %collective-permute-start.5) | collective-permute-done | bytes 262176 | tf_op jit(solution)/shard_map/ppermute | solution.py:363
  80.8 1.8 %collective-permute-done.6.above_ref = f32[8,8,1024]{2,1,0:T(8,128)S(1)} collective-permute-done((f32[8,8,1024]{2,1,0:T(8,128)S(1)}, f32[8,8,1024]{2,1,0:T(8,128)S(1)}, u32[]{:S(2)}, u32[]{:S(2)}) %collective-permute-start.6) | collective-permute-done | bytes 262176 | tf_op jit(solution)/shard_map/ppermute | solution.py:363
  82.5 0.0 copy-done
  82.5 3.3 %edge_steps.1 = (f32[8,32768]{1,0:T(8,128)}, f32[8,32768]{1,0:T(8,128)}, f32[3,6,8,1024]{3,2,1,0:T(8,128)S(1)}, f32[2,4,8,1024]{3,2,1,0:T(8,128)S(1)}, f32[2,4,8,1024]{3,2,1,0:T(8,128)S(1)}) custom-call(s32[1]{0:T(128)} %bitcast.here_ref, f32[3,8,8192]{2,1,0:T(8,128)S(1)} %get-tuple-element.32.edge_ref, f32[8,8,1024]{2,1,0:T(8,128)S(1)} %collective-permute-done.5.below_ref, ...), custom_call_target="tpu_custom_call" | custom-call | flops 1000000 | bytes 8388608 | tf_op jit(solution)/shard_map/edge_steps/pallas_call | solution.py:435
  85.9 0.0 collective-permute-done.4.back_ref
  85.9 11.0 %main_steps.1 = (f32[8,32768]{1,0:T(8,128)}, f32[8,32768]{1,0:T(8,128)}) custom-call(s32[1]{0:T(128)} %bitcast.here_ref, f32[3,8,24576]{2,1,0:T(8,128)S(1)} %get-tuple-element.25.stay_ref, f32[3,8,32768]{2,1,0:T(8,128)S(1)} %collective-permute-done.1.far_ref, ...), custom_call_target="tpu_custom_call", output_to_operand_aliasing={{0}: (8, {}), {1}: (9, {})} | custom-call | flops 1000000 | bytes 20971520 | tf_op jit(solution)/shard_map/main_steps/pallas_call | solution.py:448
Async XLA Ops:
  0.6 12.1 %copy-start.1 = (s32[16]{0:T(128)S(1)}, s32[16]{0:T(128)}, u32[]{:S(2)}) copy-start(s32[16]{0:T(128)} %slot_ref.3) | copy-start | bytes 196
  3.8 8.9 %collective-permute-start.2 = (f32[3,8,32768]{2,1,0:T(8,128)S(1)}, f32[3,8,32768]{2,1,0:T(8,128)S(1)}, u32[]{:S(2)}, u32[]{:S(2)}) collective-permute-start(f32[3,8,32768]{2,1,0:T(8,128)S(1)} %get-tuple-element.27), channel_id=1, source_target_pairs={{0,1},{1,0},{2,3},{3,2},{4,5},{5,4},{6,7},{7,6},{8,9},{9,8},{10,11... | collective-permute-start | bytes 9437192 | tf_op jit(solution)/shard_map/ppermute | solution.py:363
  3.9 12.8 %collective-permute-start = (f32[3,8,32768]{2,1,0:T(8,128)S(1)}, f32[3,8,32768]{2,1,0:T(8,128)S(1)}, u32[]{:S(2)}, u32[]{:S(2)}) collective-permute-start(f32[3,8,32768]{2,1,0:T(8,128)S(1)} %get-tuple-element.24), channel_id=1, source_target_pairs={{0,1},{1,0},{2,3},{3,2},{4,5},{5,4},{6,7},{7,6},{8,9},{9,8},{10,11... | collective-permute-start | bytes 9437192 | tf_op jit(solution)/shard_map/ppermute | solution.py:363
  4.4 61.4 %collective-permute-start.1 = (f32[3,8,32768]{2,1,0:T(8,128)S(1)}, f32[3,8,32768]{2,1,0:T(8,128)S(1)}, u32[]{:S(2)}, u32[]{:S(2)}) collective-permute-start(f32[3,8,32768]{2,1,0:T(8,128)S(1)} %get-tuple-element.26), channel_id=1, source_target_pairs={{1,3},{2,0},{3,5},{4,2},{5,7},{6,4},{7,9},{8,6},{9,11},{10,8},{11,... | collective-permute-start | bytes 9437192 | tf_op jit(solution)/shard_map/ppermute | solution.py:363
  14.8 26.6 %collective-permute-start.3 = (f32[3,8,8192]{2,1,0:T(8,128)S(1)}, f32[3,8,8192]{2,1,0:T(8,128)S(1)}, u32[]{:S(2)}, u32[]{:S(2)}) collective-permute-start(f32[3,8,8192]{2,1,0:T(8,128)S(1)} %get-tuple-element.29), channel_id=1, source_target_pairs={{0,2},{2,4},{3,1},{4,6},{5,3},{6,8},{7,5},{8,10},{9,7},{10,12},{11... | collective-permute-start | bytes 2359304 | tf_op jit(solution)/shard_map/ppermute | solution.py:363
  41.4 41.2 %copy-start = (s32[8,6]{1,0:T(8,128)S(1)}, s32[8,6]{1,0:T(8,128)}, u32[]{:S(2)}) copy-start(s32[8,6]{1,0:T(8,128)} %nbr_ref.3) | copy-start | bytes 580
  41.4 44.5 %collective-permute-start.4 = (f32[3,8,24576]{2,1,0:T(8,128)S(1)}, f32[3,8,24576]{2,1,0:T(8,128)S(1)}, u32[]{:S(2)}, u32[]{:S(2)}) collective-permute-start(f32[3,8,24576]{2,1,0:T(8,128)S(1)} %get-tuple-element.31), channel_id=1, source_target_pairs={{0,2},{2,4},{3,1},{4,6},{5,3},{6,8},{7,5},{8,10},{9,7},{10,12},{11... | collective-permute-start | bytes 7077896 | tf_op jit(solution)/shard_map/ppermute | solution.py:363
  66.0 14.8 %collective-permute-start.5 = (f32[8,8,1024]{2,1,0:T(8,128)S(1)}, f32[8,8,1024]{2,1,0:T(8,128)S(1)}, u32[]{:S(2)}, u32[]{:S(2)}) collective-permute-start(f32[8,8,1024]{2,1,0:T(8,128)S(1)} %get-tuple-element.33), channel_id=1, source_target_pairs={{0,1},{1,2},{2,3},{3,4},{4,5},{5,6},{6,7},{7,8},{8,9},{9,10},{10,1... | collective-permute-start | bytes 786440 | tf_op jit(solution)/shard_map/ppermute | solution.py:363
  67.9 14.6 %collective-permute-start.6 = (f32[8,8,1024]{2,1,0:T(8,128)S(1)}, f32[8,8,1024]{2,1,0:T(8,128)S(1)}, u32[]{:S(2)}, u32[]{:S(2)}) collective-permute-start(f32[8,8,1024]{2,1,0:T(8,128)S(1)} %get-tuple-element.34), channel_id=1, source_target_pairs={{1,0},{2,1},{3,2},{4,3},{5,4},{6,5},{7,6},{8,7},{9,8},{10,9},{11,1... | collective-permute-start | bytes 786440 | tf_op jit(solution)/shard_map/ppermute | solution.py:363

commit v11 on v10

--- a/solution.py
+++ b/solution.py
@@ -257,8 +257,8 @@
 
 def edge_kernel(
     here_ref, edge_ref, below_ref, above_ref, nbr_ref,
-    phase_ref, solute_ref, kept0_ref, kept1_ref, kept2_ref,
-    phi0, conc0, mob, phi1, conc1, phi2, conc2,
+    phase_hbm, solute_hbm, kept0_ref, kept1_ref, kept2_ref,
+    phi0, conc0, mob, phi1, conc1, phi2, conc2, phase_ref, solute_ref, sems,
 ):
     st = Stencil(here_ref[0], nbr_ref[...])
     states = (phi0, conc0, mob)
@@ -278,10 +278,15 @@
                     mirror = ref[EDGE + HALO - 1 - d, :, lanes]
                     taken = st.rows(above_ref[LOW_PLANES[f, d], :, lanes], st.above_x)
                     ref[EDGE + HALO + d, :, lanes] = jnp.where(st.has_above_x, taken, mirror)
-    for first, last in ((1, REST_AT - 1), (TOP_AT + 1, EXT - 1)):
+    copies = []
+    for n, (first, last) in enumerate(((1, REST_AT - 1), (TOP_AT + 1, EXT - 1))):
         st.sweep(first, last, 5, (phi0, conc0), mob, (phi1, conc1))
         st.sweep(first + 1, last - 1, 3, (phi1, conc1), mob, (phi2, conc2))
-        st.sweep(first + 2, last - 2, 1, (phi2, conc2), mob, (phase_ref, solute_ref), HALO)
+        st.sweep(first + 2, last - 2, 1, (phi2, conc2), mob, (phase_ref, solute_ref), first + 2 - n)
+        source, target = pl.ds(n * FACE, FACE), pl.ds(n * (EDGE - 1) * FACE, FACE)
+        for k, (ref, hbm) in enumerate(((phase_ref, phase_hbm), (solute_ref, solute_hbm))):
+            copies.append(pltpu.make_async_copy(ref.at[:, source], hbm.at[:, target], sems.at[n, k]))
+            copies[-1].start()
     for f, ref in enumerate(states):
         for n, x in enumerate((*range(REST_AT - 3, REST_AT), *range(TOP_AT, TOP_AT + 3))):
             kept0_ref[f, n] = ref[x]
@@ -291,6 +296,8 @@
     for f, ref in enumerate((phi2, conc2)):
         for n, x in enumerate((REST_AT - 4, REST_AT - 3, TOP_AT + 2, TOP_AT + 3)):
             kept2_ref[f, n] = ref[x]
+    for copy in copies:
+        copy.wait()
 
 
 BACK = REST_AT - 4
@@ -435,9 +442,9 @@
     phase, solute, kept0, kept1, kept2 = pl.pallas_call(
         edge_kernel,
         in_specs=[SMEM] + [VMEM] * 4,
-        out_specs=[VMEM] * 5,
+        out_specs=[HBM] * 2 + [VMEM] * 3,
         out_shape=[whole, whole, kept(3, 6), kept(2, 4), kept(2, 4)],
-        scratch_shapes=[state] * 7,
+        scratch_shapes=[state] * 7 + [pltpu.VMEM((CAP, 2 * FACE), jnp.float32)] * 2 + [pltpu.SemaphoreType.DMA((2, 2))],
         compiler_params=PARAMS,
         cost_estimate=cost(8 * MB),
         name="edge_steps",

time: 97.6 us -> 97 us (level)
  transfers between devices with their start and end apart: 7 -> 7, of which waited for: 4 -> 4; matrix products, arithmetic and copies ran while one was open for 0% -> 0% of each run, Pallas kernels for 8% -> 7%
where the time goes in v11:
time: 97 us; the launch traced here: 96.5 us
  waiting for transfers between devices  51.6 us (53%)
  starting transfers between devices  22.8 us (24%)
  Pallas kernels  21.1 us (22%)
    ppermute x7, waiting for transfers between devices, sent(): lax.ppermute(block, 'blk', [(p, q) for p, q in route if 0 <= q < count])  51.6 us
    ppermute x7, starting transfers between devices, sent(): lax.ppermute(block, 'blk', [(p, q) for p, q in route if 0 <= q < count])  22.8 us
    pallas_call x1, Pallas kernels, on_device(): pl.pallas_call(main_kernel, in_specs=[SMEM] + [VMEM] * 7 + [HBM] * 2, out...  11.1 us
    pallas_call x1, Pallas kernels, on_device(): pl.pallas_call(pack_kernel, in_specs=[SMEM, HBM, HBM, HBM, HBM], out_spec...  3.19 us
    pallas_call x1, Pallas kernels, on_device(): pl.pallas_call(edge_kernel, in_specs=[SMEM] + [VMEM] * 4, out_specs=[HBM]...  2.72 us
    pallas_call x1, Pallas kernels, on_device(): pl.pallas_call(relay_kernel, in_specs=[SMEM, SMEM] + [VMEM] * 4, out_spec...  1.99 us
    pallas_call x1, Pallas kernels, on_device(): pl.pallas_call(stay_kernel, in_specs=[SMEM, SMEM] + [VMEM] * 4, out_specs...  1.99 us
  transfers between devices with their start and end apart: 7, of which 4 were waited for; matrix products, arithmetic and copies ran while one was open for 0% of the time, Pallas kernels for 7%

profile of v11, /device:TPU:24, one launch (start us, length us, event | category | flops | bytes accessed | tf_op | source)
XLA Modules:
  0.0 96.5 jit_solution(9962705834103471131)
XLA Ops:
  0.6 0.0 copy-start.1
  0.6 3.2 %pack.1 = (f32[16,32768]{1,0:T(8,128)S(1)}, f32[16,32768]{1,0:T(8,128)S(1)}, f32[16,32768]{1,0:T(8,128)S(1)}, f32[3,8,32768]{2,1,0:T(8,128)S(1)}, f32[3,8,32768]...) custom-call(s32[1]{0:T(128)} %bitcast.here_ref, s32[16]{0:T(128)} %slot_ref.3, f32[16,32768]{1,0:T(8,128)} %phi_hbm.1, ...), custom_call_target="tpu_custom_call" | custom-call | flops 1000000 | bytes 6291456 | tf_op jit(solution)/shard_map/pack/pallas_call | solution.py:384
  3.8 0.1 collective-permute-start.2
  3.9 0.5 collective-permute-start
  4.4 8.3 %collective-permute-start.1 = (f32[3,8,32768]{2,1,0:T(8,128)S(1)}, f32[3,8,32768]{2,1,0:T(8,128)S(1)}, u32[]{:S(2)}, u32[]{:S(2)}) collective-permute-start(f32[3,8,32768]{2,1,0:T(8,128)S(1)} %get-tuple-element.26), channel_id=1, source_target_pairs={{1,3},{2,0},{3,5},{4,2},{5,7},{6,4},{7,9},{8,6},{9,11},{10,8},{11,... | collective-permute-start | bytes 9437192 | tf_op jit(solution)/shard_map/ppermute | solution.py:370
  12.8 0.0 collective-permute-done.2.merge_ref
  12.8 0.0 copy-done.1
  12.8 2.0 %relay.1 = (f32[3,8,8192]{2,1,0:T(8,128)S(1)}, f32[3,8,24576]{2,1,0:T(8,128)S(1)}) custom-call(s32[1]{0:T(128)} %bitcast.here_ref, s32[16]{0:T(128)S(1)} %copy-done.1, f32[16,32768]{1,0:T(8,128)S(1)} %get-tuple-element.21.phi_ref, f32[16,32768]{1,0:T(8,128)S(1)} %get-tuple-element.22.conc_ref, f32[16,32768]{1,0:T(8,128)S(1)} %get-tuple-element.23.mob_ref, ...), custom_call_target="tpu_custom_call" | custom-call | flops 1000000 | bytes 6291456 | tf_op jit(solution)/shard_map/relay/pallas_call | solution.py:399
  14.8 1.9 %collective-permute-start.3 = (f32[3,8,8192]{2,1,0:T(8,128)S(1)}, f32[3,8,8192]{2,1,0:T(8,128)S(1)}, u32[]{:S(2)}, u32[]{:S(2)}) collective-permute-start(f32[3,8,8192]{2,1,0:T(8,128)S(1)} %get-tuple-element.29), channel_id=1, source_target_pairs={{0,2},{2,4},{3,1},{4,6},{5,3},{6,8},{7,5},{8,10},{9,7},{10,12},{11... | collective-permute-start | bytes 2359304 | tf_op jit(solution)/shard_map/ppermute | solution.py:370
  16.7 0.0 collective-permute-done.final_ref
  16.7 2.0 %stay.1 = (f32[3,8,8192]{2,1,0:T(8,128)S(1)}, f32[3,8,24576]{2,1,0:T(8,128)S(1)}) custom-call(s32[1]{0:T(128)} %bitcast.here_ref, s32[16]{0:T(128)S(1)} %copy-done.1, f32[16,32768]{1,0:T(8,128)S(1)} %get-tuple-element.21.phi_ref, f32[16,32768]{1,0:T(8,128)S(1)} %get-tuple-element.22.conc_ref, f32[16,32768]{1,0:T(8,128)S(1)} %get-tuple-element.23.mob_ref, ...), custom_call_target="tpu_custom_call" | custom-call | flops 1000000 | bytes 6291456 | tf_op jit(solution)/shard_map/stay/pallas_call | solution.py:410
  18.7 22.7 %collective-permute-done.3.back_ref = f32[3,8,8192]{2,1,0:T(8,128)S(1)} collective-permute-done((f32[3,8,8192]{2,1,0:T(8,128)S(1)}, f32[3,8,8192]{2,1,0:T(8,128)S(1)}, u32[]{:S(2)}, u32[]{:S(2)}) %collective-permute-start.3) | collective-permute-done | bytes 786464 | tf_op jit(solution)/shard_map/ppermute | solution.py:370
  41.4 0.0 copy-start
  41.4 2.0 %collective-permute-start.4 = (f32[3,8,24576]{2,1,0:T(8,128)S(1)}, f32[3,8,24576]{2,1,0:T(8,128)S(1)}, u32[]{:S(2)}, u32[]{:S(2)}) collective-permute-start(f32[3,8,24576]{2,1,0:T(8,128)S(1)} %get-tuple-element.31), channel_id=1, source_target_pairs={{0,2},{2,4},{3,1},{4,6},{5,3},{6,8},{7,5},{8,10},{9,7},{10,12},{11... | collective-permute-start | bytes 7077896 | tf_op jit(solution)/shard_map/ppermute | solution.py:370
  43.4 22.4 %collective-permute-done.1.far_ref = f32[3,8,32768]{2,1,0:T(8,128)S(1)} collective-permute-done((f32[3,8,32768]{2,1,0:T(8,128)S(1)}, f32[3,8,32768]{2,1,0:T(8,128)S(1)}, u32[]{:S(2)}, u32[]{:S(2)}) %collective-permute-start.1) | collective-permute-done | bytes 3145760 | tf_op jit(solution)/shard_map/ppermute | solution.py:370
  65.8 0.2 faces.1
  66.0 1.9 %collective-permute-start.5 = (f32[8,8,1024]{2,1,0:T(8,128)S(1)}, f32[8,8,1024]{2,1,0:T(8,128)S(1)}, u32[]{:S(2)}, u32[]{:S(2)}) collective-permute-start(f32[8,8,1024]{2,1,0:T(8,128)S(1)} %get-tuple-element.33), channel_id=1, source_target_pairs={{0,1},{1,2},{2,3},{3,4},{4,5},{5,6},{6,7},{7,8},{8,9},{9,10},{10,1... | collective-permute-start | bytes 786440 | tf_op jit(solution)/shard_map/ppermute | solution.py:370
  67.9 8.0 %collective-permute-start.6 = (f32[8,8,1024]{2,1,0:T(8,128)S(1)}, f32[8,8,1024]{2,1,0:T(8,128)S(1)}, u32[]{:S(2)}, u32[]{:S(2)}) collective-permute-start(f32[8,8,1024]{2,1,0:T(8,128)S(1)} %get-tuple-element.34), channel_id=1, source_target_pairs={{1,0},{2,1},{3,2},{4,3},{5,4},{6,5},{7,6},{8,7},{9,8},{10,9},{11,1... | collective-permute-start | bytes 786440 | tf_op jit(solution)/shard_map/ppermute | solution.py:370
  76.0 4.8 %collective-permute-done.5.below_ref = f32[8,8,1024]{2,1,0:T(8,128)S(1)} collective-permute-done((f32[8,8,1024]{2,1,0:T(8,128)S(1)}, f32[8,8,1024]{2,1,0:T(8,128)S(1)}, u32[]{:S(2)}, u32[]{:S(2)}) %collective-permute-start.5) | collective-permute-done | bytes 262176 | tf_op jit(solution)/shard_map/ppermute | solution.py:370
  80.8 1.8 %collective-permute-done.6.above_ref = f32[8,8,1024]{2,1,0:T(8,128)S(1)} collective-permute-done((f32[8,8,1024]{2,1,0:T(8,128)S(1)}, f32[8,8,1024]{2,1,0:T(8,128)S(1)}, u32[]{:S(2)}, u32[]{:S(2)}) %collective-permute-start.6) | collective-permute-done | bytes 262176 | tf_op jit(solution)/shard_map/ppermute | solution.py:370
  82.5 0.0 copy-done
  82.5 2.7 %edge_steps.1 = (f32[8,32768]{1,0:T(8,128)}, f32[8,32768]{1,0:T(8,128)}, f32[3,6,8,1024]{3,2,1,0:T(8,128)S(1)}, f32[2,4,8,1024]{3,2,1,0:T(8,128)S(1)}, f32[2,4,8,1024]{3,2,1,0:T(8,128)S(1)}) custom-call(s32[1]{0:T(128)} %bitcast.here_ref, f32[3,8,8192]{2,1,0:T(8,128)S(1)} %get-tuple-element.32.edge_ref, f32[8,8,1024]{2,1,0:T(8,128)S(1)} %collective-permute-done.5.below_ref, ...), custom_call_target="tpu_custom_call" | custom-call | flops 1000000 | bytes 8388608 | tf_op jit(solution)/shard_map/edge_steps/pallas_call | solution.py:442
  85.3 0.0 collective-permute-done.4.back_ref
  85.3 11.1 %main_steps.1 = (f32[8,32768]{1,0:T(8,128)}, f32[8,32768]{1,0:T(8,128)}) custom-call(s32[1]{0:T(128)} %bitcast.here_ref, f32[3,8,24576]{2,1,0:T(8,128)S(1)} %get-tuple-element.25.stay_ref, f32[3,8,32768]{2,1,0:T(8,128)S(1)} %collective-permute-done.1.far_ref, ...), custom_call_target="tpu_custom_call", output_to_operand_aliasing={{0}: (8, {}), {1}: (9, {})} | custom-call | flops 1000000 | bytes 20971520 | tf_op jit(solution)/shard_map/main_steps/pallas_call | solution.py:455
Async XLA Ops:
  0.6 12.1 %copy-start.1 = (s32[16]{0:T(128)S(1)}, s32[16]{0:T(128)}, u32[]{:S(2)}) copy-start(s32[16]{0:T(128)} %slot_ref.3) | copy-start | bytes 196
  3.8 8.9 %collective-permute-start.2 = (f32[3,8,32768]{2,1,0:T(8,128)S(1)}, f32[3,8,32768]{2,1,0:T(8,128)S(1)}, u32[]{:S(2)}, u32[]{:S(2)}) collective-permute-start(f32[3,8,32768]{2,1,0:T(8,128)S(1)} %get-tuple-element.27), channel_id=1, source_target_pairs={{0,1},{1,0},{2,3},{3,2},{4,5},{5,4},{6,7},{7,6},{8,9},{9,8},{10,11... | collective-permute-start | bytes 9437192 | tf_op jit(solution)/shard_map/ppermute | solution.py:370
  3.9 12.8 %collective-permute-start = (f32[3,8,32768]{2,1,0:T(8,128)S(1)}, f32[3,8,32768]{2,1,0:T(8,128)S(1)}, u32[]{:S(2)}, u32[]{:S(2)}) collective-permute-start(f32[3,8,32768]{2,1,0:T(8,128)S(1)} %get-tuple-element.24), channel_id=1, source_target_pairs={{0,1},{1,0},{2,3},{3,2},{4,5},{5,4},{6,7},{7,6},{8,9},{9,8},{10,11... | collective-permute-start | bytes 9437192 | tf_op jit(solution)/shard_map/ppermute | solution.py:370
  4.4 61.4 %collective-permute-start.1 = (f32[3,8,32768]{2,1,0:T(8,128)S(1)}, f32[3,8,32768]{2,1,0:T(8,128)S(1)}, u32[]{:S(2)}, u32[]{:S(2)}) collective-permute-start(f32[3,8,32768]{2,1,0:T(8,128)S(1)} %get-tuple-element.26), channel_id=1, source_target_pairs={{1,3},{2,0},{3,5},{4,2},{5,7},{6,4},{7,9},{8,6},{9,11},{10,8},{11,... | collective-permute-start | bytes 9437192 | tf_op jit(solution)/shard_map/ppermute | solution.py:370
  14.8 26.6 %collective-permute-start.3 = (f32[3,8,8192]{2,1,0:T(8,128)S(1)}, f32[3,8,8192]{2,1,0:T(8,128)S(1)}, u32[]{:S(2)}, u32[]{:S(2)}) collective-permute-start(f32[3,8,8192]{2,1,0:T(8,128)S(1)} %get-tuple-element.29), channel_id=1, source_target_pairs={{0,2},{2,4},{3,1},{4,6},{5,3},{6,8},{7,5},{8,10},{9,7},{10,12},{11... | collective-permute-start | bytes 2359304 | tf_op jit(solution)/shard_map/ppermute | solution.py:370
  41.4 41.2 %copy-start = (s32[8,6]{1,0:T(8,128)S(1)}, s32[8,6]{1,0:T(8,128)}, u32[]{:S(2)}) copy-start(s32[8,6]{1,0:T(8,128)} %nbr_ref.3) | copy-start | bytes 580
  41.4 43.9 %collective-permute-start.4 = (f32[3,8,24576]{2,1,0:T(8,128)S(1)}, f32[3,8,24576]{2,1,0:T(8,128)S(1)}, u32[]{:S(2)}, u32[]{:S(2)}) collective-permute-start(f32[3,8,24576]{2,1,0:T(8,128)S(1)} %get-tuple-element.31), channel_id=1, source_target_pairs={{0,2},{2,4},{3,1},{4,6},{5,3},{6,8},{7,5},{8,10},{9,7},{10,12},{11... | collective-permute-start | bytes 7077896 | tf_op jit(solution)/shard_map/ppermute | solution.py:370
  66.0 14.8 %collective-permute-start.5 = (f32[8,8,1024]{2,1,0:T(8,128)S(1)}, f32[8,8,1024]{2,1,0:T(8,128)S(1)}, u32[]{:S(2)}, u32[]{:S(2)}) collective-permute-start(f32[8,8,1024]{2,1,0:T(8,128)S(1)} %get-tuple-element.33), channel_id=1, source_target_pairs={{0,1},{1,2},{2,3},{3,4},{4,5},{5,6},{6,7},{7,8},{8,9},{9,10},{10,1... | collective-permute-start | bytes 786440 | tf_op jit(solution)/shard_map/ppermute | solution.py:370
  67.9 14.6 %collective-permute-start.6 = (f32[8,8,1024]{2,1,0:T(8,128)S(1)}, f32[8,8,1024]{2,1,0:T(8,128)S(1)}, u32[]{:S(2)}, u32[]{:S(2)}) collective-permute-start(f32[8,8,1024]{2,1,0:T(8,128)S(1)} %get-tuple-element.34), channel_id=1, source_target_pairs={{1,0},{2,1},{3,2},{4,3},{5,4},{6,5},{7,6},{8,7},{9,8},{10,9},{11,1... | collective-permute-start | bytes 786440 | tf_op jit(solution)/shard_map/ppermute | solution.py:370
